TPU v7x, 128 devices: a whole 4x4x4 slice. The times are simulated.
128 devices in a mesh: clip: 16 (over z_lo, y, core), tile: 8 (over x, z_hi).
Axes of the slice: x: 4, y: 4, z: 4 (z_hi: 2, z_lo: 2; z = z_hi * 2 + z_lo), core: 2. Of those that a mesh axis runs over, the one named last changes fastest.
Arguments:
- features: bfloat16 [32, 128, 128, 256], P('clip', 'tile'), may hold values from -6 to 6
- conv_weight: bfloat16 [9, 256, 256], replicated, may hold values from -0.125 to 0.125
- codebook: bfloat16 [16384, 256], replicated, may hold values from -4 to 4
- codes: int32 [4, 32, 128, 128], P(None, 'clip', 'tile'), may hold values from 0 to 16383
- upstream: bfloat16 [32, 128, 128, 256], P('clip', 'tile'), may hold values from -6 to 6
Outputs:
- feature_grad: bfloat16 [32, 128, 128, 256], P('clip', 'tile')
- weight_grad: float32 [9, 256, 256], replicated
- codebook_grad: float32 [16384, 256], P(('clip', 'tile'))
All inputs are finite; a program needn't handle non-finite values.
Results may differ from a plain program's by a relative error of at most 0.0085.
Values may be sent and summed in bfloat16 or wider, within the bound.
No kernel may reach another device: no remote copies, remote signals or barrier semaphores. Data moves between devices by JAX's collectives and lax.ppermute only.
A program may use at most 192 MiB of HBM per device.

v0:
```python
import jax
import jax.numpy as jnp
from jax import lax
from jax.sharding import PartitionSpec as P

BETA = 0.25


def extended_2(array, sides, width):
    for axis, dim in sides:
        devices, length = (lax.axis_size(axis), array.shape[dim])
        up = [(i, (i + 1) % devices) for i in range(devices - 1)]
        down = [(j, i) for i, j in up]
        last = lax.slice_in_dim(array, length - width, length, axis=dim)
        leading = lax.slice_in_dim(array, 0, width, axis=dim)
        before = lax.ppermute(last, axis, up)
        after = lax.ppermute(leading, axis, down)
        array = jnp.concatenate([before, array, after], axis=dim)
    return array


def spread_rows(flat):
    return lax.psum_scatter(flat, ("clip", "tile"), scatter_dimension=0, tiled=True).reshape(
        flat.shape[1:]
    )


def on_device(features, conv_weight, codebook, codes, upstream):
    clips_here, rows, width, chans = features.shape
    devices = lax.axis_size("clip") * lax.axis_size("tile")
    extended = extended_2(features, (("tile", 1),), 1)
    padded = jnp.pad(extended, ((0, 0), (0, 0), (1, 1), (0, 0)))
    latent = jnp.zeros((clips_here, rows, width, chans), jnp.float32)
    for a in range(3):
        for b in range(3):
            latent = latent + jnp.einsum(
                "nhwc,cd->nhwd",
                padded[:, a : a + rows, b : b + width],
                conv_weight[3 * a + b],
                preferred_element_type=jnp.float32,
            )
    resid = latent
    total = jnp.zeros_like(latent)
    stacked = []
    for depth in range(codes.shape[0]):
        resid = resid - jnp.take(codebook, codes[depth], axis=0).astype(jnp.float32)
        total = total + resid
        stacked.append(resid)
    grad = (upstream.astype(jnp.float32) + 2.0 * BETA * total).astype(jnp.bfloat16)
    grad_ext = extended_2(grad, (("tile", 1),), 1)
    gpad = jnp.pad(grad_ext, ((0, 0), (0, 0), (1, 1), (0, 0)))
    back = jnp.zeros_like(latent)
    pieces = []
    for a in range(3):
        for b in range(3):
            back = back + jnp.einsum(
                "nhwd,cd->nhwc",
                gpad[:, 2 - a : 2 - a + rows, 2 - b : 2 - b + width],
                conv_weight[3 * a + b],
                preferred_element_type=jnp.float32,
            )
            pieces.append(
                jnp.einsum(
                    "nhwc,nhwd->cd",
                    padded[:, a : a + rows, b : b + width],
                    grad,
                    preferred_element_type=jnp.float32,
                )
            )
    local_weight = jnp.stack(pieces)
    values = -2.0 * jnp.stack(stacked).reshape(-1, chans)
    num_codes = codebook.shape[0]
    term = jax.ops.segment_sum(values, codes.reshape(-1), num_segments=num_codes)
    code_flat = term.reshape(devices, -1)
    weight_grad = lax.psum(local_weight, ("clip", "tile"))
    code_part = spread_rows(code_flat).reshape(num_codes // devices, chans)
    return (back.astype(jnp.bfloat16), weight_grad, code_part)


def solution(mesh):
    in_specs = (
        P("clip", "tile", None, None),
        P(),
        P(),
        P(None, "clip", "tile", None),
        P("clip", "tile", None, None),
    )
    out_specs = (P("clip", "tile", None, None), P(), P(("clip", "tile"), None))
    return jax.shard_map(
        on_device, mesh=mesh, in_specs=in_specs, out_specs=out_specs, check_vma=False
    )
```

profile of v0, /device:TPU:1, one launch (start us, length us, event | category | flops | bytes accessed | tf_op | source)
XLA Modules:
  0.0 522.9 jit_solution(7777707091847326861)
XLA Ops:
  8.2 6.3 %collective-permute-start = (bf16[2,1,128,256]{3,2,1,0:T(8,128)(2,1)S(1)}, bf16[2,1,128,256]{3,2,1,0:T(8,128)(2,1)S(1)}, u32[]{:S(2)}, u32[]{:S(2)}) collective-permute-start(bf16[2,1,128,256]{3,2,1,0:T(8,128)(2,1)S(1)} %get-tuple-element.20), channel_id=1, source_target_pairs={{0,1},{1,2},{2,3},{3,4},{4,5},{5,6},{6,7},{8,9},{9,10},{10,11},{11... | collective-permute-start | bytes 393224 | tf_op jit(solution)/shard_map/ppermute | solution.py:16
  16.6 4.2 fusion.124
  20.9 20.4 %gather_fusion = bf16[4096,256]{1,0:T(8,128)(2,1)} fusion(bf16[16384,256]{1,0:T(8,128)(2,1)} %param.9, s32[4096]{0:T(1024)S(1)} %get-tuple-element.33), kind=kCustom, calls=%fused_computation.clone | custom fusion | bytes 4210688 | tf_op jit(solution)/shard_map/jit(_take)/gather | solution.py:46
  41.3 20.4 %gather_fusion.1 = bf16[4096,256]{1,0:T(8,128)(2,1)} fusion(bf16[16384,256]{1,0:T(8,128)(2,1)} %param.9, s32[4096]{0:T(1024)S(1)} %get-tuple-element.32), kind=kCustom, calls=%fused_computation.1.clone | custom fusion | bytes 4210688 | tf_op jit(solution)/shard_map/jit(_take)/gather | solution.py:46
  61.7 20.4 %gather_fusion.2 = bf16[4096,256]{1,0:T(8,128)(2,1)} fusion(bf16[16384,256]{1,0:T(8,128)(2,1)} %param.9, s32[4096]{0:T(1024)S(1)} %get-tuple-element.31), kind=kCustom, calls=%fused_computation.2.clone | custom fusion | bytes 4210688 | tf_op jit(solution)/shard_map/jit(_take)/gather | solution.py:46
  82.1 20.5 %gather_fusion.3 = bf16[4096,256]{1,0:T(8,128)(2,1)} fusion(bf16[16384,256]{1,0:T(8,128)(2,1)} %param.9, s32[4096]{0:T(1024)S(1)} %get-tuple-element.30), kind=kCustom, calls=%fused_computation.3.clone | custom fusion | bytes 4210688 | tf_op jit(solution)/shard_map/jit(_take)/gather | solution.py:46
  103.9 2.7 fusion.106
  106.7 2.7 fusion.117
  109.4 2.7 fusion.120
  112.1 2.6 fusion.127
  114.7 2.7 fusion.130
  117.4 6.4 %fusion.170 = (bf16[2,16,128,256]{3,2,1,0:T(8,128)(2,1)}, bf16[2,16,128,256]{3,2,1,0:T(8,128)(2,1)}, bf16[2,16,128,256]{3,2,1,0:T(8,128)(2,1)}, bf16[2,16,128,25...) fusion(bf16[2,18,130,256]{3,2,1,0:T(8,128)(2,1)S(1)} %fusion.9), kind=kLoop, calls=%fused_computation.166 | loop fusion | bytes 25165824 | tf_op jit(solution)/shard_map/slice | solution.py:38
  124.3 3.1 fusion.114
  127.7 2.8 fusion.133
  132.0 10.7 %convert_subtract_fusion.3 = f32[2,16,128,256]{3,2,1,0:T(8,128)S(1)} fusion(f32[2,16,128,256]{3,2,1,0:T(8,128)} %fusion.114, f32[2,16,128,256]{3,2,1,0:T(8,128)} %fusion.117, f32[2,16,128,256]{3,2,1,0:T(8,128)} %fusion.120, f32[2,16,128,256]{3,2,1,0:T(8,128)S(1)} %copy-done.3, f32[2,16,128,256]{3,2,1,0:T(8,128)} %fusion.127, ...), kind=kOutput, calls=%fused_computation.16 | convolution fusion | flops 548405248 | bytes 42078208 | tf_op jit(solution)/shard_map/nhwc,cd->nhwd/dot_general | solution.py:36
  142.7 6.9 %fusion.4 = (f32[1,2,16,128,256]{4,3,2,1,0:T(8,128)S(1)}, bf16[2,16,128,256]{3,2,1,0:T(8,128)(2,1)S(1)}, f32[1,2,16,128,256]{4,3,2,1,0:T(8,128)S(1)}, f32[1,2,16,128,256]{4,3,2,1,0:T(8,128)S(1)}) fusion(f32[2,16,128,256]{3,2,1,0:T(8,128)S(1)} %convert_subtract_fusion.3, bf16[2,16,128,256]{3,2,1,0:T(8,128)(2,1)} %bitcast.196, ...), kind=kLoop, calls=%fused_computation.18 | loop fusion | flops 16777216 | bytes 27275264 | tf_op jit(solution)/shard_map/stack | solution.py:71
  149.7 6.1 %maximum_multiply_fusion = f32[4,2,16,128,256]{4,3,2,1,0:T(8,128)} fusion(f32[1,2,16,128,256]{4,3,2,1,0:T(8,128)S(1)} %get-tuple-element.6, f32[1,2,16,128,256]{4,3,2,1,0:T(8,128)S(1)} %get-tuple-element.8, f32[1,2,16,128,256]{4,3,2,1,0:T(8,128)S(1)} %get-tuple-element.9, f32[1,2,16,128,256]{4,3,2,1,0:T(8,128)S(1)} %bitcast.192), kind=kLoop, calls=%fused_computation.5 | loop fusion | flops 16777216 | bytes 33554432 | tf_op jit(solution)/shard_map/mul | solution.py:71
  155.8 94.9 %scatter_custom_fusion = f32[16384,256]{1,0:T(8,128)} fusion(s32[16384]{0:T(1024)S(1)} %bitcast.198, f32[16384,256]{1,0:T(8,128)} %bitcast.193, f32[]{:T(128)} %constant.3.clone.1), kind=kCustom, calls=%fused_computation.6 | custom fusion | flops 4194304 | bytes 16777728 | tf_op jit(solution)/shard_map/scatter-add | solution.py:73
  250.7 18.2 %reshape.17 = f32[128,32768]{1,0:T(8,128)} reshape(f32[16384,256]{1,0:T(8,128)} %scatter_custom_fusion) | data formatting | bytes 33554432 | tf_op jit(solution)/shard_map/reshape | solution.py:74
  268.9 3.2 fusion.60
  287.0 6.1 %collective-permute-start.2 = (bf16[2,1,128,256]{3,2,1,0:T(8,128)(2,1)S(1)}, bf16[2,1,128,256]{3,2,1,0:T(8,128)(2,1)S(1)}, u32[]{:S(2)}, u32[]{:S(2)}) collective-permute-start(bf16[2,1,128,256]{3,2,1,0:T(8,128)(2,1)S(1)} %get-tuple-element.17), channel_id=1, source_target_pairs={{0,1},{1,2},{2,3},{3,4},{4,5},{5,6},{6,7},{8,9},{9,10},{10,11},{11... | collective-permute-start | bytes 393224 | tf_op jit(solution)/shard_map/ppermute | solution.py:16
  293.2 2.7 fusion.10
  295.8 2.2 collective-permute-done.2
  298.0 2.8 fusion.14
  301.9 2.8 fusion.23
  304.7 2.7 fusion.25
  307.3 2.7 fusion.27
  310.1 2.8 fusion.29
  312.9 3.8 fusion.31
  316.7 11.5 %add_convert_fusion = bf16[2,16,128,256]{3,2,1,0:T(8,128)(2,1)} fusion(f32[2,16,128,256]{3,2,1,0:T(8,128)} %fusion.14, f32[2,16,128,256]{3,2,1,0:T(8,128)} %fusion.23, f32[2,16,128,256]{3,2,1,0:T(8,128)} %fusion.25, f32[2,16,128,256]{3,2,1,0:T(8,128)S(1)} %fusion.122, f32[2,16,128,256]{3,2,1,0:T(8,128)} %fusion.27, f32[2,16,128,256]{3,2,1,0:T(8,128)} %fusion.29, ...), kind=kOutput, calls=%fused_computation.11 | convolution fusion | flops 546308096 | bytes 37879808 | tf_op jit(solution)/shard_map/nhwd,cd->nhwc/dot_general | solution.py:56
  328.2 182.4 %all-reduce.6.cloned.1.call-done = (f32[9,256,256]{2,1,0:T(8,128)}, f32[128,32768]{1,0:T(8,128)}) async-done(((f32[9,256,256]{2,1,0:T(8,128)}, f32[128,32768]{1,0:T(8,128)}), (f32[9,256,256]{2,1,0:T(8,128)}, f32[128,32768]{1,0:T(8,128)})) %all-reduce.6.cloned.1.call-update) | async-done | bytes 19136528 | tf_op jit(solution)/shard_map/psum | solution.py:75
  512.9 3.2 copy.167
  (63 shorter events, 24.9 us)
Async XLA Ops:
  7.2 503.4 %all-reduce.6.cloned.1.call-start = ((), (), s32[]{:S(2)}) async-start(), calls=%async_computation | async-start | bytes 38273024 | tf_op jit(solution)/shard_map/psum | solution.py:75
  8.2 94.5 %collective-permute-start = (bf16[2,1,128,256]{3,2,1,0:T(8,128)(2,1)S(1)}, bf16[2,1,128,256]{3,2,1,0:T(8,128)(2,1)S(1)}, u32[]{:S(2)}, u32[]{:S(2)}) collective-permute-start(bf16[2,1,128,256]{3,2,1,0:T(8,128)(2,1)S(1)} %get-tuple-element.20), channel_id=1, source_target_pairs={{0,1},{1,2},{2,3},{3,4},{4,5},{5,6},{6,7},{8,9},{9,10},{10,11},{11... | collective-permute-start | bytes 393224 | tf_op jit(solution)/shard_map/ppermute | solution.py:16
  14.6 88.1 %collective-permute-start.1 = (bf16[2,1,128,256]{3,2,1,0:T(8,128)(2,1)S(1)}, bf16[2,1,128,256]{3,2,1,0:T(8,128)(2,1)S(1)}, u32[]{:S(2)}, u32[]{:S(2)}) collective-permute-start(bf16[2,1,128,256]{3,2,1,0:T(8,128)(2,1)S(1)} %get-tuple-element.21), channel_id=1, source_target_pairs={{1,0},{2,1},{3,2},{4,3},{5,4},{6,5},{7,6},{9,8},{10,9},{11,10},{12... | collective-permute-start | bytes 393224 | tf_op jit(solution)/shard_map/ppermute | solution.py:17
  82.1 20.6 %copy-start.16 = (s32[4,2,16,128]{3,2,1,0:T(8,128)S(1)}, s32[4,2,16,128]{3,2,1,0:T(8,128)}, u32[]{:S(2)}) copy-start(s32[4,2,16,128]{3,2,1,0:T(8,128)} %param.10) | copy-start | bytes 196612
  82.1 20.6 %copy-start = (bf16[2,16,128,256]{3,2,1,0:T(8,128)(2,1)S(1)}, bf16[2,16,128,256]{3,2,1,0:T(8,128)(2,1)}, u32[]{:S(2)}) copy-start(bf16[2,16,128,256]{3,2,1,0:T(8,128)(2,1)} %param.7) | copy-start | bytes 6291460
  102.7 1.3 copy-start.7
  124.3 3.3 copy-start.9
  124.3 3.1 copy-start.4
  127.7 3.5 copy-start.3
  127.7 4.4 copy-start.6
  268.9 3.2 copy-start.10
  272.1 1.6 copy-start.15
  273.7 1.6 copy-start.14
  275.2 1.6 copy-start.1
  276.8 1.7 copy-start.13
  278.5 1.6 copy-start.12
  280.1 1.6 copy-start.5
  281.7 1.6 copy-start.11
  284.8 1.5 copy-start.8
  284.8 8.3 %collective-permute-start.3 = (bf16[2,1,128,256]{3,2,1,0:T(8,128)(2,1)S(1)}, bf16[2,1,128,256]{3,2,1,0:T(8,128)(2,1)S(1)}, u32[]{:S(2)}, u32[]{:S(2)}) collective-permute-start(bf16[2,1,128,256]{3,2,1,0:T(8,128)(2,1)S(1)} %get-tuple-element.16), channel_id=1, source_target_pairs={{1,0},{2,1},{3,2},{4,3},{5,4},{6,5},{7,6},{9,8},{10,9},{11,10},{12... | collective-permute-start | bytes 393224 | tf_op jit(solution)/shard_map/ppermute | solution.py:17
  287.0 11.0 %collective-permute-start.2 = (bf16[2,1,128,256]{3,2,1,0:T(8,128)(2,1)S(1)}, bf16[2,1,128,256]{3,2,1,0:T(8,128)(2,1)S(1)}, u32[]{:S(2)}, u32[]{:S(2)}) collective-permute-start(bf16[2,1,128,256]{3,2,1,0:T(8,128)(2,1)S(1)} %get-tuple-element.17), channel_id=1, source_target_pairs={{0,1},{1,2},{2,3},{3,4},{4,5},{5,6},{6,7},{8,9},{9,10},{10,11},{11... | collective-permute-start | bytes 393224 | tf_op jit(solution)/shard_map/ppermute | solution.py:16
  312.9 3.8 copy-start.2
Sparse Core Ops, SparseCore 0:
  284.9 225.6 all-reduce.5
where the time goes:
time: 524 us; the launch traced here: 523 us
  waiting for transfers between devices  185 us (35%)
  local copies, waits for them, and re-layouts  116 us (22%)
  other arithmetic  111 us (21%)
  matrix products  81.9 us (16%)
  starting transfers between devices  15.2 us (3%)
  between operations  14.2 us (3%)
    psum x1, waiting for transfers between devices, on_device(): weight_grad = lax.psum(local_weight, ('clip', 'tile'))  182 us
    scatter-add x1, other arithmetic, on_device(): jax.ops.segment_sum(values, codes.reshape(-1), num_segments=num_codes)  94.9 us
    gather x4, local copies, waits for them, and re-layouts, on_device(): resid = resid - jnp.take(codebook, codes[depth], axis=0).astype(jnp.float32)  81.7 us
    dot_general x9, matrix products, on_device(): jnp.einsum('nhwc,cd->nhwd', padded[:, a:a + rows, b:b + width], conv_weig...  34.3 us
    dot_general x9, matrix products, on_device(): jnp.einsum('nhwd,cd->nhwc', gpad[:, 2 - a:2 - a + rows, 2 - b:2 - b + wid...  32.5 us
    reshape x1, local copies, waits for them, and re-layouts, on_device(): code_flat = term.reshape(devices, -1)  18.2 us
    dot_general x9, matrix products, on_device(): jnp.einsum('nhwc,nhwd->cd', padded[:, a:a + rows, b:b + width], grad, pre...  15.1 us
    ppermute x2, starting transfers between devices, extended_2(): before = lax.ppermute(last, axis, up)  12.5 us
  transfers between devices with their start and end apart: 5, of which 2 were waited for; matrix products, arithmetic and copies ran while one was open for 23% of the time, Pallas kernels for 0%

commit v1 on v0

v1 whole, which is shorter than its diff:
```python
import jax
import jax.numpy as jnp
from jax import lax
from jax.experimental import pallas as pl
from jax.experimental.pallas import tpu as pltpu
from jax.sharding import PartitionSpec as P

BETA = 0.25
BOTH = ("clip", "tile")
F32, BF16 = jnp.float32, jnp.bfloat16

CHANS = 256
CODES = 16384
DEPTHS = 4
COLS = 128
ROWS = 16
HERE = 2
SPOTS = HERE * ROWS * COLS
BLOCK = 4 * COLS
BLOCKS = SPOTS // BLOCK
GROUP = 16
GROUPS = DEPTHS * SPOTS // GROUP
SPILL = 256
TABLE_STEP = 4096
TABLE_STEPS = CODES // TABLE_STEP
SHARE = CODES // 128
OUT_STEPS = 8
FIRST_OUT = TABLE_STEPS + BLOCKS


def lin(x, y, z, core):
    return (((z % 2) * 4 + y) * 2 + core) * 8 + x * 2 + z // 2


def moves(where):
    return [
        (lin(x, y, z, c), lin(*where(x, y, z, c)))
        for x in range(4)
        for y in range(4)
        for z in range(4)
        for c in range(2)
    ]


SWAP = moves(lambda x, y, z, c: (x, y, z, 1 - c))


def first_ring(d):
    return moves(lambda x, y, z, c: ((x + d) % 4, y, z, c) if c == 0 else (x, (y + d) % 4, z, c))


PLANES = [[lin(x, y, z, 0) for y in range(4) for z in range(4)] for x in range(4)] + [
    [lin(x, y, z, 1) for x in range(4) for z in range(4)] for y in range(4)
]


def place():
    clip, tile = lax.axis_index("clip"), lax.axis_index("tile")
    core, y, z_lo = clip % 2, (clip // 2) % 4, clip // 8
    x, z_hi = tile // 2, tile % 2
    return jnp.stack([x, y, z_hi * 2 + z_lo, core]).astype(jnp.int32)


def owner(x0, y0, core, j, m):
    other, z = m // 4, m % 4
    x = jnp.where(core == 0, (x0 + j) % 4, other)
    y = jnp.where(core == 0, other, (y0 + j) % 4)
    return lin(x, y, z, core)


def shifted(value, by):
    n = value.shape[0]
    col = lax.broadcasted_iota(jnp.int32, value.shape, 0) % COLS
    if by == 1:
        return jnp.where(col == 0, 0.0, pltpu.roll(value, 1, axis=0))
    return jnp.where(col == COLS - 1, 0.0, pltpu.roll(value, n - 1, axis=0))


def quantizer_kernel(
    codes, plain, spilled, info,
    table_in, feats, above, below, weights, up,
    grad, send, keep,
    table, sums, lat, window, sems,
):
    i = pl.program_id(0)

    def window_copies():
        found = []
        for n in range(HERE):
            for source, row, count in ((above, 0, 1), (feats, 1, ROWS), (below, ROWS + 1, 1)):
                found.append(
                    pltpu.make_async_copy(
                        source.at[n], window.at[n, pl.ds(row, count)], sems.at[len(found)]
                    )
                )
        return found

    @pl.when(i == 0)
    def _():
        for copy in window_copies():
            copy.start()

    @pl.when(i < TABLE_STEPS)
    def _():
        base = pl.multiple_of(i * (2 * TABLE_STEP), 8)

        def convert(t, carry):
            part = table_in[pl.ds(pl.multiple_of(t * 512, 16), 512), :].astype(F32)
            at = pl.multiple_of(base + t * 1024, 8)
            table[pl.ds(at, 512, stride=2), :] = part[:, :128]
            table[pl.ds(at + 1, 512, stride=2), :] = part[:, 128:]
            sums[pl.ds(at, 1024), :] = jnp.zeros((1024, 128), F32)
            return carry

        lax.fori_loop(0, TABLE_STEP // 512, convert, 0)

    @pl.when(i == TABLE_STEPS)
    def _():
        for copy in window_copies():
            copy.wait()
        sums[pl.ds(2 * CODES, 2 * SPILL), :] = jnp.zeros((2 * SPILL, 128), F32)

        def lend(s, carry):
            table[pl.ds(2 * (CODES + s), 2), :] = table[pl.ds(spilled[s], 2), :]
            return carry

        lax.fori_loop(0, jnp.minimum(info[4], SPILL), lend, 0)

    @pl.when((i >= TABLE_STEPS) & (i < FIRST_OUT))
    def _():
        block = i - TABLE_STEPS
        clip = block // (ROWS // 4)
        row = (block % (ROWS // 4)) * 4
        conv = None
        for a in range(3):
            part = window[clip, pl.ds(row + a, 4)].reshape(BLOCK, CHANS)
            term = jnp.dot(part, weights[a], preferred_element_type=F32)
            conv = term if conv is None else conv + term
        latent = (
            shifted(conv[:, :CHANS], 1)
            + conv[:, CHANS : 2 * CHANS]
            + shifted(conv[:, 2 * CHANS :], -1)
        )
        lat[pl.ds(0, BLOCK, stride=2), :] = latent[:, :128]
        lat[pl.ds(1, BLOCK, stride=2), :] = latent[:, 128:]

        def resids(at, ids):
            found = []
            for r in range(4):
                place_r = pl.ds(2 * (r * COLS + at), 2)
                resid, total = lat[place_r, :], None
                for d in range(DEPTHS):
                    k = ids(r, d)
                    resid = resid - table[pl.ds(k, 2), :]
                    total = resid if total is None else total + resid
                    found.append((k, resid))
                lat[place_r, :] = total
            return found

        def step(at, carry):
            base = (block * COLS + at) * GROUP
            found = resids(at, lambda r, d: codes[base + (r * DEPTHS + d)])
            new = [sums[pl.ds(k, 2), :] + v for k, v in found]
            for (k, _), v in zip(found, new):
                sums[pl.ds(k, 2), :] = v
            return carry

        def slow_step(at, carry):
            base = (block * COLS + at) * GROUP
            for k, v in resids(at, lambda r, d: plain[base + (r * DEPTHS + d)]):
                sums[pl.ds(k, 2), :] = sums[pl.ds(k, 2), :] + v
            return carry

        @pl.when(info[4] <= SPILL)
        def _():
            lax.fori_loop(0, COLS, step, 0, unroll=2)

        @pl.when(info[4] > SPILL)
        def _():
            lax.fori_loop(0, COLS, slow_step, 0)

        total = jnp.concatenate(
            [lat[pl.ds(0, BLOCK, stride=2), :], lat[pl.ds(1, BLOCK, stride=2), :]], axis=1
        )
        grad[...] = (up[...].astype(F32) + 2.0 * BETA * total).astype(BF16)

    @pl.when((i == FIRST_OUT) & (info[4] <= SPILL))
    def _():
        def give_back(s, carry):
            k = spilled[s]
            sums[pl.ds(k, 2), :] = sums[pl.ds(k, 2), :] + sums[pl.ds(2 * (CODES + s), 2), :]
            return carry

        lax.fori_loop(0, info[4], give_back, 0)

    def put_out(out, core, j):
        for m in range(16):
            at = pl.multiple_of(owner(info[0], info[1], core, j, m) * (2 * SHARE), 8)
            out[0, m, :, :128] = (sums[pl.ds(at, SHARE, stride=2), :] * -2.0).astype(BF16)
            out[0, m, :, 128:] = (sums[pl.ds(at + 1, SHARE, stride=2), :] * -2.0).astype(BF16)

    @pl.when((i >= FIRST_OUT) & (i < FIRST_OUT + 4))
    def _():
        put_out(send, 1 - info[3], i - FIRST_OUT)

    @pl.when(i >= FIRST_OUT + 4)
    def _():
        put_out(keep, info[3], i - FIRST_OUT - 4)


def quantizer(codes, plain, spilled, info, codebook, feats, above, below, weights, up):
    def spot(i, *_):
        return (jnp.clip(i - TABLE_STEPS, 0, BLOCKS - 1), 0)

    out_block = (1, 16, SHARE, CHANS)
    return pl.pallas_call(
        quantizer_kernel,
        grid_spec=pltpu.PrefetchScalarGridSpec(
            num_scalar_prefetch=4,
            grid=(FIRST_OUT + OUT_STEPS,),
            in_specs=[
                pl.BlockSpec(
                    (TABLE_STEP, CHANS), lambda i, *_: (jnp.minimum(i, TABLE_STEPS - 1), 0)
                ),
                pl.BlockSpec(memory_space=pl.ANY),
                pl.BlockSpec(memory_space=pl.ANY),
                pl.BlockSpec(memory_space=pl.ANY),
                pl.BlockSpec((3, CHANS, 3 * CHANS), lambda i, *_: (0, 0, 0)),
                pl.BlockSpec((BLOCK, CHANS), spot),
            ],
            out_specs=[
                pl.BlockSpec((BLOCK, CHANS), spot),
                pl.BlockSpec(out_block, lambda i, *_: (jnp.clip(i - FIRST_OUT, 0, 3), 0, 0, 0)),
                pl.BlockSpec(
                    out_block, lambda i, *_: (jnp.clip(i - FIRST_OUT - 4, 0, 3), 0, 0, 0)
                ),
            ],
            scratch_shapes=[
                pltpu.VMEM((2 * (CODES + SPILL), 128), F32),
                pltpu.VMEM((2 * (CODES + SPILL), 128), F32),
                pltpu.VMEM((2 * BLOCK, 128), F32),
                pltpu.VMEM((HERE, ROWS + 2, COLS, CHANS), BF16),
                pltpu.SemaphoreType.DMA((3 * HERE,)),
            ],
        ),
        out_shape=[
            jax.ShapeDtypeStruct((SPOTS, CHANS), BF16),
            jax.ShapeDtypeStruct((4, 16, SHARE, CHANS), BF16),
            jax.ShapeDtypeStruct((4, 16, SHARE, CHANS), BF16),
        ],
        compiler_params=pltpu.CompilerParams(
            vmem_limit_bytes=58 << 20, dimension_semantics=("arbitrary",)
        ),
        cost_estimate=pl.CostEstimate(
            flops=2 * 9 * SPOTS * CHANS * CHANS, bytes_accessed=32 << 20, transcendentals=0
        ),
    )(codes, plain, spilled, info, codebook, feats, above, below, weights, up)


def weight_kernel(info, feats, above, below, grad, send, keep, window, total, sems):
    i = pl.program_id(0)

    def window_copies():
        found = []
        for n in range(HERE):
            for source, row, count in ((above, 0, 1), (feats, 1, ROWS), (below, ROWS + 1, 1)):
                found.append(
                    pltpu.make_async_copy(
                        source.at[n], window.at[n, pl.ds(row, count)], sems.at[len(found)]
                    )
                )
        return found

    @pl.when(i == 0)
    def _():
        for copy in window_copies():
            copy.start()
        for copy in window_copies():
            copy.wait()

    clip = i // (ROWS // 4)
    row = (i % (ROWS // 4)) * 4
    mid = grad[...].astype(F32)
    wide = jnp.concatenate(
        [shifted(mid, -1).astype(BF16), grad[...], shifted(mid, 1).astype(BF16)], axis=1
    )
    for a in range(3):
        part = window[clip, pl.ds(row + a, 4)].reshape(BLOCK, CHANS)
        term = lax.dot_general(part, wide, (((0,), (0,)), ((), ())), preferred_element_type=F32)

        @pl.when(i == 0)
        def _():
            total[pl.ds(a * CHANS, CHANS), :] = term

        @pl.when(i > 0)
        def _():
            total[pl.ds(a * CHANS, CHANS), :] += term

    @pl.when(i == BLOCKS - 1)
    def _():
        for out, core in ((send, 1 - info[3]), (keep, info[3])):
            for j in range(4):
                for m in range(16):
                    b = jnp.minimum(owner(info[0], info[1], core, j, m), 95)
                    rows = total[pl.ds(pl.multiple_of(b * 8, 8), 8), :]
                    for q in range(3):
                        out[j, m, pl.ds(8 * q, 8), :] = rows[:, q * CHANS : (q + 1) * CHANS]


def weight_sums(info, feats, above, below, grad):
    shape = (4, 16, 24, CHANS)
    return pl.pallas_call(
        weight_kernel,
        grid_spec=pltpu.PrefetchScalarGridSpec(
            num_scalar_prefetch=1,
            grid=(BLOCKS,),
            in_specs=[
                pl.BlockSpec(memory_space=pl.ANY),
                pl.BlockSpec(memory_space=pl.ANY),
                pl.BlockSpec(memory_space=pl.ANY),
                pl.BlockSpec((BLOCK, CHANS), lambda i, *_: (i, 0)),
            ],
            out_specs=[
                pl.BlockSpec(shape, lambda i, *_: (0, 0, 0, 0)),
                pl.BlockSpec(shape, lambda i, *_: (0, 0, 0, 0)),
            ],
            scratch_shapes=[
                pltpu.VMEM((HERE, ROWS + 2, COLS, CHANS), BF16),
                pltpu.VMEM((3 * CHANS, 3 * CHANS), F32),
                pltpu.SemaphoreType.DMA((3 * HERE,)),
            ],
        ),
        out_shape=[jax.ShapeDtypeStruct(shape, F32)] * 2,
        compiler_params=pltpu.CompilerParams(
            vmem_limit_bytes=32 << 20, dimension_semantics=("arbitrary",)
        ),
        cost_estimate=pl.CostEstimate(
            flops=2 * 9 * SPOTS * CHANS * CHANS, bytes_accessed=8 << 20, transcendentals=0
        ),
    )(info, feats, above, below, grad)


def back_kernel(grad, above, below, weights, out, window, sems):
    i = pl.program_id(0)

    def window_copies():
        found = []
        for n in range(HERE):
            for source, row, count in ((above, 0, 1), (grad, 1, ROWS), (below, ROWS + 1, 1)):
                found.append(
                    pltpu.make_async_copy(
                        source.at[n], window.at[n, pl.ds(row, count)], sems.at[len(found)]
                    )
                )
        return found

    @pl.when(i == 0)
    def _():
        for copy in window_copies():
            copy.start()
        for copy in window_copies():
            copy.wait()

    clip = i // (ROWS // 4)
    row = (i % (ROWS // 4)) * 4
    conv = None
    for a in range(3):
        part = window[clip, pl.ds(row + 2 - a, 4)].reshape(BLOCK, CHANS)
        term = jnp.dot(part, weights[a], preferred_element_type=F32)
        conv = term if conv is None else conv + term
    back = (
        shifted(conv[:, :CHANS], -1)
        + conv[:, CHANS : 2 * CHANS]
        + shifted(conv[:, 2 * CHANS :], 1)
    )
    out[...] = back.astype(BF16)


def feature_grads(grad, above, below, weights):
    return pl.pallas_call(
        back_kernel,
        grid=(BLOCKS,),
        in_specs=[
            pl.BlockSpec(memory_space=pl.ANY),
            pl.BlockSpec(memory_space=pl.ANY),
            pl.BlockSpec(memory_space=pl.ANY),
            pl.BlockSpec((3, CHANS, 3 * CHANS), lambda i: (0, 0, 0)),
        ],
        out_specs=pl.BlockSpec((BLOCK, CHANS), lambda i: (i, 0)),
        scratch_shapes=[
            pltpu.VMEM((HERE, ROWS + 2, COLS, CHANS), BF16),
            pltpu.SemaphoreType.DMA((3 * HERE,)),
        ],
        out_shape=jax.ShapeDtypeStruct((SPOTS, CHANS), BF16),
        compiler_params=pltpu.CompilerParams(
            vmem_limit_bytes=32 << 20, dimension_semantics=("arbitrary",)
        ),
        cost_estimate=pl.CostEstimate(
            flops=2 * 9 * SPOTS * CHANS * CHANS, bytes_accessed=8 << 20, transcendentals=0
        ),
    )(grad, above, below, weights)


def edges(array):
    n = lax.axis_size("tile")
    up = [(i, i + 1) for i in range(n - 1)]
    down = [(i + 1, i) for i in range(n - 1)]
    above = lax.ppermute(array[:, -1:], "tile", up)
    below = lax.ppermute(array[:, :1], "tile", down)
    return above, below


def entry_lists(codes):
    parts = codes.reshape(DEPTHS, BLOCKS, 4, COLS)
    cells = [parts[d, :, r] for r in range(4) for d in range(DEPTHS)]
    later = []
    for a in range(GROUP):
        hit = jnp.zeros((BLOCKS, COLS), jnp.bool_)
        for b in range(a + 1, GROUP):
            hit = hit | (cells[a] == cells[b])
        later.append(hit)
    flags = jnp.stack(later).reshape(128, 128).astype(F32)
    entries = jnp.stack(cells).reshape(128, 128)
    lane = jnp.arange(128)
    inside = jnp.dot(flags, (lane[:, None] < lane[None, :]).astype(F32))
    per_row = flags.sum(1)
    ahead = jnp.where(lane[None, :] < lane[:, None], per_row[None, :], 0.0).sum(1)
    rank = (inside + ahead[:, None]).astype(jnp.int32)
    total = per_row.sum().astype(jnp.int32)
    hits = flags > 0
    marked = jnp.where(hits, CODES + rank, entries)
    wanted = jnp.where(hits, rank, -1).reshape(1, -1) == jnp.arange(SPILL)[:, None]
    spilled = jnp.where(wanted, entries.reshape(1, -1), 0).sum(1)

    def grouped(array):
        return (2 * array).reshape(GROUP, GROUPS).T.reshape(-1)

    return grouped(marked), grouped(entries), 2 * spilled, total


def on_device(features, conv_weight, codebook, codes, upstream):
    info = place()
    above, below = edges(features)
    taps = conv_weight.reshape(3, 3, CHANS, CHANS)
    forward = taps.transpose(0, 2, 1, 3).reshape(3, CHANS, 3 * CHANS)
    backward = taps.transpose(0, 3, 1, 2).reshape(3, CHANS, 3 * CHANS)
    marked, plain, spilled, total = entry_lists(codes)
    info = jnp.concatenate([info, total[None]])
    grad, send, keep = quantizer(
        marked, plain, spilled, info, codebook, features, above, below, forward,
        upstream.reshape(SPOTS, CHANS),
    )
    got = lax.ppermute(send, BOTH, SWAP)
    weight_send, weight_keep = weight_sums(info, features, above, below, grad)
    weight_got = lax.ppermute(weight_send.astype(BF16), BOTH, SWAP)
    grad4 = grad.reshape(features.shape)
    back = feature_grads(grad4, *edges(grad4), backward)
    chip = jnp.concatenate(
        [
            (keep.astype(F32) + got.astype(F32)).astype(BF16),
            (weight_keep + weight_got.astype(F32)).astype(BF16),
        ],
        axis=2,
    )
    ring = chip[0].astype(F32)
    for d in (1, 2, 3):
        ring = ring + lax.ppermute(chip[d], BOTH, first_ring(d)).astype(F32)
    plane = lax.all_to_all(ring.astype(BF16), BOTH, 0, 0, axis_index_groups=PLANES)
    block = plane.astype(F32).sum(0)
    code_part = block[:SHARE]
    piece = block[SHARE:].astype(BF16)
    pieces = lax.all_to_all(jnp.broadcast_to(piece[None], (128, 24, CHANS)), BOTH, 0, 0)
    weight_grad = pieces[:96].reshape(96, 3, 8, CHANS).transpose(0, 2, 1, 3)
    weight_grad = weight_grad.reshape(3, CHANS, 3, CHANS).transpose(0, 2, 1, 3)
    weight_grad = weight_grad.reshape(9, CHANS, CHANS).astype(F32)
    return back.reshape(features.shape), weight_grad, code_part


def solution(mesh):
    in_specs = (
        P("clip", "tile", None, None),
        P(),
        P(),
        P(None, "clip", "tile", None),
        P("clip", "tile", None, None),
    )
    out_specs = (P("clip", "tile", None, None), P(), P(BOTH, None))
    return jax.shard_map(
        on_device, mesh=mesh, in_specs=in_specs, out_specs=out_specs, check_vma=False
    )
```

time: 524 us -> 204 us (0.39)
  waiting for transfers between devices: 185 us -> 45.2 us
  other arithmetic: 111 us -> 9.27 us
  local copies, waits for them, and re-layouts: 116 us -> 18.4 us
  matrix products: 81.9 us -> 0.15 us
  Pallas kernels: 0 us -> 74.1 us
  blocking collectives: 0 us -> 22.9 us
  starting transfers between devices: 15.2 us -> 30.2 us
  between operations: 14.2 us -> 1.84 us
    psum x1 -> x0, waiting for transfers between devices: 182 us -> none  [on_device(): weight_grad = lax.psum(local_weight, ('clip', 'tile'))]
    scatter-add x1 -> x0, other arithmetic: 94.9 us -> none  [on_device(): jax.ops.segment_sum(values, codes.reshape(-1), num_segments=num_codes)]
    gather x4 -> x0, local copies, waits for them, and re-layouts: 81.7 us -> none  [on_device(): resid = resid - jnp.take(codebook, codes[depth], axis=0).astype(jnp.float32)]
    dot_general x27 -> x1, matrix products: 81.9 us -> 0.15 us  [entry_lists(): inside = jnp.dot(flags, (lane[:, None] < lane[None, :]).astype(F32))]
    pallas_call x0 -> x3, Pallas kernels: none -> 74.1 us  [the longest x1 52.5 us: quantizer(): pl.pallas_call(quantizer_kernel, grid_spec=pltpu.PrefetchScalarGridSpec(n...]
    ppermute x4 -> x9, waiting for transfers between devices: 2.17 us -> 45.2 us  [the longest x3 26.9 us: on_device(): ring = ring + lax.ppermute(chip[d], BOTH, first_ring(d)).astype(F32)]
    all_to_all x0 -> x1, blocking collectives: none -> 22.9 us  [on_device(): lax.all_to_all(ring.astype(BF16), BOTH, 0, 0, axis_index_groups=PLANES)]
    reshape x1 -> x6, local copies, waits for them, and re-layouts: 18.2 us -> 4.94 us  [the longest x4 1.83 us: grouped(): return (2 * array).reshape(GROUP, GROUPS).T.reshape(-1)]
  transfers between devices with their start and end apart: 5 -> 10, of which waited for: 2 -> 5; matrix products, arithmetic and copies ran while one was open for 23% -> 7% of each run, Pallas kernels for 0% -> 11%
where the time goes in v1:
time: 204 us; the launch traced here: 202 us
  Pallas kernels  74.1 us (36%)
  waiting for transfers between devices  45.2 us (22%)
  starting transfers between devices  30.2 us (15%)
  blocking collectives  22.9 us (11%)
  local copies, waits for them, and re-layouts  18.4 us (9%)
  other arithmetic  9.27 us (5%)
    pallas_call x1, Pallas kernels, quantizer(): pl.pallas_call(quantizer_kernel, grid_spec=pltpu.PrefetchScalarGridSpec(n...  52.5 us
    ppermute x3, waiting for transfers between devices, on_device(): ring = ring + lax.ppermute(chip[d], BOTH, first_ring(d)).astype(F32)  26.9 us
    all_to_all x1, blocking collectives, on_device(): lax.all_to_all(ring.astype(BF16), BOTH, 0, 0, axis_index_groups=PLANES)  22.9 us
    ppermute x2, waiting for transfers between devices, edges(): above = lax.ppermute(array[:, -1:], 'tile', up)  15.2 us
    pallas_call x1, Pallas kernels, weight_sums(): pl.pallas_call(weight_kernel, grid_spec=pltpu.PrefetchScalarGridSpec(num_...  14 us
    ppermute x2, starting transfers between devices, edges(): above = lax.ppermute(array[:, -1:], 'tile', up)  11.5 us
    all_to_all x1, starting transfers between devices, on_device(): lax.all_to_all(jnp.broadcast_to(piece[None], (128, 24, CHANS)), BOTH, 0, 0)  9.67 us
    pallas_call x1, Pallas kernels, feature_grads(): pl.pallas_call(back_kernel, grid=(BLOCKS,), in_specs=[pl.BlockSpec(memory...  7.6 us
  transfers between devices with their start and end apart: 10, of which 5 were waited for; matrix products, arithmetic and copies ran while one was open for 7% of the time, Pallas kernels for 11%

profile of v1, /device:TPU:1, one launch (start us, length us, event | category | flops | bytes accessed | tf_op | source)
XLA Modules:
  0.0 202.0 jit_solution(18368848075167404457)
XLA Ops:
  0.6 1.1 fusion.14
  1.7 6.3 %collective-permute-start = (bf16[2,1,128,256]{3,2,1,0:T(8,128)(2,1)S(1)}, bf16[2,1,128,256]{3,2,1,0:T(8,128)(2,1)S(1)}, u32[]{:S(2)}, u32[]{:S(2)}) collective-permute-start(bf16[2,1,128,256]{3,2,1,0:T(8,128)(2,1)S(1)} %get-tuple-element.21), channel_id=1, source_target_pairs={{0,1},{1,2},{2,3},{3,4},{4,5},{5,6},{6,7},{8,9},{9,10},{10,11},{11... | collective-permute-start | bytes 393224 | tf_op jit(solution)/shard_map/ppermute | solution.py:408
  8.1 1.3 collective-permute-start.1
  9.4 1.0 fusion.15
  10.3 1.0 slice_bitcast_fusion.1
  15.0 0.8 reshape.2350.plain
  16.5 1.5 copy.96.weights
  18.1 3.0 %select_reduce_fusion = s32[256]{0:T(256)S(1)} fusion(s32[16384]{0:T(1024)S(1)} %bitcast.284, s32[16384]{0:T(1024)S(1)} %get-tuple-element.22), kind=kLoop, calls=%fused_computation | loop fusion | flops 12582656 | bytes 132096 | tf_op jit(solution)/shard_map/reduce_sum | solution.py:433
  22.9 52.5 %shard_map.76 = (bf16[4096,256]{1,0:T(8,128)(2,1)}, bf16[4,16,128,256]{3,2,1,0:T(8,128)(2,1)}, bf16[4,16,128,256]{3,2,1,0:T(8,128)(2,1)}) custom-call(s32[16384]{0:T(1024)} %reshape.2349.codes, s32[16384]{0:T(1024)} %reshape.2350.plain, s32[256]{0:T(256)} %broadcast_multiply_fusion.spilled, s32[5]{0:T(128)} %concatenate.7.info, bf16[16384,256]{1,0:T(8,128)(2,1)} %table_in.1, ...), custom_call_target="tpu_custom_call" | custom-call | flops 4831838208 | bytes 33554432 | tf_op jit(solution)/shard_map/pallas_call | solution.py:216
  75.4 1.1 collective-permute-start.4
  76.5 1.6 copy-done.1
  78.1 0.9 copy-done.5
  79.0 0.9 copy-done.7
  79.9 14.0 %shard_map.78 = (f32[4,16,24,256]{3,2,1,0:T(8,128)S(1)}, f32[4,16,24,256]{3,2,1,0:T(8,128)S(1)}) custom-call(s32[5]{0:T(128)S(1)} %copy-done.3, bf16[2,16,128,256]{3,2,1,0:T(8,128)(2,1)S(1)} %copy-done, bf16[2,1,128,256]{3,2,1,0:T(8,128)(2,1)S(1)} %copy-done.5, bf16[2,1,128,256]{3,2,1,0:T(8,128)(2,1)S(1)} %copy-done.7, bf16[4096,256]{1,0:T(8,128)(2,1)S(1)} %copy-done.1), custom_call_target="tpu_custom_call" | custom-call | flops 4831838208 | bytes 8388608 | tf_op jit(solution)/shard_map/pallas_call | solution.py:312
  94.1 2.3 %collective-permute-done.5 = bf16[4,16,24,256]{3,2,1,0:T(8,128)(2,1)S(1)} collective-permute-done((bf16[4,16,24,256]{3,2,1,0:T(8,128)(2,1)S(1)}, bf16[4,16,24,256]{3,2,1,0:T(8,128)(2,1)S(1)}, u32[]{:S(2)}, u32[]{:S(2)}) %collective-permute-start.5) | collective-permute-done | bytes 786464 | tf_op jit(solution)/shard_map/ppermute | solution.py:455
  96.7 1.9 add_convert_fusion
  98.9 1.5 collective-permute-start.6
  100.4 2.7 %collective-permute-start.7 = (bf16[16,152,256]{2,1,0:T(8,128)(2,1)S(1)}, bf16[16,152,256]{2,1,0:T(8,128)(2,1)S(1)}, u32[]{:S(2)}, u32[]{:S(2)}) collective-permute-start(bf16[16,152,256]{2,1,0:T(8,128)(2,1)S(1)} %get-tuple-element.17), channel_id=1, source_target_pairs={{0,4},{8,40},{64,68},{72,104},{1,5},{9,41},{65,69},{73,105},{16,20... | collective-permute-start | bytes 3735560 | tf_op jit(solution)/shard_map/ppermute | solution.py:467
  103.0 1.0 collective-permute-start.8
  104.1 12.4 %collective-permute-done.6 = bf16[16,152,256]{2,1,0:T(8,128)(2,1)S(1)} collective-permute-done((bf16[16,152,256]{2,1,0:T(8,128)(2,1)S(1)}, bf16[16,152,256]{2,1,0:T(8,128)(2,1)S(1)}, u32[]{:S(2)}, u32[]{:S(2)}) %collective-permute-start.6) | collective-permute-done | bytes 1245216 | tf_op jit(solution)/shard_map/ppermute | solution.py:467
  116.4 14.5 %collective-permute-done.7 = bf16[16,152,256]{2,1,0:T(8,128)(2,1)S(1)} collective-permute-done((bf16[16,152,256]{2,1,0:T(8,128)(2,1)S(1)}, bf16[16,152,256]{2,1,0:T(8,128)(2,1)S(1)}, u32[]{:S(2)}, u32[]{:S(2)}) %collective-permute-start.7) | collective-permute-done | bytes 1245216 | tf_op jit(solution)/shard_map/ppermute | solution.py:467
  131.6 22.9 %all_to_all.10 = bf16[16,152,256]{2,1,0:T(8,128)(2,1)S(1)} all-to-all(bf16[16,152,256]{2,1,0:T(8,128)(2,1)S(1)} %fusion.2), channel_id=1, replica_groups={{0,64,1,65,16,80,17,81,32,96,33,97,48,112,49,113},{2,66,3,67,18,82,19,8..., dimensions={0} | all-to-all | bytes 2490368 | tf_op jit(solution)/shard_map/all_to_all | solution.py:468
  154.7 1.2 broadcast_in_dim.53
  155.9 9.7 %all-to-all-start.1 = ((bf16[128,24,256]{2,1,0:T(8,128)(2,1)}), bf16[128,24,256]{2,1,0:T(8,128)(2,1)}, u32[]{:S(2)}, u32[]{:S(2)}) async-start(bf16[128,24,256]{2,1,0:T(8,128)(2,1)} %broadcast_in_dim.53), calls=%async_computation.1 | async-start | bytes 3145728 | tf_op jit(solution)/shard_map/all_to_all | solution.py:472
  166.3 5.2 %collective-permute-start.2 = (bf16[2,1,128,256]{3,2,1,0:T(8,128)(2,1)}, bf16[2,1,128,256]{3,2,1,0:T(8,128)(2,1)S(1)}, u32[]{:S(2)}, u32[]{:S(2)}) collective-permute-start(bf16[2,1,128,256]{3,2,1,0:T(8,128)(2,1)} %get-tuple-element.19), channel_id=1, source_target_pairs={{0,1},{1,2},{2,3},{3,4},{4,5},{5,6},{6,7},{8,9},{9,10},{10,11},{11... | collective-permute-start | bytes 393224 | tf_op jit(solution)/shard_map/ppermute | solution.py:408
  171.5 1.3 collective-permute-start.3
  172.8 1.6 copy.98.weights
  174.4 15.2 %collective-permute-done.2.above = bf16[2,1,128,256]{3,2,1,0:T(8,128)(2,1)S(1)} collective-permute-done((bf16[2,1,128,256]{3,2,1,0:T(8,128)(2,1)}, bf16[2,1,128,256]{3,2,1,0:T(8,128)(2,1)S(1)}, u32[]{:S(2)}, u32[]{:S(2)}) %collective-permute-start.2) | collective-permute-done | bytes 131104 | tf_op jit(solution)/shard_map/ppermute | solution.py:408
  189.6 0.8 collective-permute-done.3.below
  190.5 7.6 %shard_map.77 = bf16[4096,256]{1,0:T(8,128)(2,1)} custom-call(bf16[2,16,128,256]{3,2,1,0:T(8,128)(2,1)S(1)} %bitcast.154, bf16[2,1,128,256]{3,2,1,0:T(8,128)(2,1)S(1)} %collective-permute-done.2.above, bf16[2,1,128,256]{3,2,1,0:T(8,128)(2,1)S(1)} %collective-permute-done.3.below, bf16[3,256,768]{2,1,0:T(8,128)(2,1)S(1)} %copy.98.weights), custom_call_target="tpu_custom_call" | custom-call | flops 4831838208 | bytes 8388608 | tf_op jit(solution)/shard_map/pallas_call | solution.py:380
  198.7 1.4 convert_bitcast_fusion
  200.4 1.6 copy.100
  (81 shorter events, 8.4 us)
Async XLA Ops:
  0.6 15.2 %copy-start.8 = (bf16[9,256,256]{2,1,0:T(8,128)(2,1)S(1)}, bf16[9,256,256]{2,1,0:T(8,128)(2,1)}, u32[]{:S(2)}) copy-start(bf16[9,256,256]{2,1,0:T(8,128)(2,1)} %param.6) | copy-start | bytes 3538948
  1.7 20.5 %collective-permute-start = (bf16[2,1,128,256]{3,2,1,0:T(8,128)(2,1)S(1)}, bf16[2,1,128,256]{3,2,1,0:T(8,128)(2,1)S(1)}, u32[]{:S(2)}, u32[]{:S(2)}) collective-permute-start(bf16[2,1,128,256]{3,2,1,0:T(8,128)(2,1)S(1)} %get-tuple-element.21), channel_id=1, source_target_pairs={{0,1},{1,2},{2,3},{3,4},{4,5},{5,6},{6,7},{8,9},{9,10},{10,11},{11... | collective-permute-start | bytes 393224 | tf_op jit(solution)/shard_map/ppermute | solution.py:408
  8.1 14.1 %collective-permute-start.1 = (bf16[2,1,128,256]{3,2,1,0:T(8,128)(2,1)S(1)}, bf16[2,1,128,256]{3,2,1,0:T(8,128)(2,1)S(1)}, u32[]{:S(2)}, u32[]{:S(2)}) collective-permute-start(bf16[2,1,128,256]{3,2,1,0:T(8,128)(2,1)S(1)} %get-tuple-element.20), channel_id=1, source_target_pairs={{1,0},{2,1},{3,2},{4,3},{5,4},{6,5},{7,6},{9,8},{10,9},{11,10},{12... | collective-permute-start | bytes 393224 | tf_op jit(solution)/shard_map/ppermute | solution.py:409
  22.2 0.7 copy-start.4
  22.2 0.7 copy-start.6
  22.9 53.6 %copy-start = (bf16[2,16,128,256]{3,2,1,0:T(8,128)(2,1)S(1)}, bf16[2,16,128,256]{3,2,1,0:T(8,128)(2,1)}, u32[]{:S(2)}) copy-start(bf16[2,16,128,256]{3,2,1,0:T(8,128)(2,1)} %feats.3) | copy-start | bytes 6291460
  22.9 53.6 %copy-start.3 = (s32[5]{0:T(128)S(1)}, s32[5]{0:T(128)}, u32[]{:S(2)}) copy-start(s32[5]{0:T(128)} %concatenate.7.info) | copy-start | bytes 64
  75.4 21.2 %collective-permute-start.4 = (bf16[4,16,128,256]{3,2,1,0:T(8,128)(2,1)}, bf16[4,16,128,256]{3,2,1,0:T(8,128)(2,1)S(1)}, u32[]{:S(2)}, u32[]{:S(2)}) collective-permute-start(bf16[4,16,128,256]{3,2,1,0:T(8,128)(2,1)} %get-tuple-element.10), channel_id=1, source_target_pairs={{0,8},{8,0},{64,72},{72,64},{1,9},{9,1},{65,73},{73,65},{16,24},{2... | collective-permute-start | bytes 12582920 | tf_op jit(solution)/shard_map/ppermute | solution.py:453
  76.5 1.6 copy-start.1
  78.1 0.9 copy-start.5
  79.0 0.9 copy-start.7
  93.9 2.7 %copy-start.9 = (bf16[4,16,128,256]{3,2,1,0:T(8,128)(2,1)S(1)}, bf16[4,16,128,256]{3,2,1,0:T(8,128)(2,1)}, u32[]{:S(2)}) copy-start(bf16[4,16,128,256]{3,2,1,0:T(8,128)(2,1)} %get-tuple-element.9) | copy-start | bytes 12582916
  94.0 2.4 %collective-permute-start.5 = (bf16[4,16,24,256]{3,2,1,0:T(8,128)(2,1)S(1)}, bf16[4,16,24,256]{3,2,1,0:T(8,128)(2,1)S(1)}, u32[]{:S(2)}, u32[]{:S(2)}) collective-permute-start(bf16[4,16,24,256]{3,2,1,0:T(8,128)(2,1)S(1)} %convert_element_type.76), channel_id=1, source_target_pairs={{0,8},{8,0},{64,72},{72,64},{1,9},{9,1},{65,73},{73,65},{16,24},{2... | collective-permute-start | bytes 2359304 | tf_op jit(solution)/shard_map/ppermute | solution.py:455
  98.9 17.6 %collective-permute-start.6 = (bf16[16,152,256]{2,1,0:T(8,128)(2,1)S(1)}, bf16[16,152,256]{2,1,0:T(8,128)(2,1)S(1)}, u32[]{:S(2)}, u32[]{:S(2)}) collective-permute-start(bf16[16,152,256]{2,1,0:T(8,128)(2,1)S(1)} %get-tuple-element.15), channel_id=1, source_target_pairs={{0,2},{8,24},{64,66},{72,88},{1,3},{9,25},{65,67},{73,89},{16,18},... | collective-permute-start | bytes 3735560 | tf_op jit(solution)/shard_map/ppermute | solution.py:467
  100.4 30.6 %collective-permute-start.7 = (bf16[16,152,256]{2,1,0:T(8,128)(2,1)S(1)}, bf16[16,152,256]{2,1,0:T(8,128)(2,1)S(1)}, u32[]{:S(2)}, u32[]{:S(2)}) collective-permute-start(bf16[16,152,256]{2,1,0:T(8,128)(2,1)S(1)} %get-tuple-element.17), channel_id=1, source_target_pairs={{0,4},{8,40},{64,68},{72,104},{1,5},{9,41},{65,69},{73,105},{16,20... | collective-permute-start | bytes 3735560 | tf_op jit(solution)/shard_map/ppermute | solution.py:467
  103.0 27.9 %collective-permute-start.8 = (bf16[16,152,256]{2,1,0:T(8,128)(2,1)S(1)}, bf16[16,152,256]{2,1,0:T(8,128)(2,1)S(1)}, u32[]{:S(2)}, u32[]{:S(2)}) collective-permute-start(bf16[16,152,256]{2,1,0:T(8,128)(2,1)S(1)} %get-tuple-element.16), channel_id=1, source_target_pairs={{0,6},{8,56},{64,70},{72,120},{1,7},{9,57},{65,71},{73,121},{16,22... | collective-permute-start | bytes 3735560 | tf_op jit(solution)/shard_map/ppermute | solution.py:467
  154.6 1.3 copy-start.10
  154.7 10.9 %copy-start.2 = (bf16[4096,256]{1,0:T(8,128)(2,1)S(1)}, bf16[4096,256]{1,0:T(8,128)(2,1)}, u32[]{:S(2)}) copy-start(bf16[4096,256]{1,0:T(8,128)(2,1)} %get-tuple-element.8.grad) | copy-start | bytes 6291460
  155.9 42.8 %all-to-all-start.1 = ((bf16[128,24,256]{2,1,0:T(8,128)(2,1)}), bf16[128,24,256]{2,1,0:T(8,128)(2,1)}, u32[]{:S(2)}, u32[]{:S(2)}) async-start(bf16[128,24,256]{2,1,0:T(8,128)(2,1)} %broadcast_in_dim.53), calls=%async_computation.1 | async-start | bytes 3145728 | tf_op jit(solution)/shard_map/all_to_all | solution.py:472
  166.3 23.3 %collective-permute-start.2 = (bf16[2,1,128,256]{3,2,1,0:T(8,128)(2,1)}, bf16[2,1,128,256]{3,2,1,0:T(8,128)(2,1)S(1)}, u32[]{:S(2)}, u32[]{:S(2)}) collective-permute-start(bf16[2,1,128,256]{3,2,1,0:T(8,128)(2,1)} %get-tuple-element.19), channel_id=1, source_target_pairs={{0,1},{1,2},{2,3},{3,4},{4,5},{5,6},{6,7},{8,9},{9,10},{10,11},{11... | collective-permute-start | bytes 393224 | tf_op jit(solution)/shard_map/ppermute | solution.py:408
  171.5 18.9 %collective-permute-start.3 = (bf16[2,1,128,256]{3,2,1,0:T(8,128)(2,1)}, bf16[2,1,128,256]{3,2,1,0:T(8,128)(2,1)S(1)}, u32[]{:S(2)}, u32[]{:S(2)}) collective-permute-start(bf16[2,1,128,256]{3,2,1,0:T(8,128)(2,1)} %get-tuple-element.18), channel_id=1, source_target_pairs={{1,0},{2,1},{3,2},{4,3},{5,4},{6,5},{7,6},{9,8},{10,9},{11,10},{12... | collective-permute-start | bytes 393224 | tf_op jit(solution)/shard_map/ppermute | solution.py:409
  174.4 23.7 %copy-start.11 = (f32[152,256]{1,0:T(8,128)S(1)}, f32[152,256]{1,0:T(8,128)}, u32[]{:S(2)}) copy-start(f32[152,256]{1,0:T(8,128)} %copy-done.10) | copy-start | bytes 466948

commit v2 on v1

v2 whole, which is shorter than its diff:
```python
import functools

import jax
import jax.numpy as jnp
from jax import lax
from jax.experimental import pallas as pl
from jax.experimental.pallas import tpu as pltpu
from jax.sharding import PartitionSpec as P

BETA = 0.25
BOTH = ("clip", "tile")
F32, BF16 = jnp.float32, jnp.bfloat16

CHANS = 256
CODES = 16384
DEPTHS = 4
COLS = 128
ROWS = 16
HERE = 2
SPOTS = HERE * ROWS * COLS
BLOCK = 4 * COLS
BLOCKS = SPOTS // BLOCK
GROUP = 16
GROUPS = DEPTHS * SPOTS // GROUP
SPILL = 64
CHUNKS = 8
UNROLL = 8
SHARE = CODES // 128


def lin(x, y, z, core):
    return (((z % 2) * 4 + y) * 2 + core) * 8 + x * 2 + z // 2


def moves(where):
    return [
        (lin(x, y, z, c), lin(*where(x, y, z, c)))
        for x in range(4)
        for y in range(4)
        for z in range(4)
        for c in range(2)
    ]


SWAP = moves(lambda x, y, z, c: (x, y, z, 1 - c))


def first_ring(d):
    return moves(lambda x, y, z, c: ((x + d) % 4, y, z, c) if c == 0 else (x, (y + d) % 4, z, c))


PLANES = [[lin(x, y, z, 0) for y in range(4) for z in range(4)] for x in range(4)] + [
    [lin(x, y, z, 1) for x in range(4) for z in range(4)] for y in range(4)
]


def place():
    clip, tile = lax.axis_index("clip"), lax.axis_index("tile")
    core, y, z_lo = clip % 2, (clip // 2) % 4, clip // 8
    x, z_hi = tile // 2, tile % 2
    return jnp.stack([x, y, z_hi * 2 + z_lo, core]).astype(jnp.int32)


def owner(x0, y0, core, j, m):
    other, z = m // 4, m % 4
    x = jnp.where(core == 0, (x0 + j) % 4, other)
    y = jnp.where(core == 0, other, (y0 + j) % 4)
    return lin(x, y, z, core)


def shifted(value, by):
    n = value.shape[0]
    col = lax.broadcasted_iota(jnp.int32, value.shape, 0) % COLS
    if by == 1:
        return jnp.where(col == 0, 0.0, pltpu.roll(value, 1, axis=0))
    return jnp.where(col == COLS - 1, 0.0, pltpu.roll(value, n - 1, axis=0))


def window_copies(above, mid, below, window, sems, first=0):
    found = []
    for n in range(HERE):
        for source, row, count in ((above, 0, 1), (mid, 1, ROWS), (below, ROWS + 1, 1)):
            found.append(
                pltpu.make_async_copy(
                    source.at[n], window.at[n, pl.ds(row, count)], sems.at[first + len(found)]
                )
            )
    return found


def list_kernel(codes, marked, spilled, count):
    cells = [codes[pl.ds(d * 32 + r, BLOCKS, stride=4), :] for r in range(4) for d in range(DEPTHS)]
    later = []
    for a in range(GROUP):
        hit = None
        for b in range(a + 1, GROUP):
            same = (cells[a] == cells[b]).astype(jnp.int32)
            hit = same if hit is None else jnp.maximum(hit, same)
        later.append(jnp.zeros_like(cells[a]) if hit is None else hit)
    flags = jnp.concatenate(later, axis=0)
    entries = jnp.concatenate(cells, axis=0)
    line = lax.broadcasted_iota(jnp.int32, (128, 128), 0)
    lane = lax.broadcasted_iota(jnp.int32, (128, 128), 1)
    bits = flags.astype(F32)
    inside = jnp.dot(bits, (line < lane).astype(F32), preferred_element_type=F32)
    per_row = jnp.dot(bits, jnp.ones((128, 128), F32), preferred_element_type=F32)
    ahead = jnp.dot((lane < line).astype(F32), per_row, preferred_element_type=F32)
    rank = (inside + ahead).astype(jnp.int32)
    marked[...] = 2 * jnp.where(flags > 0, CODES + rank, entries)
    rank = jnp.where(flags > 0, rank, -1)
    for s in range(SPILL):
        spilled[pl.ds(s, 1), :] = jnp.sum(
            jnp.where(rank == s, 2 * entries, 0), axis=0, keepdims=True
        )
    spilled[...] = jnp.broadcast_to(
        jnp.sum(spilled[...].astype(F32), axis=1, keepdims=True), (SPILL, 128)
    ).astype(jnp.int32)
    whole = jnp.sum(per_row, axis=0, keepdims=True).astype(jnp.int32)
    count[...] = jnp.broadcast_to(whole, (8, 128))


def entry_lists(codes):
    ints = jnp.int32
    return pl.pallas_call(
        list_kernel,
        out_shape=[
            jax.ShapeDtypeStruct((128, 128), ints),
            jax.ShapeDtypeStruct((SPILL, 128), ints),
            jax.ShapeDtypeStruct((8, 128), ints),
        ],
    )(codes.reshape(128, 128))


def quantizer_kernel(
    spilled, info, count,
    marked, plain, codebook, feats, above, below, weights, up,
    grad, send, keep,
    table, sums, lat, raw, near, taps, window, ids, sems,
):
    many = count[0, 0]
    windows = window_copies(above, feats, below, window, sems)
    get_taps = pltpu.make_async_copy(weights, taps, sems.at[6])
    get_ids = pltpu.make_async_copy(marked, ids, sems.at[7])
    get_up = pltpu.make_async_copy(up, near, sems.at[8])
    chunk = CODES // CHUNKS

    def get_table(c):
        rows = pl.ds(c * chunk, chunk)
        return pltpu.make_async_copy(codebook.at[rows], raw.at[rows], sems.at[16 + c])

    for copy in windows + [get_taps]:
        copy.start()
    for c in range(CHUNKS):
        get_table(c).start()
    get_ids.start()
    get_up.start()
    for copy in windows + [get_taps]:
        copy.wait()

    def convolve(block, carry):
        clip = block // (ROWS // 4)
        row = (block % (ROWS // 4)) * 4
        cols = [None] * 3
        for a in range(3):
            part = window[clip, pl.ds(row + a, 4)].reshape(BLOCK, CHANS)
            for b in range(3):
                term = jnp.dot(part, taps[3 * a + b], preferred_element_type=F32)
                cols[b] = term if a == 0 else cols[b] + term
        latent = shifted(cols[0], 1) + cols[1] + shifted(cols[2], -1)
        at = pl.multiple_of(block * (2 * BLOCK), 8)
        lat[pl.ds(at, BLOCK, stride=2), :] = latent[:, :128]
        lat[pl.ds(at + 1, BLOCK, stride=2), :] = latent[:, 128:]
        return carry

    lax.fori_loop(0, BLOCKS, convolve, 0)

    for c in range(CHUNKS):
        get_table(c).wait()

        def convert(t, carry):
            at = pl.multiple_of(c * chunk + t * 512, 16)
            part = raw[pl.ds(at, 512), :].astype(F32)
            at = pl.multiple_of(2 * at, 8)
            table[pl.ds(at, 512, stride=2), :] = part[:, :128]
            table[pl.ds(at + 1, 512, stride=2), :] = part[:, 128:]
            sums[pl.ds(at, 1024), :] = jnp.zeros((1024, 128), F32)
            return carry

        lax.fori_loop(0, chunk // 512, convert, 0)

    sums[pl.ds(2 * CODES, 2 * SPILL), :] = jnp.zeros((2 * SPILL, 128), F32)

    def lend(s, carry):
        table[pl.ds(2 * (CODES + s), 2), :] = table[pl.ds(spilled[s, 0], 2), :]
        return carry

    lax.fori_loop(0, jnp.minimum(many, SPILL), lend, 0)

    def resids(spot, code):
        found = []
        for r in range(4):
            here = pl.ds(2 * (spot + r * COLS), 2)
            resid, total = lat[here, :], None
            for d in range(DEPTHS):
                k = code(r, d)
                resid = resid - table[pl.ds(k, 2), :]
                total = resid if total is None else total + resid
                found.append((k, resid))
            lat[here, :] = total
        return found

    get_ids.wait()

    @pl.when(many <= SPILL)
    def _():
        def blocks(block, carry):
            def step(col, carry):
                first = block * COLS + col
                found = resids(
                    block * BLOCK + col, lambda r, d: ids[first + (r * DEPTHS + d) * (GROUPS)]
                )
                new = [sums[pl.ds(k, 2), :] + v for k, v in found]
                for (k, _), v in zip(found, new):
                    sums[pl.ds(k, 2), :] = v
                return carry

            return lax.fori_loop(0, COLS, step, carry, unroll=UNROLL)

        lax.fori_loop(0, BLOCKS, blocks, 0)

        def give_back(s, carry):
            k = spilled[s, 0]
            sums[pl.ds(k, 2), :] = sums[pl.ds(k, 2), :] + sums[pl.ds(2 * (CODES + s), 2), :]
            return carry

        lax.fori_loop(0, many, give_back, 0)

    @pl.when(many > SPILL)
    def _():
        again = pltpu.make_async_copy(plain, ids, sems.at[7])
        again.start()
        again.wait()

        def blocks(block, carry):
            def step(col, carry):
                spot = block * BLOCK + col
                for k, v in resids(spot, lambda r, d: 2 * ids[d * SPOTS + spot + r * COLS]):
                    sums[pl.ds(k, 2), :] = sums[pl.ds(k, 2), :] + v
                return carry

            return lax.fori_loop(0, COLS, step, carry)

        lax.fori_loop(0, BLOCKS, blocks, 0)

    get_up.wait()

    def put_grad(block):
        rows = pl.ds(pl.multiple_of(block * BLOCK, 16), BLOCK)
        return pltpu.make_async_copy(near.at[rows], grad.at[rows], sems.at[8 + block])

    def gradient(block, carry):
        rows = pl.ds(pl.multiple_of(block * BLOCK, 16), BLOCK)
        at = pl.multiple_of(block * (2 * BLOCK), 8)
        total = jnp.concatenate(
            [lat[pl.ds(at, BLOCK, stride=2), :], lat[pl.ds(at + 1, BLOCK, stride=2), :]], axis=1
        )
        near[rows, :] = (near[rows, :].astype(F32) + 2.0 * BETA * total).astype(BF16)
        put_grad(block).start()
        return carry

    lax.fori_loop(0, BLOCKS, gradient, 0)

    def put_out(out, first, j):
        rows = pl.ds((first + j) * 16 * SHARE, 16 * SHARE)
        return pltpu.make_async_copy(raw.at[rows], out.at[j], sems.at[16 + first + j])

    def fill(m, carry, first, core, j):
        at = pl.multiple_of(owner(info[0], info[1], core, j, m) * (2 * SHARE), 8)
        rows = pl.ds(pl.multiple_of(((first + j) * 16 + m) * SHARE, 16), SHARE)
        raw[rows, :128] = (sums[pl.ds(at, SHARE, stride=2), :] * -2.0).astype(BF16)
        raw[rows, 128:] = (sums[pl.ds(at + 1, SHARE, stride=2), :] * -2.0).astype(BF16)
        return carry

    for first, core, out in ((0, 1 - info[3], send), (4, info[3], keep)):
        for j in range(4):
            lax.fori_loop(0, 16, functools.partial(fill, first=first, core=core, j=j), 0, unroll=2)
            put_out(out, first, j).start()
    for block in range(BLOCKS):
        put_grad(block).wait()
    for first, out in ((0, send), (4, keep)):
        for j in range(4):
            put_out(out, first, j).wait()


def quantizer(marked, plain, spilled, info, count, codebook, feats, above, below, weights, up):
    hbm = pl.BlockSpec(memory_space=pl.ANY)
    smem = pl.BlockSpec(memory_space=pltpu.SMEM)
    out_shape = (4, 16 * SHARE, CHANS)
    return pl.pallas_call(
        quantizer_kernel,
        in_specs=[smem] * 3 + [hbm] * 8,
        out_specs=[hbm] * 3,
        scratch_shapes=[
            pltpu.VMEM((2 * (CODES + SPILL), 128), F32),
            pltpu.VMEM((2 * (CODES + SPILL), 128), F32),
            pltpu.VMEM((2 * SPOTS, 128), F32),
            pltpu.VMEM((CODES, CHANS), BF16),
            pltpu.VMEM((SPOTS, CHANS), BF16),
            pltpu.VMEM((9, CHANS, CHANS), BF16),
            pltpu.VMEM((HERE, ROWS + 2, COLS, CHANS), BF16),
            pltpu.SMEM((DEPTHS * SPOTS,), jnp.int32),
            pltpu.SemaphoreType.DMA((24,)),
        ],
        out_shape=[
            jax.ShapeDtypeStruct((SPOTS, CHANS), BF16),
            jax.ShapeDtypeStruct(out_shape, BF16),
            jax.ShapeDtypeStruct(out_shape, BF16),
        ],
        compiler_params=pltpu.CompilerParams(vmem_limit_bytes=58 << 20),
        cost_estimate=pl.CostEstimate(
            flops=2 * 9 * SPOTS * CHANS * CHANS, bytes_accessed=32 << 20, transcendentals=0
        ),
    )(spilled, info, count, marked, plain, codebook, feats, above, below, weights, up)


def weight_kernel(info, feats, above, below, grad, send, keep, window, total, sems):
    i = pl.program_id(0)

    copies = window_copies(above, feats, below, window, sems)

    @pl.when(i == 0)
    def _():
        for copy in copies:
            copy.start()
        for copy in copies:
            copy.wait()

    clip = i // (ROWS // 4)
    row = (i % (ROWS // 4)) * 4
    mid = grad[...].astype(F32)
    wide = jnp.concatenate(
        [shifted(mid, -1).astype(BF16), grad[...], shifted(mid, 1).astype(BF16)], axis=1
    )
    for a in range(3):
        part = window[clip, pl.ds(row + a, 4)].reshape(BLOCK, CHANS)
        term = lax.dot_general(part, wide, (((0,), (0,)), ((), ())), preferred_element_type=F32)

        @pl.when(i == 0)
        def _():
            total[pl.ds(a * CHANS, CHANS), :] = term

        @pl.when(i > 0)
        def _():
            total[pl.ds(a * CHANS, CHANS), :] += term

    @pl.when(i == BLOCKS - 1)
    def _():
        for out, core in ((send, 1 - info[3]), (keep, info[3])):
            for j in range(4):
                for m in range(16):
                    near = jnp.where(core == 0, info[0], info[1])
                    b = jnp.minimum(core * 64 + (near + j) % 4 * 16 + m, 95)
                    rows = total[pl.ds(pl.multiple_of(b * 8, 8), 8), :]
                    for q in range(3):
                        out[j, m, pl.ds(8 * q, 8), :] = rows[:, q * CHANS : (q + 1) * CHANS]


def weight_sums(info, feats, above, below, grad):
    shape = (4, 16, 24, CHANS)
    return pl.pallas_call(
        weight_kernel,
        grid_spec=pltpu.PrefetchScalarGridSpec(
            num_scalar_prefetch=1,
            grid=(BLOCKS,),
            in_specs=[
                pl.BlockSpec(memory_space=pl.ANY),
                pl.BlockSpec(memory_space=pl.ANY),
                pl.BlockSpec(memory_space=pl.ANY),
                pl.BlockSpec((BLOCK, CHANS), lambda i, *_: (i, 0)),
            ],
            out_specs=[
                pl.BlockSpec(shape, lambda i, *_: (0, 0, 0, 0)),
                pl.BlockSpec(shape, lambda i, *_: (0, 0, 0, 0)),
            ],
            scratch_shapes=[
                pltpu.VMEM((HERE, ROWS + 2, COLS, CHANS), BF16),
                pltpu.VMEM((3 * CHANS, 3 * CHANS), F32),
                pltpu.SemaphoreType.DMA((3 * HERE,)),
            ],
        ),
        out_shape=[jax.ShapeDtypeStruct(shape, F32)] * 2,
        compiler_params=pltpu.CompilerParams(
            vmem_limit_bytes=32 << 20, dimension_semantics=("arbitrary",)
        ),
        cost_estimate=pl.CostEstimate(
            flops=2 * 9 * SPOTS * CHANS * CHANS, bytes_accessed=8 << 20, transcendentals=0
        ),
    )(info, feats, above, below, grad)


def back_kernel(grad, above, below, weights, out, window, sems):
    i = pl.program_id(0)

    copies = window_copies(above, grad, below, window, sems)

    @pl.when(i == 0)
    def _():
        for copy in copies:
            copy.start()
        for copy in copies:
            copy.wait()

    clip = i // (ROWS // 4)
    row = (i % (ROWS // 4)) * 4
    cols = [None] * 3
    for a in range(3):
        part = window[clip, pl.ds(row + 2 - a, 4)].reshape(BLOCK, CHANS)
        for b in range(3):
            term = lax.dot_general(
                part, weights[3 * a + b], (((1,), (1,)), ((), ())), preferred_element_type=F32
            )
            cols[b] = term if a == 0 else cols[b] + term
    back = shifted(cols[0], -1) + cols[1] + shifted(cols[2], 1)
    out[...] = back.astype(BF16)


def feature_grads(grad, above, below, weights):
    return pl.pallas_call(
        back_kernel,
        grid=(BLOCKS,),
        in_specs=[
            pl.BlockSpec(memory_space=pl.ANY),
            pl.BlockSpec(memory_space=pl.ANY),
            pl.BlockSpec(memory_space=pl.ANY),
            pl.BlockSpec((9, CHANS, CHANS), lambda i: (0, 0, 0)),
        ],
        out_specs=pl.BlockSpec((BLOCK, CHANS), lambda i: (i, 0)),
        scratch_shapes=[
            pltpu.VMEM((HERE, ROWS + 2, COLS, CHANS), BF16),
            pltpu.SemaphoreType.DMA((3 * HERE,)),
        ],
        out_shape=jax.ShapeDtypeStruct((SPOTS, CHANS), BF16),
        compiler_params=pltpu.CompilerParams(
            vmem_limit_bytes=32 << 20, dimension_semantics=("arbitrary",)
        ),
        cost_estimate=pl.CostEstimate(
            flops=2 * 9 * SPOTS * CHANS * CHANS, bytes_accessed=8 << 20, transcendentals=0
        ),
    )(grad, above, below, weights)


def edges(array):
    n = lax.axis_size("tile")
    up = [(i, i + 1) for i in range(n - 1)]
    down = [(i + 1, i) for i in range(n - 1)]
    above = lax.ppermute(array[:, -1:], "tile", up)
    below = lax.ppermute(array[:, :1], "tile", down)
    return above, below


def on_device(features, conv_weight, codebook, codes, upstream):
    info = place()
    above, below = edges(features)
    marked, spilled, count = entry_lists(codes)
    grad, send, keep = quantizer(
        marked.reshape(-1), codes.reshape(-1), spilled, info, count, codebook, features, above,
        below, conv_weight, upstream.reshape(SPOTS, CHANS),
    )
    got = lax.ppermute(send, BOTH, SWAP)
    grad4 = grad.reshape(features.shape)
    grad_above, grad_below = edges(grad4)
    weight_send, weight_keep = weight_sums(info, features, above, below, grad)
    weight_got = lax.ppermute(weight_send.astype(BF16), BOTH, SWAP)
    weight_chip = (weight_keep + weight_got.astype(F32)).astype(BF16)
    keep, got, grad_above, grad_below, weight_chip = lax.optimization_barrier(
        (keep, got, grad_above, grad_below, weight_chip)
    )
    weight_ring = weight_chip[0].astype(F32)
    for d in (1, 2, 3):
        weight_ring = weight_ring + lax.ppermute(weight_chip[d], BOTH, first_ring(d)).astype(F32)
    chip = (keep.astype(F32) + got.astype(F32)).astype(BF16).reshape(4, 16, SHARE, CHANS)
    others = [lax.ppermute(chip[d], BOTH, first_ring(d)) for d in (1, 2, 3)]
    plane = lax.all_to_all(weight_ring.astype(BF16), BOTH, 0, 0, axis_index_groups=PLANES)
    piece = plane.astype(F32).sum(0).astype(BF16)
    pieces = lax.all_to_all(
        jnp.broadcast_to(piece[None], (16, 24, CHANS)), BOTH, 0, 0, axis_index_groups=PLANES
    )
    back = feature_grads(grad4, grad_above, grad_below, conv_weight)
    others, pieces, back = lax.optimization_barrier((others, pieces, back))
    around = [lax.ppermute(pieces, BOTH, first_ring(d)) for d in (1, 2, 3)]
    ring = chip[0].astype(F32)
    for other in others:
        ring = ring + other.astype(F32)
    plane = lax.all_to_all(ring.astype(BF16), BOTH, 0, 0, axis_index_groups=PLANES)
    code_part = plane.astype(F32).sum(0)
    core = info[3]
    at = jnp.where(core == 0, info[0], info[1])
    turned = jnp.concatenate([jnp.stack(around[::-1] + [pieces])] * 2)
    mine = lax.dynamic_slice_in_dim(turned, 3 - at, 4, axis=0)
    theirs = lax.ppermute(mine, BOTH, SWAP)
    weight_grad = jnp.where(core == 0, jnp.stack([mine, theirs]), jnp.stack([theirs, mine]))
    weight_grad = weight_grad.reshape(128, 24, CHANS)[:96].reshape(96, 3, 8, CHANS)
    weight_grad = weight_grad.transpose(0, 2, 1, 3).reshape(3, CHANS, 3, CHANS)
    weight_grad = weight_grad.transpose(0, 2, 1, 3).reshape(9, CHANS, CHANS).astype(F32)
    return back.reshape(features.shape), weight_grad, code_part


def solution(mesh):
    in_specs = (
        P("clip", "tile", None, None),
        P(),
        P(),
        P(None, "clip", "tile", None),
        P("clip", "tile", None, None),
    )
    out_specs = (P("clip", "tile", None, None), P(), P(BOTH, None))
    return jax.shard_map(
        on_device, mesh=mesh, in_specs=in_specs, out_specs=out_specs, check_vma=False
    )
```

time: 204 us -> 180 us (0.88)
  waiting for transfers between devices: 45.2 us -> 27.5 us
  starting transfers between devices: 30.2 us -> 45.3 us
  local copies, waits for them, and re-layouts: 18.4 us -> 11.8 us
  Pallas kernels: 74.1 us -> 67.5 us
  blocking collectives: 22.9 us -> 16.8 us
    ppermute x3 -> x10, waiting for transfers between devices: 26.9 us -> 7.63 us  [the longest x3 7.61 us: on_device(): around = [lax.ppermute(pieces, BOTH, first_ring(d)) for d in (1, 2, 3)]]
    ppermute x2, waiting for transfers between devices: 15.2 us -> 0.83 us  [edges(): above = lax.ppermute(array[:, -1:], 'tile', up)]
    ppermute x3 -> x10, starting transfers between devices: 5.21 us -> 16.7 us  [the longest x1 5.27 us: on_device(): theirs = lax.ppermute(mine, BOTH, SWAP)]
    all_to_all x1 -> x2, waiting for transfers between devices: 0.01 us -> 10.9 us  [the longest x1 10.9 us: on_device(): lax.all_to_all(ring.astype(BF16), BOTH, 0, 0, axis_index_groups=PLANES)]
    ppermute x2, waiting for transfers between devices: 0.82 us -> 8.08 us  [edges(): below = lax.ppermute(array[:, :1], 'tile', down)]
    pallas_call x1 -> x2, Pallas kernels: 52.5 us -> 45.8 us  [the longest x1 43.4 us: quantizer(): pl.pallas_call(quantizer_kernel, in_specs=[smem] * 3 + [hbm] * 8, out_spe...]
    all_to_all x1, blocking collectives: 22.9 us -> 16.8 us  [on_device(): lax.all_to_all(weight_ring.astype(BF16), BOTH, 0, 0, axis_index_groups=PL...]
    reshape x6 -> x0, local copies, waits for them, and re-layouts: 4.94 us -> none  [the longest x4 1.83 us: grouped(): return (2 * array).reshape(GROUP, GROUPS).T.reshape(-1)]
  transfers between devices with their start and end apart: 10 -> 18, of which waited for: 5 -> 7; matrix products, arithmetic and copies ran while one was open for 7% -> 7% of each run, Pallas kernels for 11% -> 13%
where the time goes in v2:
time: 180 us; the launch traced here: 179 us
  Pallas kernels  67.5 us (38%)
  starting transfers between devices  45.3 us (25%)
  waiting for transfers between devices  27.5 us (15%)
  blocking collectives  16.8 us (9%)
  local copies, waits for them, and re-layouts  11.8 us (7%)
  other arithmetic  9.36 us (5%)
    pallas_call x1, Pallas kernels, quantizer(): pl.pallas_call(quantizer_kernel, in_specs=[smem] * 3 + [hbm] * 8, out_spe...  43.4 us
    all_to_all x1, blocking collectives, on_device(): lax.all_to_all(weight_ring.astype(BF16), BOTH, 0, 0, axis_index_groups=PL...  16.8 us
    pallas_call x1, Pallas kernels, weight_sums(): pl.pallas_call(weight_kernel, grid_spec=pltpu.PrefetchScalarGridSpec(num_...  13.8 us
    all_to_all x1, waiting for transfers between devices, on_device(): lax.all_to_all(ring.astype(BF16), BOTH, 0, 0, axis_index_groups=PLANES)  10.9 us
    ppermute x2, starting transfers between devices, edges(): above = lax.ppermute(array[:, -1:], 'tile', up)  9.42 us
    all_to_all x1, starting transfers between devices, on_device(): lax.all_to_all(jnp.broadcast_to(piece[None], (16, 24, CHANS)), BOTH, 0, 0...  8.28 us
    ppermute x2, waiting for transfers between devices, edges(): below = lax.ppermute(array[:, :1], 'tile', down)  8.08 us
    pallas_call x1, Pallas kernels, feature_grads(): pl.pallas_call(back_kernel, grid=(BLOCKS,), in_specs=[pl.BlockSpec(memory...  7.89 us
  transfers between devices with their start and end apart: 18, of which 7 were waited for; matrix products, arithmetic and copies ran while one was open for 7% of the time, Pallas kernels for 13%

profile of v2, /device:TPU:1, one launch (start us, length us, event | category | flops | bytes accessed | tf_op | source)
XLA Modules:
  0.0 179.2 jit_solution(301001509743358421)
XLA Ops:
  0.6 1.0 fusion.8
  1.6 6.3 %collective-permute-start = (bf16[2,1,128,256]{3,2,1,0:T(8,128)(2,1)S(1)}, bf16[2,1,128,256]{3,2,1,0:T(8,128)(2,1)S(1)}, u32[]{:S(2)}, u32[]{:S(2)}) collective-permute-start(bf16[2,1,128,256]{3,2,1,0:T(8,128)(2,1)S(1)} %get-tuple-element.46), channel_id=1, source_target_pairs={{0,1},{1,2},{2,3},{3,4},{4,5},{5,6},{6,7},{8,9},{9,10},{10,11},{11... | collective-permute-start | bytes 393224 | tf_op jit(solution)/shard_map/ppermute | solution.py:456
  8.0 1.3 collective-permute-start.1
  9.3 2.4 %shard_map.76 = (s32[128,128]{1,0:T(8,128)}, s32[64,128]{1,0:T(8,128)}, s32[8,128]{1,0:T(8,128)}) custom-call(s32[128,128]{1,0:T(8,128)} %bitcast.57), custom_call_target="tpu_custom_call" | custom-call | tf_op jit(solution)/shard_map/pallas_call | solution.py:124
  12.4 2.8 %collective-permute-done.1.below = bf16[2,1,128,256]{3,2,1,0:T(8,128)(2,1)S(1)} collective-permute-done((bf16[2,1,128,256]{3,2,1,0:T(8,128)(2,1)S(1)}, bf16[2,1,128,256]{3,2,1,0:T(8,128)(2,1)S(1)}, u32[]{:S(2)}, u32[]{:S(2)}) %collective-permute-start.1) | collective-permute-done | bytes 131104 | tf_op jit(solution)/shard_map/ppermute | solution.py:457
  15.8 43.4 %shard_map.77 = (bf16[4096,256]{1,0:T(8,128)(2,1)}, bf16[4,2048,256]{2,1,0:T(8,128)(2,1)}, bf16[4,2048,256]{2,1,0:T(8,128)(2,1)}) custom-call(s32[64,128]{1,0:T(8,128)} %get-tuple-element.21.spilled, s32[4]{0:T(128)} %pad_add_fusion.info, s32[8,128]{1,0:T(8,128)} %get-tuple-element.22.count, s32[16384]{0:T(1024)} %bitcast.60, s32[16384]{0:T(1024)} %bitcast.58, ...), custom_call_target="tpu_custom_call" | custom-call | flops 4831838208 | bytes 33554432 | tf_op jit(solution)/shard_map/pallas_call | solution.py:299
  59.2 2.2 %collective-permute-start.2 = (bf16[4,2048,256]{2,1,0:T(8,128)(2,1)}, bf16[4,2048,256]{2,1,0:T(8,128)(2,1)S(1)}, u32[]{:S(2)}, u32[]{:S(2)}) collective-permute-start(bf16[4,2048,256]{2,1,0:T(8,128)(2,1)} %get-tuple-element.25), channel_id=1, source_target_pairs={{0,8},{8,0},{64,72},{72,64},{1,9},{9,1},{65,73},{73,65},{16,24},{2... | collective-permute-start | bytes 12582920 | tf_op jit(solution)/shard_map/ppermute | solution.py:469
  61.4 1.6 copy-done.1
  64.8 13.8 %shard_map.78 = (f32[4,16,24,256]{3,2,1,0:T(8,128)S(1)}, f32[4,16,24,256]{3,2,1,0:T(8,128)S(1)}) custom-call(s32[4]{0:T(128)S(1)} %copy-done.3, bf16[2,16,128,256]{3,2,1,0:T(8,128)(2,1)S(1)} %copy-done, bf16[2,1,128,256]{3,2,1,0:T(8,128)(2,1)S(1)} %copy-done.6, bf16[2,1,128,256]{3,2,1,0:T(8,128)(2,1)S(1)} %copy-done.8, bf16[4096,256]{1,0:T(8,128)(2,1)S(1)} %copy-done.1), custom_call_target="tpu_custom_call" | custom-call | flops 4831838208 | bytes 8388608 | tf_op jit(solution)/shard_map/pallas_call | solution.py:370
  78.9 3.1 %collective-permute-start.3 = (bf16[2,1,128,256]{3,2,1,0:T(8,128)(2,1)S(1)}, bf16[2,1,128,256]{3,2,1,0:T(8,128)(2,1)S(1)}, u32[]{:S(2)}, u32[]{:S(2)}) collective-permute-start(bf16[2,1,128,256]{3,2,1,0:T(8,128)(2,1)S(1)} %get-tuple-element.44), channel_id=1, source_target_pairs={{0,1},{1,2},{2,3},{3,4},{4,5},{5,6},{6,7},{8,9},{9,10},{10,11},{11... | collective-permute-start | bytes 393224 | tf_op jit(solution)/shard_map/ppermute | solution.py:456
  82.0 1.3 collective-permute-start.4
  84.3 5.3 %collective-permute-done.4.below = bf16[2,1,128,256]{3,2,1,0:T(8,128)(2,1)S(1)} collective-permute-done((bf16[2,1,128,256]{3,2,1,0:T(8,128)(2,1)S(1)}, bf16[2,1,128,256]{3,2,1,0:T(8,128)(2,1)S(1)}, u32[]{:S(2)}, u32[]{:S(2)}) %collective-permute-start.4) | collective-permute-done | bytes 131104 | tf_op jit(solution)/shard_map/ppermute | solution.py:457
  89.7 3.0 %collective-permute-start.10 = (bf16[16,24,256]{2,1,0:T(8,128)(2,1)S(1)}, bf16[16,24,256]{2,1,0:T(8,128)(2,1)S(1)}, u32[]{:S(2)}, u32[]{:S(2)}) collective-permute-start(bf16[16,24,256]{2,1,0:T(8,128)(2,1)S(1)} %get-tuple-element.49), channel_id=1, source_target_pairs={{0,4},{8,40},{64,68},{72,104},{1,5},{9,41},{65,69},{73,105},{16,20... | collective-permute-start | bytes 589832 | tf_op jit(solution)/shard_map/ppermute | solution.py:480
  94.2 1.1 add_convert_fusion
  95.3 2.1 %fusion.6 = (bf16[1,2048,256]{2,1,0:T(8,128)(2,1)}, bf16[1,2048,256]{2,1,0:T(8,128)(2,1)}, bf16[1,2048,256]{2,1,0:T(8,128)(2,1)}, bf16[1,2048,256]{2,1,0:T(8,128)(2,1)}) fusion(bf16[4,2048,256]{2,1,0:T(8,128)(2,1)S(1)} %add_convert_fusion), kind=kLoop, calls=%fused_computation.27 | loop fusion | bytes 8388608 | tf_op jit(solution)/shard_map/slice | solution.py:491
  97.8 2.7 %collective-permute-start.7 = (bf16[16,128,256]{2,1,0:T(8,128)(2,1)}, bf16[16,128,256]{2,1,0:T(8,128)(2,1)}, u32[]{:S(2)}, u32[]{:S(2)}) collective-permute-start(bf16[16,128,256]{2,1,0:T(8,128)(2,1)} %bitcast.10), channel_id=1, source_target_pairs={{0,4},{8,40},{64,68},{72,104},{1,5},{9,41},{65,69},{73,105},{16,20... | collective-permute-start | bytes 3145736 | tf_op jit(solution)/shard_map/ppermute | solution.py:482
  100.7 16.8 %all_to_all.15 = bf16[16,24,256]{2,1,0:T(8,128)(2,1)} all-to-all(bf16[16,24,256]{2,1,0:T(8,128)(2,1)S(1)} %fusion.5), channel_id=1, replica_groups={{0,64,1,65,16,80,17,81,32,96,33,97,48,112,49,113},{2,66,3,67,18,82,19,8..., dimensions={0} | all-to-all | bytes 393216 | tf_op jit(solution)/shard_map/all_to_all | solution.py:483
  117.5 1.0 reduce_sum.21
  119.2 8.3 %all-to-all-start.1 = ((bf16[16,24,256]{2,1,0:T(8,128)(2,1)}), bf16[16,24,256]{2,1,0:T(8,128)(2,1)}, u32[]{:S(2)}, u32[]{:S(2)}) async-start(bf16[16,24,256]{2,1,0:T(8,128)(2,1)} %broadcast_in_dim.2), calls=%async_computation.1 | async-start | bytes 393216 | tf_op jit(solution)/shard_map/all_to_all | solution.py:485
  127.5 7.9 %shard_map.79 = bf16[4096,256]{1,0:T(8,128)(2,1)} custom-call(bf16[2,16,128,256]{3,2,1,0:T(8,128)(2,1)S(1)} %bitcast.52, bf16[2,1,128,256]{3,2,1,0:T(8,128)(2,1)S(1)} %collective-permute-done.3.above, bf16[2,1,128,256]{3,2,1,0:T(8,128)(2,1)S(1)} %collective-permute-done.4.below, bf16[9,256,256]{2,1,0:T(8,128)(2,1)S(1)} %copy-done.4), custom_call_target="tpu_custom_call" | custom-call | flops 4831838208 | bytes 8388608 | tf_op jit(solution)/shard_map/pallas_call | solution.py:428
  135.4 2.8 %collective-permute-start.12 = (bf16[16,24,256]{2,1,0:T(8,128)(2,1)}, bf16[16,24,256]{2,1,0:T(8,128)(2,1)S(1)}, u32[]{:S(2)}, u32[]{:S(2)}) collective-permute-start(bf16[16,24,256]{2,1,0:T(8,128)(2,1)} %all-to-all-done.1), channel_id=1, source_target_pairs={{0,6},{8,56},{64,70},{72,120},{1,7},{9,57},{65,71},{73,121},{16,22... | collective-permute-start | bytes 589832 | tf_op jit(solution)/shard_map/ppermute | solution.py:490
  139.2 4.0 %collective-permute-done.12 = bf16[16,24,256]{2,1,0:T(8,128)(2,1)S(1)} collective-permute-done((bf16[16,24,256]{2,1,0:T(8,128)(2,1)}, bf16[16,24,256]{2,1,0:T(8,128)(2,1)S(1)}, u32[]{:S(2)}, u32[]{:S(2)}) %collective-permute-start.12) | collective-permute-done | bytes 196640 | tf_op jit(solution)/shard_map/ppermute | solution.py:490
  143.3 1.3 collective-permute-done.13
  144.6 2.3 %collective-permute-done.14 = bf16[16,24,256]{2,1,0:T(8,128)(2,1)S(1)} collective-permute-done((bf16[16,24,256]{2,1,0:T(8,128)(2,1)}, bf16[16,24,256]{2,1,0:T(8,128)(2,1)S(1)}, u32[]{:S(2)}, u32[]{:S(2)}) %collective-permute-start.14) | collective-permute-done | bytes 196640 | tf_op jit(solution)/shard_map/ppermute | solution.py:490
  146.9 0.9 bitcast_dynamic-update-slice_fusion
  147.9 1.0 bitcast_dynamic-update-slice_fusion.1
  149.0 5.3 %collective-permute-start.15 = (bf16[4,16,24,256]{3,2,1,0:T(8,128)(2,1)S(1)}, bf16[4,16,24,256]{3,2,1,0:T(8,128)(2,1)}, u32[]{:S(2)}, u32[]{:S(2)}) collective-permute-start(bf16[4,16,24,256]{3,2,1,0:T(8,128)(2,1)S(1)} %constant_dynamic-slice_fusion), channel_id=1, source_target_pairs={{0,8},{8,0},{64,72},{72,64},{1,9},{9,1},{65,73},{73,65},{16,24},{2... | collective-permute-start | bytes 2359304 | tf_op jit(solution)/shard_map/ppermute | solution.py:500
  154.3 3.5 %fusion.2 = bf16[16,128,256]{2,1,0:T(8,128)(2,1)} fusion(bf16[16,128,256]{2,1,0:T(8,128)(2,1)S(1)} %bitcast.55, bf16[16,128,256]{2,1,0:T(8,128)(2,1)} %collective-permute-done.8, bf16[16,128,256]{2,1,0:T(8,128)(2,1)} %collective-permute-done.7, bf16[16,128,256]{2,1,0:T(8,128)(2,1)} %collective-permute-done.6), kind=kLoop, calls=%fused_computation.5 | loop fusion | flops 4194304 | bytes 5242880 | tf_op jit(solution)/shard_map/convert_element_type | solution.py:494
  157.8 6.0 %all-to-all-start.2 = ((bf16[16,128,256]{2,1,0:T(8,128)(2,1)}), bf16[16,128,256]{2,1,0:T(8,128)(2,1)S(1)}, u32[]{:S(2)}, u32[]{:S(2)}) async-start(bf16[16,128,256]{2,1,0:T(8,128)(2,1)} %fusion.2), calls=%async_computation.2 | async-start | bytes 2097152 | tf_op jit(solution)/shard_map/all_to_all | solution.py:494
  163.8 1.7 maximum_select_fusion
  165.9 1.6 copy.9
  167.5 10.9 %all-to-all-done.2 = bf16[16,128,256]{2,1,0:T(8,128)(2,1)S(1)} async-done(((bf16[16,128,256]{2,1,0:T(8,128)(2,1)}), bf16[16,128,256]{2,1,0:T(8,128)(2,1)S(1)}, u32[]{:S(2)}, u32[]{:S(2)}) %all-to-all-start.2) | async-done | bytes 1048608 | tf_op jit(solution)/shard_map/all_to_all | solution.py:494
  (58 shorter events, 9.5 us)
Async XLA Ops:
  1.6 10.8 %collective-permute-start = (bf16[2,1,128,256]{3,2,1,0:T(8,128)(2,1)S(1)}, bf16[2,1,128,256]{3,2,1,0:T(8,128)(2,1)S(1)}, u32[]{:S(2)}, u32[]{:S(2)}) collective-permute-start(bf16[2,1,128,256]{3,2,1,0:T(8,128)(2,1)S(1)} %get-tuple-element.46), channel_id=1, source_target_pairs={{0,1},{1,2},{2,3},{3,4},{4,5},{5,6},{6,7},{8,9},{9,10},{10,11},{11... | collective-permute-start | bytes 393224 | tf_op jit(solution)/shard_map/ppermute | solution.py:456
  8.0 7.2 %collective-permute-start.1 = (bf16[2,1,128,256]{3,2,1,0:T(8,128)(2,1)S(1)}, bf16[2,1,128,256]{3,2,1,0:T(8,128)(2,1)S(1)}, u32[]{:S(2)}, u32[]{:S(2)}) collective-permute-start(bf16[2,1,128,256]{3,2,1,0:T(8,128)(2,1)S(1)} %get-tuple-element.45), channel_id=1, source_target_pairs={{1,0},{2,1},{3,2},{4,3},{5,4},{6,5},{7,6},{9,8},{10,9},{11,10},{12... | collective-permute-start | bytes 393224 | tf_op jit(solution)/shard_map/ppermute | solution.py:457
  12.4 2.8 %copy-start.5 = (bf16[2,1,128,256]{3,2,1,0:T(8,128)(2,1)}, bf16[2,1,128,256]{3,2,1,0:T(8,128)(2,1)S(1)}, u32[]{:S(2)}) copy-start(bf16[2,1,128,256]{3,2,1,0:T(8,128)(2,1)S(1)} %collective-permute-done.above) | copy-start | bytes 393220
  15.2 0.7 copy-start.7
  15.8 45.6 %copy-start = (bf16[2,16,128,256]{3,2,1,0:T(8,128)(2,1)S(1)}, bf16[2,16,128,256]{3,2,1,0:T(8,128)(2,1)}, u32[]{:S(2)}) copy-start(bf16[2,16,128,256]{3,2,1,0:T(8,128)(2,1)} %feats.3) | copy-start | bytes 6291460
  15.8 45.6 %copy-start.3 = (s32[4]{0:T(128)S(1)}, s32[4]{0:T(128)}, u32[]{:S(2)}) copy-start(s32[4]{0:T(128)} %pad_add_fusion.info) | copy-start | bytes 52
  59.2 30.4 %collective-permute-start.2 = (bf16[4,2048,256]{2,1,0:T(8,128)(2,1)}, bf16[4,2048,256]{2,1,0:T(8,128)(2,1)S(1)}, u32[]{:S(2)}, u32[]{:S(2)}) collective-permute-start(bf16[4,2048,256]{2,1,0:T(8,128)(2,1)} %get-tuple-element.25), channel_id=1, source_target_pairs={{0,8},{8,0},{64,72},{72,64},{1,9},{9,1},{65,73},{73,65},{16,24},{2... | collective-permute-start | bytes 12582920 | tf_op jit(solution)/shard_map/ppermute | solution.py:469
  61.4 1.6 copy-start.1
  63.0 0.9 copy-start.6
  63.9 0.9 copy-start.8
  78.8 4.5 %collective-permute-start.5 = (bf16[4,16,24,256]{3,2,1,0:T(8,128)(2,1)S(1)}, bf16[4,16,24,256]{3,2,1,0:T(8,128)(2,1)S(1)}, u32[]{:S(2)}, u32[]{:S(2)}) collective-permute-start(bf16[4,16,24,256]{3,2,1,0:T(8,128)(2,1)S(1)} %convert_element_type.74), channel_id=1, source_target_pairs={{0,8},{8,0},{64,72},{72,64},{1,9},{9,1},{65,73},{73,65},{16,24},{2... | collective-permute-start | bytes 2359304 | tf_op jit(solution)/shard_map/ppermute | solution.py:473
  78.9 5.5 %collective-permute-start.3 = (bf16[2,1,128,256]{3,2,1,0:T(8,128)(2,1)S(1)}, bf16[2,1,128,256]{3,2,1,0:T(8,128)(2,1)S(1)}, u32[]{:S(2)}, u32[]{:S(2)}) collective-permute-start(bf16[2,1,128,256]{3,2,1,0:T(8,128)(2,1)S(1)} %get-tuple-element.44), channel_id=1, source_target_pairs={{0,1},{1,2},{2,3},{3,4},{4,5},{5,6},{6,7},{8,9},{9,10},{10,11},{11... | collective-permute-start | bytes 393224 | tf_op jit(solution)/shard_map/ppermute | solution.py:456
  82.0 7.7 %collective-permute-start.4 = (bf16[2,1,128,256]{3,2,1,0:T(8,128)(2,1)S(1)}, bf16[2,1,128,256]{3,2,1,0:T(8,128)(2,1)S(1)}, u32[]{:S(2)}, u32[]{:S(2)}) collective-permute-start(bf16[2,1,128,256]{3,2,1,0:T(8,128)(2,1)S(1)} %get-tuple-element.43), channel_id=1, source_target_pairs={{1,0},{2,1},{3,2},{4,3},{5,4},{6,5},{7,6},{9,8},{10,9},{11,10},{12... | collective-permute-start | bytes 393224 | tf_op jit(solution)/shard_map/ppermute | solution.py:457
  83.3 10.9 %copy-start.9 = (bf16[4,2048,256]{2,1,0:T(8,128)(2,1)S(1)}, bf16[4,2048,256]{2,1,0:T(8,128)(2,1)}, u32[]{:S(2)}) copy-start(bf16[4,2048,256]{2,1,0:T(8,128)(2,1)} %get-tuple-element.29) | copy-start | bytes 12582916
  89.7 10.9 %collective-permute-start.10 = (bf16[16,24,256]{2,1,0:T(8,128)(2,1)S(1)}, bf16[16,24,256]{2,1,0:T(8,128)(2,1)S(1)}, u32[]{:S(2)}, u32[]{:S(2)}) collective-permute-start(bf16[16,24,256]{2,1,0:T(8,128)(2,1)S(1)} %get-tuple-element.49), channel_id=1, source_target_pairs={{0,4},{8,40},{64,68},{72,104},{1,5},{9,41},{65,69},{73,105},{16,20... | collective-permute-start | bytes 589832 | tf_op jit(solution)/shard_map/ppermute | solution.py:480
  92.7 7.9 %collective-permute-start.11 = (bf16[16,24,256]{2,1,0:T(8,128)(2,1)S(1)}, bf16[16,24,256]{2,1,0:T(8,128)(2,1)S(1)}, u32[]{:S(2)}, u32[]{:S(2)}) collective-permute-start(bf16[16,24,256]{2,1,0:T(8,128)(2,1)S(1)} %get-tuple-element.48), channel_id=1, source_target_pairs={{0,6},{8,56},{64,70},{72,120},{1,7},{9,57},{65,71},{73,121},{16,22... | collective-permute-start | bytes 589832 | tf_op jit(solution)/shard_map/ppermute | solution.py:480
  93.5 7.1 %collective-permute-start.9 = (bf16[16,24,256]{2,1,0:T(8,128)(2,1)S(1)}, bf16[16,24,256]{2,1,0:T(8,128)(2,1)S(1)}, u32[]{:S(2)}, u32[]{:S(2)}) collective-permute-start(bf16[16,24,256]{2,1,0:T(8,128)(2,1)S(1)} %get-tuple-element.47), channel_id=1, source_target_pairs={{0,2},{8,24},{64,66},{72,88},{1,3},{9,25},{65,67},{73,89},{16,18},... | collective-permute-start | bytes 589832 | tf_op jit(solution)/shard_map/ppermute | solution.py:480
  95.3 32.2 %copy-start.4 = (bf16[9,256,256]{2,1,0:T(8,128)(2,1)S(1)}, bf16[9,256,256]{2,1,0:T(8,128)(2,1)}, u32[]{:S(2)}) copy-start(bf16[9,256,256]{2,1,0:T(8,128)(2,1)} %weights.3) | copy-start | bytes 3538948
  97.4 30.1 %copy-start.2 = (bf16[4096,256]{1,0:T(8,128)(2,1)S(1)}, bf16[4096,256]{1,0:T(8,128)(2,1)}, u32[]{:S(2)}) copy-start(bf16[4096,256]{1,0:T(8,128)(2,1)} %get-tuple-element.26.grad) | copy-start | bytes 6291460
  97.4 38.0 %collective-permute-start.6 = (bf16[16,128,256]{2,1,0:T(8,128)(2,1)}, bf16[16,128,256]{2,1,0:T(8,128)(2,1)}, u32[]{:S(2)}, u32[]{:S(2)}) collective-permute-start(bf16[16,128,256]{2,1,0:T(8,128)(2,1)} %bitcast.9), channel_id=1, source_target_pairs={{0,2},{8,24},{64,66},{72,88},{1,3},{9,25},{65,67},{73,89},{16,18},... | collective-permute-start | bytes 3145736 | tf_op jit(solution)/shard_map/ppermute | solution.py:482
  97.8 37.5 %collective-permute-start.7 = (bf16[16,128,256]{2,1,0:T(8,128)(2,1)}, bf16[16,128,256]{2,1,0:T(8,128)(2,1)}, u32[]{:S(2)}, u32[]{:S(2)}) collective-permute-start(bf16[16,128,256]{2,1,0:T(8,128)(2,1)} %bitcast.10), channel_id=1, source_target_pairs={{0,4},{8,40},{64,68},{72,104},{1,5},{9,41},{65,69},{73,105},{16,20... | collective-permute-start | bytes 3145736 | tf_op jit(solution)/shard_map/ppermute | solution.py:482
  100.6 34.8 %collective-permute-start.8 = (bf16[16,128,256]{2,1,0:T(8,128)(2,1)}, bf16[16,128,256]{2,1,0:T(8,128)(2,1)}, u32[]{:S(2)}, u32[]{:S(2)}) collective-permute-start(bf16[16,128,256]{2,1,0:T(8,128)(2,1)} %bitcast.11), channel_id=1, source_target_pairs={{0,6},{8,56},{64,70},{72,120},{1,7},{9,57},{65,71},{73,121},{16,22... | collective-permute-start | bytes 3145736 | tf_op jit(solution)/shard_map/ppermute | solution.py:482
  119.2 16.2 %all-to-all-start.1 = ((bf16[16,24,256]{2,1,0:T(8,128)(2,1)}), bf16[16,24,256]{2,1,0:T(8,128)(2,1)}, u32[]{:S(2)}, u32[]{:S(2)}) async-start(bf16[16,24,256]{2,1,0:T(8,128)(2,1)} %broadcast_in_dim.2), calls=%async_computation.1 | async-start | bytes 393216 | tf_op jit(solution)/shard_map/all_to_all | solution.py:485
  135.4 7.9 %collective-permute-start.12 = (bf16[16,24,256]{2,1,0:T(8,128)(2,1)}, bf16[16,24,256]{2,1,0:T(8,128)(2,1)S(1)}, u32[]{:S(2)}, u32[]{:S(2)}) collective-permute-start(bf16[16,24,256]{2,1,0:T(8,128)(2,1)} %all-to-all-done.1), channel_id=1, source_target_pairs={{0,6},{8,56},{64,70},{72,120},{1,7},{9,57},{65,71},{73,121},{16,22... | collective-permute-start | bytes 589832 | tf_op jit(solution)/shard_map/ppermute | solution.py:490
  138.2 6.3 %collective-permute-start.13 = (bf16[16,24,256]{2,1,0:T(8,128)(2,1)}, bf16[16,24,256]{2,1,0:T(8,128)(2,1)S(1)}, u32[]{:S(2)}, u32[]{:S(2)}) collective-permute-start(bf16[16,24,256]{2,1,0:T(8,128)(2,1)} %all-to-all-done.1), channel_id=1, source_target_pairs={{0,4},{8,40},{64,68},{72,104},{1,5},{9,41},{65,69},{73,105},{16,20... | collective-permute-start | bytes 589832 | tf_op jit(solution)/shard_map/ppermute | solution.py:490
  138.6 8.3 %collective-permute-start.14 = (bf16[16,24,256]{2,1,0:T(8,128)(2,1)}, bf16[16,24,256]{2,1,0:T(8,128)(2,1)S(1)}, u32[]{:S(2)}, u32[]{:S(2)}) collective-permute-start(bf16[16,24,256]{2,1,0:T(8,128)(2,1)} %all-to-all-done.1), channel_id=1, source_target_pairs={{0,2},{8,24},{64,66},{72,88},{1,3},{9,25},{65,67},{73,89},{16,18},... | collective-permute-start | bytes 589832 | tf_op jit(solution)/shard_map/ppermute | solution.py:490
  147.8 6.4 %copy-start.10 = (bf16[1,2048,256]{2,1,0:T(8,128)(2,1)S(1)}, bf16[1,2048,256]{2,1,0:T(8,128)(2,1)}, u32[]{:S(2)}) copy-start(bf16[1,2048,256]{2,1,0:T(8,128)(2,1)} %get-tuple-element.39) | copy-start | bytes 3145732
  149.0 14.8 %collective-permute-start.15 = (bf16[4,16,24,256]{3,2,1,0:T(8,128)(2,1)S(1)}, bf16[4,16,24,256]{3,2,1,0:T(8,128)(2,1)}, u32[]{:S(2)}, u32[]{:S(2)}) collective-permute-start(bf16[4,16,24,256]{3,2,1,0:T(8,128)(2,1)S(1)} %constant_dynamic-slice_fusion), channel_id=1, source_target_pairs={{0,8},{8,0},{64,72},{72,64},{1,9},{9,1},{65,73},{73,65},{16,24},{2... | collective-permute-start | bytes 2359304 | tf_op jit(solution)/shard_map/ppermute | solution.py:500
  157.8 20.6 %all-to-all-start.2 = ((bf16[16,128,256]{2,1,0:T(8,128)(2,1)}), bf16[16,128,256]{2,1,0:T(8,128)(2,1)S(1)}, u32[]{:S(2)}, u32[]{:S(2)}) async-start(bf16[16,128,256]{2,1,0:T(8,128)(2,1)} %fusion.2), calls=%async_computation.2 | async-start | bytes 2097152 | tf_op jit(solution)/shard_map/all_to_all | solution.py:494

commit v3 on v2

--- a/solution.py
+++ b/solution.py
@@ -25,6 +25,8 @@
 SPILL = 64
 CHUNKS = 8
 UNROLL = 8
+PIECES = 96
+PIECE = (16, 384)
 SHARE = CODES // 128
 
 
@@ -134,8 +136,8 @@
 def quantizer_kernel(
     spilled, info, count,
     marked, plain, codebook, feats, above, below, weights, up,
-    grad, send, keep,
-    table, sums, lat, raw, near, taps, window, ids, sems,
+    grad, send, keep, weight_send, weight_keep,
+    table, sums, lat, raw, near, taps, window, weight_sum, weight_out, ids, sems,
 ):
     many = count[0, 0]
     windows = window_copies(above, feats, below, window, sems)
@@ -167,9 +169,11 @@
                 term = jnp.dot(part, taps[3 * a + b], preferred_element_type=F32)
                 cols[b] = term if a == 0 else cols[b] + term
         latent = shifted(cols[0], 1) + cols[1] + shifted(cols[2], -1)
-        at = pl.multiple_of(block * (2 * BLOCK), 8)
-        lat[pl.ds(at, BLOCK, stride=2), :] = latent[:, :128]
-        lat[pl.ds(at + 1, BLOCK, stride=2), :] = latent[:, 128:]
+        for r in range(4):
+            at = pl.multiple_of(block * (2 * BLOCK), 8) + 2 * r
+            own = latent[r * COLS : (r + 1) * COLS]
+            lat[pl.ds(at, COLS, stride=8), :] = own[:, :128]
+            lat[pl.ds(at + 1, COLS, stride=8), :] = own[:, 128:]
         return carry
 
     lax.fori_loop(0, BLOCKS, convolve, 0)
@@ -196,10 +200,11 @@
 
     lax.fori_loop(0, jnp.minimum(many, SPILL), lend, 0)
 
-    def resids(spot, code):
+    def resids(group, code):
         found = []
+        first = pl.multiple_of(group * 8, 8)
         for r in range(4):
-            here = pl.ds(2 * (spot + r * COLS), 2)
+            here = pl.ds(first + 2 * r, 2)
             resid, total = lat[here, :], None
             for d in range(DEPTHS):
                 k = code(r, d)
@@ -216,9 +221,7 @@
         def blocks(block, carry):
             def step(col, carry):
                 first = block * COLS + col
-                found = resids(
-                    block * BLOCK + col, lambda r, d: ids[first + (r * DEPTHS + d) * (GROUPS)]
-                )
+                found = resids(first, lambda r, d: ids[first + (r * DEPTHS + d) * GROUPS])
                 new = [sums[pl.ds(k, 2), :] + v for k, v in found]
                 for (k, _), v in zip(found, new):
                     sums[pl.ds(k, 2), :] = v
@@ -244,7 +247,7 @@
         def blocks(block, carry):
             def step(col, carry):
                 spot = block * BLOCK + col
-                for k, v in resids(spot, lambda r, d: 2 * ids[d * SPOTS + spot + r * COLS]):
+                for k, v in resids(block * COLS + col, lambda r, d: 2 * ids[d * SPOTS + spot + r * COLS]):
                     sums[pl.ds(k, 2), :] = sums[pl.ds(k, 2), :] + v
                 return carry
 
@@ -261,9 +264,11 @@
     def gradient(block, carry):
         rows = pl.ds(pl.multiple_of(block * BLOCK, 16), BLOCK)
         at = pl.multiple_of(block * (2 * BLOCK), 8)
-        total = jnp.concatenate(
-            [lat[pl.ds(at, BLOCK, stride=2), :], lat[pl.ds(at + 1, BLOCK, stride=2), :]], axis=1
-        )
+        halves = [
+            jnp.concatenate([lat[pl.ds(at + 2 * r + h, COLS, stride=8), :] for r in range(4)], axis=0)
+            for h in range(2)
+        ]
+        total = jnp.concatenate(halves, axis=1)
         near[rows, :] = (near[rows, :].astype(F32) + 2.0 * BETA * total).astype(BF16)
         put_grad(block).start()
         return carry
@@ -285,21 +290,59 @@
         for j in range(4):
             lax.fori_loop(0, 16, functools.partial(fill, first=first, core=core, j=j), 0, unroll=2)
             put_out(out, first, j).start()
+
+    weight_sum[...] = jnp.zeros_like(weight_sum)
+
+    def weigh(block, carry):
+        clip = block // (ROWS // 4)
+        row = (block % (ROWS // 4)) * 4
+        own = near[pl.ds(pl.multiple_of(block * BLOCK, 16), BLOCK), :]
+        mid = own.astype(F32)
+        wide = jnp.concatenate(
+            [shifted(mid, -1).astype(BF16), own, shifted(mid, 1).astype(BF16)], axis=1
+        )
+        for a in range(3):
+            part = window[clip, pl.ds(row + a, 4)].reshape(BLOCK, CHANS)
+            weight_sum[pl.ds(a * CHANS, CHANS), :] += lax.dot_general(
+                part, wide, (((0,), (0,)), ((), ())), preferred_element_type=F32
+            )
+        return carry
+
+    lax.fori_loop(0, BLOCKS, weigh, 0)
+
+    def cut(m, carry, side, core, j):
+        near_by = jnp.where(core == 0, info[0], info[1])
+        b = jnp.minimum(core * 64 + (near_by + j) % 4 * 16 + m, PIECES - 1)
+        rows = weight_sum[pl.ds(pl.multiple_of(b * 8, 8), 8), :]
+        both = jnp.concatenate([rows[:, :384], rows[:, 384:]], axis=0)
+        weight_out[side, j, m] = both.astype(BF16)
+        return carry
+
+    def put_weights(out, side):
+        return pltpu.make_async_copy(weight_out.at[side], out, sems.at[24 + side])
+
+    for side, core, out in ((0, 1 - info[3], weight_send), (1, info[3], weight_keep)):
+        for j in range(4):
+            lax.fori_loop(0, 16, functools.partial(cut, side=side, core=core, j=j), 0, unroll=4)
+        put_weights(out, side).start()
     for block in range(BLOCKS):
         put_grad(block).wait()
     for first, out in ((0, send), (4, keep)):
         for j in range(4):
             put_out(out, first, j).wait()
+    put_weights(weight_send, 0).wait()
+    put_weights(weight_keep, 1).wait()
 
 
 def quantizer(marked, plain, spilled, info, count, codebook, feats, above, below, weights, up):
     hbm = pl.BlockSpec(memory_space=pl.ANY)
     smem = pl.BlockSpec(memory_space=pltpu.SMEM)
     out_shape = (4, 16 * SHARE, CHANS)
+    weight_shape = (4, 16) + PIECE
     return pl.pallas_call(
         quantizer_kernel,
         in_specs=[smem] * 3 + [hbm] * 8,
-        out_specs=[hbm] * 3,
+        out_specs=[hbm] * 5,
         scratch_shapes=[
             pltpu.VMEM((2 * (CODES + SPILL), 128), F32),
             pltpu.VMEM((2 * (CODES + SPILL), 128), F32),
@@ -308,94 +351,23 @@
             pltpu.VMEM((SPOTS, CHANS), BF16),
             pltpu.VMEM((9, CHANS, CHANS), BF16),
             pltpu.VMEM((HERE, ROWS + 2, COLS, CHANS), BF16),
+            pltpu.VMEM((3 * CHANS, 3 * CHANS), F32),
+            pltpu.VMEM((2,) + weight_shape, BF16),
             pltpu.SMEM((DEPTHS * SPOTS,), jnp.int32),
-            pltpu.SemaphoreType.DMA((24,)),
+            pltpu.SemaphoreType.DMA((26,)),
         ],
         out_shape=[
             jax.ShapeDtypeStruct((SPOTS, CHANS), BF16),
             jax.ShapeDtypeStruct(out_shape, BF16),
             jax.ShapeDtypeStruct(out_shape, BF16),
+            jax.ShapeDtypeStruct(weight_shape, BF16),
+            jax.ShapeDtypeStruct(weight_shape, BF16),
         ],
         compiler_params=pltpu.CompilerParams(vmem_limit_bytes=58 << 20),
         cost_estimate=pl.CostEstimate(
-            flops=2 * 9 * SPOTS * CHANS * CHANS, bytes_accessed=32 << 20, transcendentals=0
+            flops=4 * 9 * SPOTS * CHANS * CHANS, bytes_accessed=64 << 20, transcendentals=0
         ),
     )(spilled, info, count, marked, plain, codebook, feats, above, below, weights, up)
-
-
-def weight_kernel(info, feats, above, below, grad, send, keep, window, total, sems):
-    i = pl.program_id(0)
-
-    copies = window_copies(above, feats, below, window, sems)
-
-    @pl.when(i == 0)
-    def _():
-        for copy in copies:
-            copy.start()
-        for copy in copies:
-            copy.wait()
-
-    clip = i // (ROWS // 4)
-    row = (i % (ROWS // 4)) * 4
-    mid = grad[...].astype(F32)
-    wide = jnp.concatenate(
-        [shifted(mid, -1).astype(BF16), grad[...], shifted(mid, 1).astype(BF16)], axis=1
-    )
-    for a in range(3):
-        part = window[clip, pl.ds(row + a, 4)].reshape(BLOCK, CHANS)
-        term = lax.dot_general(part, wide, (((0,), (0,)), ((), ())), preferred_element_type=F32)
-
-        @pl.when(i == 0)
-        def _():
-            total[pl.ds(a * CHANS, CHANS), :] = term
-
-        @pl.when(i > 0)
-        def _():
-            total[pl.ds(a * CHANS, CHANS), :] += term
-
-    @pl.when(i == BLOCKS - 1)
-    def _():
-        for out, core in ((send, 1 - info[3]), (keep, info[3])):
-            for j in range(4):
-                for m in range(16):
-                    near = jnp.where(core == 0, info[0], info[1])
-                    b = jnp.minimum(core * 64 + (near + j) % 4 * 16 + m, 95)
-                    rows = total[pl.ds(pl.multiple_of(b * 8, 8), 8), :]
-                    for q in range(3):
-                        out[j, m, pl.ds(8 * q, 8), :] = rows[:, q * CHANS : (q + 1) * CHANS]
-
-
-def weight_sums(info, feats, above, below, grad):
-    shape = (4, 16, 24, CHANS)
-    return pl.pallas_call(
-        weight_kernel,
-        grid_spec=pltpu.PrefetchScalarGridSpec(
-            num_scalar_prefetch=1,
-            grid=(BLOCKS,),
-            in_specs=[
-                pl.BlockSpec(memory_space=pl.ANY),
-                pl.BlockSpec(memory_space=pl.ANY),
-                pl.BlockSpec(memory_space=pl.ANY),
-                pl.BlockSpec((BLOCK, CHANS), lambda i, *_: (i, 0)),
-            ],
-            out_specs=[
-                pl.BlockSpec(shape, lambda i, *_: (0, 0, 0, 0)),
-                pl.BlockSpec(shape, lambda i, *_: (0, 0, 0, 0)),
-            ],
-            scratch_shapes=[
-                pltpu.VMEM((HERE, ROWS + 2, COLS, CHANS), BF16),
-                pltpu.VMEM((3 * CHANS, 3 * CHANS), F32),
-                pltpu.SemaphoreType.DMA((3 * HERE,)),
-            ],
-        ),
-        out_shape=[jax.ShapeDtypeStruct(shape, F32)] * 2,
-        compiler_params=pltpu.CompilerParams(
-            vmem_limit_bytes=32 << 20, dimension_semantics=("arbitrary",)
-        ),
-        cost_estimate=pl.CostEstimate(
-            flops=2 * 9 * SPOTS * CHANS * CHANS, bytes_accessed=8 << 20, transcendentals=0
-        ),
-    )(info, feats, above, below, grad)
 
 
 def back_kernel(grad, above, below, weights, out, window, sems):
@@ -449,6 +421,56 @@
     )(grad, above, below, weights)
 
 
+def turn_kernel(info, *refs):
+    at = jnp.where(info[3] == 0, info[0], info[1])
+    for d in range(4):
+        refs[4][(at + 4 - d) % 4] = refs[d][...]
+
+
+def turned(info, pieces, around):
+    return pl.pallas_call(
+        turn_kernel,
+        in_specs=[pl.BlockSpec(memory_space=pltpu.SMEM)] + [pl.BlockSpec()] * 4,
+        out_shape=jax.ShapeDtypeStruct((4,) + pieces.shape, BF16),
+    )(info, pieces, *around)
+
+
+def join_kernel(info, mine, theirs, out):
+    def join(low, high):
+        for a in range(3):
+            for r in range(2):
+
+                def place(m, carry):
+                    ref, ring = (low, 2 * a + r) if a < 2 else (high, r)
+                    both = ref[ring, m].astype(F32)
+                    top, bottom = both[:8], both[8:]
+                    rows = pl.ds(pl.multiple_of((r * 16 + m) * 8, 8), 8)
+                    out[3 * a, rows, :] = top[:, :256]
+                    out[3 * a + 1, rows, :128] = top[:, 256:]
+                    out[3 * a + 1, rows, 128:] = bottom[:, :128]
+                    out[3 * a + 2, rows, :] = bottom[:, 128:]
+                    return carry
+
+                lax.fori_loop(0, 16, place, 0, unroll=4)
+
+    @pl.when(info[3] == 0)
+    def _():
+        join(mine, theirs)
+
+    @pl.when(info[3] != 0)
+    def _():
+        join(theirs, mine)
+
+
+def joined(info, mine, theirs):
+    return pl.pallas_call(
+        join_kernel,
+        in_specs=[pl.BlockSpec(memory_space=pltpu.SMEM)] + [pl.BlockSpec()] * 2,
+        out_shape=jax.ShapeDtypeStruct((9, CHANS, CHANS), F32),
+        compiler_params=pltpu.CompilerParams(vmem_limit_bytes=32 << 20),
+    )(info, mine, theirs)
+
+
 def edges(array):
     n = lax.axis_size("tile")
     up = [(i, i + 1) for i in range(n - 1)]
@@ -462,18 +484,17 @@
     info = place()
     above, below = edges(features)
     marked, spilled, count = entry_lists(codes)
-    grad, send, keep = quantizer(
+    grad, send, keep, weight_send, weight_keep = quantizer(
         marked.reshape(-1), codes.reshape(-1), spilled, info, count, codebook, features, above,
         below, conv_weight, upstream.reshape(SPOTS, CHANS),
     )
     got = lax.ppermute(send, BOTH, SWAP)
     grad4 = grad.reshape(features.shape)
     grad_above, grad_below = edges(grad4)
-    weight_send, weight_keep = weight_sums(info, features, above, below, grad)
-    weight_got = lax.ppermute(weight_send.astype(BF16), BOTH, SWAP)
-    weight_chip = (weight_keep + weight_got.astype(F32)).astype(BF16)
-    keep, got, grad_above, grad_below, weight_chip = lax.optimization_barrier(
-        (keep, got, grad_above, grad_below, weight_chip)
+    weight_got = lax.ppermute(weight_send, BOTH, SWAP)
+    weight_chip = (weight_keep.astype(F32) + weight_got.astype(F32)).astype(BF16)
+    keep, got, grad_above, grad_below = lax.optimization_barrier(
+        (keep, got, grad_above, grad_below)
     )
     weight_ring = weight_chip[0].astype(F32)
     for d in (1, 2, 3):
@@ -482,27 +503,21 @@
     others = [lax.ppermute(chip[d], BOTH, first_ring(d)) for d in (1, 2, 3)]
     plane = lax.all_to_all(weight_ring.astype(BF16), BOTH, 0, 0, axis_index_groups=PLANES)
     piece = plane.astype(F32).sum(0).astype(BF16)
+    piece, grad_above = lax.optimization_barrier((piece, grad_above))
     pieces = lax.all_to_all(
-        jnp.broadcast_to(piece[None], (16, 24, CHANS)), BOTH, 0, 0, axis_index_groups=PLANES
+        jnp.broadcast_to(piece[None], (16,) + PIECE), BOTH, 0, 0, axis_index_groups=PLANES
     )
     back = feature_grads(grad4, grad_above, grad_below, conv_weight)
-    others, pieces, back = lax.optimization_barrier((others, pieces, back))
-    around = [lax.ppermute(pieces, BOTH, first_ring(d)) for d in (1, 2, 3)]
     ring = chip[0].astype(F32)
     for other in others:
         ring = ring + other.astype(F32)
-    plane = lax.all_to_all(ring.astype(BF16), BOTH, 0, 0, axis_index_groups=PLANES)
+    ring, pieces, back = lax.optimization_barrier((ring.astype(BF16), pieces, back))
+    plane = lax.all_to_all(ring, BOTH, 0, 0, axis_index_groups=PLANES)
+    around = [lax.ppermute(pieces, BOTH, first_ring(d)) for d in (1, 2, 3)]
+    mine = turned(info, pieces, around)
+    theirs = lax.ppermute(mine, BOTH, SWAP)
     code_part = plane.astype(F32).sum(0)
-    core = info[3]
-    at = jnp.where(core == 0, info[0], info[1])
-    turned = jnp.concatenate([jnp.stack(around[::-1] + [pieces])] * 2)
-    mine = lax.dynamic_slice_in_dim(turned, 3 - at, 4, axis=0)
-    theirs = lax.ppermute(mine, BOTH, SWAP)
-    weight_grad = jnp.where(core == 0, jnp.stack([mine, theirs]), jnp.stack([theirs, mine]))
-    weight_grad = weight_grad.reshape(128, 24, CHANS)[:96].reshape(96, 3, 8, CHANS)
-    weight_grad = weight_grad.transpose(0, 2, 1, 3).reshape(3, CHANS, 3, CHANS)
-    weight_grad = weight_grad.transpose(0, 2, 1, 3).reshape(9, CHANS, CHANS).astype(F32)
-    return back.reshape(features.shape), weight_grad, code_part
+    return back.reshape(features.shape), joined(info, mine, theirs), code_part
 
 
 def solution(mesh):

time: 180 us -> 161 us (0.89); the launches traced: 179 us -> 158 us
  waiting for transfers between devices: 27.5 us -> 7.63 us
  local copies, waits for them, and re-layouts: 11.8 us -> 7.98 us
  starting transfers between devices: 45.3 us -> 48.9 us
    all_to_all x2, waiting for transfers between devices: 10.9 us -> 0.01 us  [the longest x1 0.01 us: on_device(): plane = lax.all_to_all(ring, BOTH, 0, 0, axis_index_groups=PLANES)]
    pallas_call x1 -> x2, Pallas kernels: 13.8 us -> 4.42 us  [the longest x1 2.24 us: joined(): pl.pallas_call(join_kernel, in_specs=[pl.BlockSpec(memory_space=pltpu.SME...]
    pallas_call x1, Pallas kernels: 43.4 us -> 51.1 us  [quantizer(): pl.pallas_call(quantizer_kernel, in_specs=[smem] * 3 + [hbm] * 8, out_spe...]
    ppermute x3, waiting for transfers between devices: 7.61 us -> 0.01 us  [on_device(): around = [lax.ppermute(pieces, BOTH, first_ring(d)) for d in (1, 2, 3)]]
    ppermute x2, waiting for transfers between devices: 8.08 us -> 2.78 us  [edges(): below = lax.ppermute(array[:, :1], 'tile', down)]
    ppermute x1, starting transfers between devices: 5.27 us -> 8.56 us  [on_device(): theirs = lax.ppermute(mine, BOTH, SWAP)]
    ppermute x1, waiting for transfers between devices: 0.01 us -> 2.7 us  [on_device(): weight_got = lax.ppermute(weight_send, BOTH, SWAP)]
    convert_element_type x1, other arithmetic: 1.13 us -> 3.35 us  [on_device(): (keep.astype(F32) + got.astype(F32)).astype(BF16)]
  transfers between devices with their start and end apart: 18 -> 18, of which waited for: 7 -> 3; matrix products, arithmetic and copies ran while one was open for 7% -> 9% of each run, Pallas kernels for 13% -> 9%
where the time goes in v3:
time: 161 us; the launch traced here: 158 us
  Pallas kernels  65.8 us (41%)
  starting transfers between devices  48.9 us (30%)
  blocking collectives  16.3 us (10%)
  other arithmetic  10.7 us (7%)
  local copies, waits for them, and re-layouts  7.98 us (5%)
  waiting for transfers between devices  7.63 us (5%)
    pallas_call x1, Pallas kernels, quantizer(): pl.pallas_call(quantizer_kernel, in_specs=[smem] * 3 + [hbm] * 8, out_spe...  51.1 us
    all_to_all x1, blocking collectives, on_device(): lax.all_to_all(weight_ring.astype(BF16), BOTH, 0, 0, axis_index_groups=PL...  16.3 us
    ppermute x2, starting transfers between devices, edges(): above = lax.ppermute(array[:, -1:], 'tile', up)  9.37 us
    ppermute x1, starting transfers between devices, on_device(): theirs = lax.ppermute(mine, BOTH, SWAP)  8.56 us
    pallas_call x1, Pallas kernels, feature_grads(): pl.pallas_call(back_kernel, grid=(BLOCKS,), in_specs=[pl.BlockSpec(memory...  7.89 us
    all_to_all x1, starting transfers between devices, on_device(): lax.all_to_all(jnp.broadcast_to(piece[None], (16,) + PIECE), BOTH, 0, 0,...  6.9 us
    all_to_all x1, starting transfers between devices, on_device(): plane = lax.all_to_all(ring, BOTH, 0, 0, axis_index_groups=PLANES)  6.61 us
    ppermute x3, starting transfers between devices, on_device(): around = [lax.ppermute(pieces, BOTH, first_ring(d)) for d in (1, 2, 3)]  4.95 us
  transfers between devices with their start and end apart: 18, of which 3 were waited for; matrix products, arithmetic and copies ran while one was open for 9% of the time, Pallas kernels for 9%

profile of v3, /device:TPU:1, one launch (start us, length us, event | category | flops | bytes accessed | tf_op | source)
XLA Modules:
  0.0 158.3 jit_solution(10428567684913418616)
XLA Ops:
  0.6 1.0 fusion.8
  1.6 6.3 %collective-permute-start = (bf16[2,1,128,256]{3,2,1,0:T(8,128)(2,1)S(1)}, bf16[2,1,128,256]{3,2,1,0:T(8,128)(2,1)S(1)}, u32[]{:S(2)}, u32[]{:S(2)}) collective-permute-start(bf16[2,1,128,256]{3,2,1,0:T(8,128)(2,1)S(1)} %get-tuple-element.44), channel_id=1, source_target_pairs={{0,1},{1,2},{2,3},{3,4},{4,5},{5,6},{6,7},{8,9},{9,10},{10,11},{11... | collective-permute-start | bytes 393224 | tf_op jit(solution)/shard_map/ppermute | solution.py:478
  8.0 1.3 collective-permute-start.1
  9.3 2.4 %shard_map.76 = (s32[128,128]{1,0:T(8,128)}, s32[64,128]{1,0:T(8,128)}, s32[8,128]{1,0:T(8,128)}) custom-call(s32[128,128]{1,0:T(8,128)} %bitcast.29), custom_call_target="tpu_custom_call" | custom-call | tf_op jit(solution)/shard_map/pallas_call | solution.py:126
  12.4 2.8 %collective-permute-done.1.below = bf16[2,1,128,256]{3,2,1,0:T(8,128)(2,1)S(1)} collective-permute-done((bf16[2,1,128,256]{3,2,1,0:T(8,128)(2,1)S(1)}, bf16[2,1,128,256]{3,2,1,0:T(8,128)(2,1)S(1)}, u32[]{:S(2)}, u32[]{:S(2)}) %collective-permute-start.1) | collective-permute-done | bytes 131104 | tf_op jit(solution)/shard_map/ppermute | solution.py:479
  15.8 51.1 %shard_map.77 = (bf16[4096,256]{1,0:T(8,128)(2,1)}, bf16[4,2048,256]{2,1,0:T(8,128)(2,1)}, bf16[4,2048,256]{2,1,0:T(8,128)(2,1)}, bf16[4,16,16,384]{3,2,1,0:T(8,128)(2,1)}, bf16[4,16,16,384]{3,2,1,0:T(8,128)(2,1)}) custom-call(s32[64,128]{1,0:T(8,128)} %get-tuple-element.20.spilled, s32[4]{0:T(128)} %pad_add_fusion.info, s32[8,128]{1,0:T(8,128)} %get-tuple-element.21.count, ...), custom_call_target="tpu_custom_call" | custom-call | flops 9663676416 | bytes 67108864 | tf_op jit(solution)/shard_map/pallas_call | solution.py:342
  66.9 2.3 %collective-permute-start.2 = (bf16[4,2048,256]{2,1,0:T(8,128)(2,1)}, bf16[4,2048,256]{2,1,0:T(8,128)(2,1)S(1)}, u32[]{:S(2)}, u32[]{:S(2)}) collective-permute-start(bf16[4,2048,256]{2,1,0:T(8,128)(2,1)} %get-tuple-element.24), channel_id=1, source_target_pairs={{0,8},{8,0},{64,72},{72,64},{1,9},{9,1},{65,73},{73,65},{16,24},{2... | collective-permute-start | bytes 12582920 | tf_op jit(solution)/shard_map/ppermute | solution.py:491
  69.3 1.0 fusion.7
  70.3 3.0 %collective-permute-start.3 = (bf16[2,1,128,256]{3,2,1,0:T(8,128)(2,1)S(1)}, bf16[2,1,128,256]{3,2,1,0:T(8,128)(2,1)S(1)}, u32[]{:S(2)}, u32[]{:S(2)}) collective-permute-start(bf16[2,1,128,256]{3,2,1,0:T(8,128)(2,1)S(1)} %get-tuple-element.42), channel_id=1, source_target_pairs={{0,1},{1,2},{2,3},{3,4},{4,5},{5,6},{6,7},{8,9},{9,10},{10,11},{11... | collective-permute-start | bytes 393224 | tf_op jit(solution)/shard_map/ppermute | solution.py:478
  73.4 1.3 collective-permute-start.4
  74.7 2.7 %collective-permute-done.8 = bf16[4,16,16,384]{3,2,1,0:T(8,128)(2,1)S(1)} collective-permute-done((bf16[4,16,16,384]{3,2,1,0:T(8,128)(2,1)}, bf16[4,16,16,384]{3,2,1,0:T(8,128)(2,1)S(1)}, u32[]{:S(2)}, u32[]{:S(2)}) %collective-permute-start.8) | collective-permute-done | bytes 786464 | tf_op jit(solution)/shard_map/ppermute | solution.py:494
  77.4 1.3 add_convert_fusion.1
  78.8 3.0 %collective-permute-start.10 = (bf16[16,16,384]{2,1,0:T(8,128)(2,1)S(1)}, bf16[16,16,384]{2,1,0:T(8,128)(2,1)S(1)}, u32[]{:S(2)}, u32[]{:S(2)}) collective-permute-start(bf16[16,16,384]{2,1,0:T(8,128)(2,1)S(1)} %get-tuple-element.47), channel_id=1, source_target_pairs={{0,4},{8,40},{64,68},{72,104},{1,5},{9,41},{65,69},{73,105},{16,20... | collective-permute-start | bytes 589832 | tf_op jit(solution)/shard_map/ppermute | solution.py:501
  82.5 0.8 collective-permute-start.9
  83.2 3.3 %add_convert_fusion = bf16[4,2048,256]{2,1,0:T(8,128)(2,1)S(1)} fusion(bf16[4,2048,256]{2,1,0:T(8,128)(2,1)S(1)} %collective-permute-done.2, bf16[4,2048,256]{2,1,0:T(8,128)(2,1)} %get-tuple-element.26), kind=kLoop, calls=%fused_computation | loop fusion | flops 8388608 | bytes 12582912 | tf_op jit(solution)/shard_map/convert_element_type | solution.py:502
  86.6 2.1 %fusion.6 = (bf16[1,2048,256]{2,1,0:T(8,128)(2,1)}, bf16[1,2048,256]{2,1,0:T(8,128)(2,1)}, bf16[1,2048,256]{2,1,0:T(8,128)(2,1)}, bf16[1,2048,256]{2,1,0:T(8,128)(2,1)}) fusion(bf16[4,2048,256]{2,1,0:T(8,128)(2,1)S(1)} %add_convert_fusion), kind=kLoop, calls=%fused_computation.16 | loop fusion | bytes 8388608 | tf_op jit(solution)/shard_map/slice | solution.py:503
  89.1 2.7 %collective-permute-start.6 = (bf16[16,128,256]{2,1,0:T(8,128)(2,1)}, bf16[16,128,256]{2,1,0:T(8,128)(2,1)}, u32[]{:S(2)}, u32[]{:S(2)}) collective-permute-start(bf16[16,128,256]{2,1,0:T(8,128)(2,1)} %bitcast.11), channel_id=1, source_target_pairs={{0,4},{8,40},{64,68},{72,104},{1,5},{9,41},{65,69},{73,105},{16,20... | collective-permute-start | bytes 3145736 | tf_op jit(solution)/shard_map/ppermute | solution.py:503
  91.9 16.3 %all_to_all.15 = bf16[16,16,384]{2,1,0:T(8,128)(2,1)} all-to-all(bf16[16,16,384]{2,1,0:T(8,128)(2,1)S(1)} %fusion.5), channel_id=1, replica_groups={{0,64,1,65,16,80,17,81,32,96,33,97,48,112,49,113},{2,66,3,67,18,82,19,8..., dimensions={0} | all-to-all | bytes 393216 | tf_op jit(solution)/shard_map/all_to_all | solution.py:504
  108.2 1.0 reduce_sum.21
  109.8 6.9 %all-to-all-start.1 = ((bf16[16,16,384]{2,1,0:T(8,128)(2,1)}), bf16[16,16,384]{2,1,0:T(8,128)(2,1)}, u32[]{:S(2)}, u32[]{:S(2)}) async-start(bf16[16,16,384]{2,1,0:T(8,128)(2,1)} %broadcast_in_dim.2), calls=%async_computation.1 | async-start | bytes 393216 | tf_op jit(solution)/shard_map/all_to_all | solution.py:507
  116.8 7.9 %shard_map.78 = bf16[4096,256]{1,0:T(8,128)(2,1)} custom-call(bf16[2,16,128,256]{3,2,1,0:T(8,128)(2,1)S(1)} %bitcast.27, bf16[2,1,128,256]{3,2,1,0:T(8,128)(2,1)S(1)} %collective-permute-done.3.above, bf16[2,1,128,256]{3,2,1,0:T(8,128)(2,1)S(1)} %collective-permute-done.4.below, bf16[9,256,256]{2,1,0:T(8,128)(2,1)S(1)} %copy-done.3), custom_call_target="tpu_custom_call" | custom-call | flops 4831838208 | bytes 8388608 | tf_op jit(solution)/shard_map/pallas_call | solution.py:400
  124.7 3.5 %fusion.2 = bf16[16,128,256]{2,1,0:T(8,128)(2,1)} fusion(bf16[16,128,256]{2,1,0:T(8,128)(2,1)S(1)} %bitcast.28, bf16[16,128,256]{2,1,0:T(8,128)(2,1)} %collective-permute-done.7, bf16[16,128,256]{2,1,0:T(8,128)(2,1)} %collective-permute-done.6, bf16[16,128,256]{2,1,0:T(8,128)(2,1)} %collective-permute-done.5), kind=kLoop, calls=%fused_computation.4 | loop fusion | flops 4194304 | bytes 5242880 | tf_op jit(solution)/shard_map/convert_element_type | solution.py:514
  128.2 1.3 collective-permute-start.12
  129.5 2.6 %collective-permute-start.13 = (bf16[16,16,384]{2,1,0:T(8,128)(2,1)}, bf16[16,16,384]{2,1,0:T(8,128)(2,1)S(1)}, u32[]{:S(2)}, u32[]{:S(2)}) collective-permute-start(bf16[16,16,384]{2,1,0:T(8,128)(2,1)} %all-to-all-done.1.refs_0_), channel_id=1, source_target_pairs={{0,4},{8,40},{64,68},{72,104},{1,5},{9,41},{65,69},{73,105},{16,20... | collective-permute-start | bytes 589832 | tf_op jit(solution)/shard_map/ppermute | solution.py:516
  132.1 1.1 collective-permute-start.14
  133.2 6.6 %all-to-all-start.2 = ((bf16[16,128,256]{2,1,0:T(8,128)(2,1)}), bf16[16,128,256]{2,1,0:T(8,128)(2,1)S(1)}, u32[]{:S(2)}, u32[]{:S(2)}) async-start(bf16[16,128,256]{2,1,0:T(8,128)(2,1)} %fusion.2), calls=%async_computation.2 | async-start | bytes 2097152 | tf_op jit(solution)/shard_map/all_to_all | solution.py:515
  141.2 2.2 %shard_map.79.mine = bf16[4,16,16,384]{3,2,1,0:T(8,128)(2,1)} custom-call(s32[4]{0:T(128)} %pad_add_fusion.info, bf16[16,16,384]{2,1,0:T(8,128)(2,1)} %all-to-all-done.1.refs_0_, bf16[16,16,384]{2,1,0:T(8,128)(2,1)} %copy-done.5, bf16[16,16,384]{2,1,0:T(8,128)(2,1)} %copy-done.6, bf16[16,16,384]{2,1,0:T(8,128)(2,1)} %copy-done.7), custom_call_target="tpu_custom_call" | custom-call | tf_op jit(solution)/shard_map/pallas_call | solution.py:431
  143.4 8.6 %collective-permute-start.15 = (bf16[4,16,16,384]{3,2,1,0:T(8,128)(2,1)}, bf16[4,16,16,384]{3,2,1,0:T(8,128)(2,1)S(1)}, u32[]{:S(2)}, u32[]{:S(2)}) collective-permute-start(bf16[4,16,16,384]{3,2,1,0:T(8,128)(2,1)} %shard_map.79.mine), channel_id=1, source_target_pairs={{0,8},{8,0},{64,72},{72,64},{1,9},{9,1},{65,73},{73,65},{16,24},{2... | collective-permute-start | bytes 2359304 | tf_op jit(solution)/shard_map/ppermute | solution.py:518
  152.0 2.1 %collective-permute-done.15.theirs = bf16[4,16,16,384]{3,2,1,0:T(8,128)(2,1)S(1)} collective-permute-done((bf16[4,16,16,384]{3,2,1,0:T(8,128)(2,1)}, bf16[4,16,16,384]{3,2,1,0:T(8,128)(2,1)S(1)}, u32[]{:S(2)}, u32[]{:S(2)}) %collective-permute-start.15) | collective-permute-done | bytes 786464 | tf_op jit(solution)/shard_map/ppermute | solution.py:518
  154.1 1.1 copy-done
  155.2 2.2 %shard_map.80 = f32[9,256,256]{2,1,0:T(8,128)} custom-call(s32[4]{0:T(128)S(1)} %copy-done.2, bf16[4,16,16,384]{3,2,1,0:T(8,128)(2,1)S(1)} %copy-done, bf16[4,16,16,384]{3,2,1,0:T(8,128)(2,1)S(1)} %collective-permute-done.15.theirs), custom_call_target="tpu_custom_call" | custom-call | tf_op jit(solution)/shard_map/pallas_call | solution.py:466
  157.5 0.8 convert_reduce_fusion
  (42 shorter events, 4.8 us)
Async XLA Ops:
  1.6 10.8 %collective-permute-start = (bf16[2,1,128,256]{3,2,1,0:T(8,128)(2,1)S(1)}, bf16[2,1,128,256]{3,2,1,0:T(8,128)(2,1)S(1)}, u32[]{:S(2)}, u32[]{:S(2)}) collective-permute-start(bf16[2,1,128,256]{3,2,1,0:T(8,128)(2,1)S(1)} %get-tuple-element.44), channel_id=1, source_target_pairs={{0,1},{1,2},{2,3},{3,4},{4,5},{5,6},{6,7},{8,9},{9,10},{10,11},{11... | collective-permute-start | bytes 393224 | tf_op jit(solution)/shard_map/ppermute | solution.py:478
  8.0 7.2 %collective-permute-start.1 = (bf16[2,1,128,256]{3,2,1,0:T(8,128)(2,1)S(1)}, bf16[2,1,128,256]{3,2,1,0:T(8,128)(2,1)S(1)}, u32[]{:S(2)}, u32[]{:S(2)}) collective-permute-start(bf16[2,1,128,256]{3,2,1,0:T(8,128)(2,1)S(1)} %get-tuple-element.43), channel_id=1, source_target_pairs={{1,0},{2,1},{3,2},{4,3},{5,4},{6,5},{7,6},{9,8},{10,9},{11,10},{12... | collective-permute-start | bytes 393224 | tf_op jit(solution)/shard_map/ppermute | solution.py:479
  12.4 2.8 %copy-start.8 = (bf16[2,1,128,256]{3,2,1,0:T(8,128)(2,1)}, bf16[2,1,128,256]{3,2,1,0:T(8,128)(2,1)S(1)}, u32[]{:S(2)}) copy-start(bf16[2,1,128,256]{3,2,1,0:T(8,128)(2,1)S(1)} %collective-permute-done.above) | copy-start | bytes 393220
  15.2 0.6 copy-start.9
  66.9 16.3 %collective-permute-start.2 = (bf16[4,2048,256]{2,1,0:T(8,128)(2,1)}, bf16[4,2048,256]{2,1,0:T(8,128)(2,1)S(1)}, u32[]{:S(2)}, u32[]{:S(2)}) collective-permute-start(bf16[4,2048,256]{2,1,0:T(8,128)(2,1)} %get-tuple-element.24), channel_id=1, source_target_pairs={{0,8},{8,0},{64,72},{72,64},{1,9},{9,1},{65,73},{73,65},{16,24},{2... | collective-permute-start | bytes 12582920 | tf_op jit(solution)/shard_map/ppermute | solution.py:491
  69.2 8.1 %collective-permute-start.8 = (bf16[4,16,16,384]{3,2,1,0:T(8,128)(2,1)}, bf16[4,16,16,384]{3,2,1,0:T(8,128)(2,1)S(1)}, u32[]{:S(2)}, u32[]{:S(2)}) collective-permute-start(bf16[4,16,16,384]{3,2,1,0:T(8,128)(2,1)} %get-tuple-element.29), channel_id=1, source_target_pairs={{0,8},{8,0},{64,72},{72,64},{1,9},{9,1},{65,73},{73,65},{16,24},{2... | collective-permute-start | bytes 2359304 | tf_op jit(solution)/shard_map/ppermute | solution.py:494
  70.3 12.1 %collective-permute-start.3 = (bf16[2,1,128,256]{3,2,1,0:T(8,128)(2,1)S(1)}, bf16[2,1,128,256]{3,2,1,0:T(8,128)(2,1)S(1)}, u32[]{:S(2)}, u32[]{:S(2)}) collective-permute-start(bf16[2,1,128,256]{3,2,1,0:T(8,128)(2,1)S(1)} %get-tuple-element.42), channel_id=1, source_target_pairs={{0,1},{1,2},{2,3},{3,4},{4,5},{5,6},{6,7},{8,9},{9,10},{10,11},{11... | collective-permute-start | bytes 393224 | tf_op jit(solution)/shard_map/ppermute | solution.py:478
  73.4 9.9 %collective-permute-start.4 = (bf16[2,1,128,256]{3,2,1,0:T(8,128)(2,1)S(1)}, bf16[2,1,128,256]{3,2,1,0:T(8,128)(2,1)S(1)}, u32[]{:S(2)}, u32[]{:S(2)}) collective-permute-start(bf16[2,1,128,256]{3,2,1,0:T(8,128)(2,1)S(1)} %get-tuple-element.41), channel_id=1, source_target_pairs={{1,0},{2,1},{3,2},{4,3},{5,4},{6,5},{7,6},{9,8},{10,9},{11,10},{12... | collective-permute-start | bytes 393224 | tf_op jit(solution)/shard_map/ppermute | solution.py:479
  78.8 13.0 %collective-permute-start.10 = (bf16[16,16,384]{2,1,0:T(8,128)(2,1)S(1)}, bf16[16,16,384]{2,1,0:T(8,128)(2,1)S(1)}, u32[]{:S(2)}, u32[]{:S(2)}) collective-permute-start(bf16[16,16,384]{2,1,0:T(8,128)(2,1)S(1)} %get-tuple-element.47), channel_id=1, source_target_pairs={{0,4},{8,40},{64,68},{72,104},{1,5},{9,41},{65,69},{73,105},{16,20... | collective-permute-start | bytes 589832 | tf_op jit(solution)/shard_map/ppermute | solution.py:501
  81.7 10.0 %collective-permute-start.11 = (bf16[16,16,384]{2,1,0:T(8,128)(2,1)S(1)}, bf16[16,16,384]{2,1,0:T(8,128)(2,1)S(1)}, u32[]{:S(2)}, u32[]{:S(2)}) collective-permute-start(bf16[16,16,384]{2,1,0:T(8,128)(2,1)S(1)} %get-tuple-element.46), channel_id=1, source_target_pairs={{0,6},{8,56},{64,70},{72,120},{1,7},{9,57},{65,71},{73,121},{16,22... | collective-permute-start | bytes 589832 | tf_op jit(solution)/shard_map/ppermute | solution.py:501
  82.5 9.3 %collective-permute-start.9 = (bf16[16,16,384]{2,1,0:T(8,128)(2,1)S(1)}, bf16[16,16,384]{2,1,0:T(8,128)(2,1)S(1)}, u32[]{:S(2)}, u32[]{:S(2)}) collective-permute-start(bf16[16,16,384]{2,1,0:T(8,128)(2,1)S(1)} %get-tuple-element.45), channel_id=1, source_target_pairs={{0,2},{8,24},{64,66},{72,88},{1,3},{9,25},{65,67},{73,89},{16,18},... | collective-permute-start | bytes 589832 | tf_op jit(solution)/shard_map/ppermute | solution.py:501
  86.6 30.2 %copy-start.3 = (bf16[9,256,256]{2,1,0:T(8,128)(2,1)S(1)}, bf16[9,256,256]{2,1,0:T(8,128)(2,1)}, u32[]{:S(2)}) copy-start(bf16[9,256,256]{2,1,0:T(8,128)(2,1)} %weights.3) | copy-start | bytes 3538948
  88.7 28.1 %copy-start.1 = (bf16[4096,256]{1,0:T(8,128)(2,1)S(1)}, bf16[4096,256]{1,0:T(8,128)(2,1)}, u32[]{:S(2)}) copy-start(bf16[4096,256]{1,0:T(8,128)(2,1)} %get-tuple-element.25) | copy-start | bytes 6291460
  88.7 36.0 %collective-permute-start.5 = (bf16[16,128,256]{2,1,0:T(8,128)(2,1)}, bf16[16,128,256]{2,1,0:T(8,128)(2,1)}, u32[]{:S(2)}, u32[]{:S(2)}) collective-permute-start(bf16[16,128,256]{2,1,0:T(8,128)(2,1)} %bitcast.10), channel_id=1, source_target_pairs={{0,2},{8,24},{64,66},{72,88},{1,3},{9,25},{65,67},{73,89},{16,18},... | collective-permute-start | bytes 3145736 | tf_op jit(solution)/shard_map/ppermute | solution.py:503
  89.1 35.6 %collective-permute-start.6 = (bf16[16,128,256]{2,1,0:T(8,128)(2,1)}, bf16[16,128,256]{2,1,0:T(8,128)(2,1)}, u32[]{:S(2)}, u32[]{:S(2)}) collective-permute-start(bf16[16,128,256]{2,1,0:T(8,128)(2,1)} %bitcast.11), channel_id=1, source_target_pairs={{0,4},{8,40},{64,68},{72,104},{1,5},{9,41},{65,69},{73,105},{16,20... | collective-permute-start | bytes 3145736 | tf_op jit(solution)/shard_map/ppermute | solution.py:503
  91.8 32.9 %collective-permute-start.7 = (bf16[16,128,256]{2,1,0:T(8,128)(2,1)}, bf16[16,128,256]{2,1,0:T(8,128)(2,1)}, u32[]{:S(2)}, u32[]{:S(2)}) collective-permute-start(bf16[16,128,256]{2,1,0:T(8,128)(2,1)} %bitcast.12), channel_id=1, source_target_pairs={{0,6},{8,56},{64,70},{72,120},{1,7},{9,57},{65,71},{73,121},{16,22... | collective-permute-start | bytes 3145736 | tf_op jit(solution)/shard_map/ppermute | solution.py:503
  109.8 18.4 %all-to-all-start.1 = ((bf16[16,16,384]{2,1,0:T(8,128)(2,1)}), bf16[16,16,384]{2,1,0:T(8,128)(2,1)}, u32[]{:S(2)}, u32[]{:S(2)}) async-start(bf16[16,16,384]{2,1,0:T(8,128)(2,1)} %broadcast_in_dim.2), calls=%async_computation.1 | async-start | bytes 393216 | tf_op jit(solution)/shard_map/all_to_all | solution.py:507
  116.7 7.9 %copy-start.4 = (bf16[1,2048,256]{2,1,0:T(8,128)(2,1)S(1)}, bf16[1,2048,256]{2,1,0:T(8,128)(2,1)}, u32[]{:S(2)}) copy-start(bf16[1,2048,256]{2,1,0:T(8,128)(2,1)} %get-tuple-element.40) | copy-start | bytes 3145732
  128.2 25.9 %copy-start.2 = (s32[4]{0:T(128)S(1)}, s32[4]{0:T(128)}, u32[]{:S(2)}) copy-start(s32[4]{0:T(128)} %pad_add_fusion.info) | copy-start | bytes 52
  128.2 11.6 %collective-permute-start.12 = (bf16[16,16,384]{2,1,0:T(8,128)(2,1)}, bf16[16,16,384]{2,1,0:T(8,128)(2,1)S(1)}, u32[]{:S(2)}, u32[]{:S(2)}) collective-permute-start(bf16[16,16,384]{2,1,0:T(8,128)(2,1)} %all-to-all-done.1.refs_0_), channel_id=1, source_target_pairs={{0,2},{8,24},{64,66},{72,88},{1,3},{9,25},{65,67},{73,89},{16,18},... | collective-permute-start | bytes 589832 | tf_op jit(solution)/shard_map/ppermute | solution.py:516
  129.5 10.3 %collective-permute-start.13 = (bf16[16,16,384]{2,1,0:T(8,128)(2,1)}, bf16[16,16,384]{2,1,0:T(8,128)(2,1)S(1)}, u32[]{:S(2)}, u32[]{:S(2)}) collective-permute-start(bf16[16,16,384]{2,1,0:T(8,128)(2,1)} %all-to-all-done.1.refs_0_), channel_id=1, source_target_pairs={{0,4},{8,40},{64,68},{72,104},{1,5},{9,41},{65,69},{73,105},{16,20... | collective-permute-start | bytes 589832 | tf_op jit(solution)/shard_map/ppermute | solution.py:516
  132.1 7.7 %collective-permute-start.14 = (bf16[16,16,384]{2,1,0:T(8,128)(2,1)}, bf16[16,16,384]{2,1,0:T(8,128)(2,1)S(1)}, u32[]{:S(2)}, u32[]{:S(2)}) collective-permute-start(bf16[16,16,384]{2,1,0:T(8,128)(2,1)} %all-to-all-done.1.refs_0_), channel_id=1, source_target_pairs={{0,6},{8,56},{64,70},{72,120},{1,7},{9,57},{65,71},{73,121},{16,22... | collective-permute-start | bytes 589832 | tf_op jit(solution)/shard_map/ppermute | solution.py:516
  133.2 24.3 %all-to-all-start.2 = ((bf16[16,128,256]{2,1,0:T(8,128)(2,1)}), bf16[16,128,256]{2,1,0:T(8,128)(2,1)S(1)}, u32[]{:S(2)}, u32[]{:S(2)}) async-start(bf16[16,128,256]{2,1,0:T(8,128)(2,1)} %fusion.2), calls=%async_computation.2 | async-start | bytes 2097152 | tf_op jit(solution)/shard_map/all_to_all | solution.py:515
  139.8 0.7 copy-start.5
  139.8 0.7 copy-start.6
  140.6 0.7 copy-start.7
  143.4 10.7 %collective-permute-start.15 = (bf16[4,16,16,384]{3,2,1,0:T(8,128)(2,1)}, bf16[4,16,16,384]{3,2,1,0:T(8,128)(2,1)S(1)}, u32[]{:S(2)}, u32[]{:S(2)}) collective-permute-start(bf16[4,16,16,384]{3,2,1,0:T(8,128)(2,1)} %shard_map.79.mine), channel_id=1, source_target_pairs={{0,8},{8,0},{64,72},{72,64},{1,9},{9,1},{65,73},{73,65},{16,24},{2... | collective-permute-start | bytes 2359304 | tf_op jit(solution)/shard_map/ppermute | solution.py:518
  154.1 1.1 copy-start

commit v4 on v3

--- a/solution.py
+++ b/solution.py
@@ -20,7 +20,9 @@
 SPOTS = HERE * ROWS * COLS
 BLOCK = 4 * COLS
 BLOCKS = SPOTS // BLOCK
-GROUP = 16
+TALL = 4
+GROUP = TALL * DEPTHS
+STRIPS = SPOTS // (TALL * COLS)
 GROUPS = DEPTHS * SPOTS // GROUP
 SPILL = 64
 CHUNKS = 8
@@ -60,7 +62,7 @@
     clip, tile = lax.axis_index("clip"), lax.axis_index("tile")
     core, y, z_lo = clip % 2, (clip // 2) % 4, clip // 8
     x, z_hi = tile // 2, tile % 2
-    return jnp.stack([x, y, z_hi * 2 + z_lo, core]).astype(jnp.int32)
+    return jnp.stack([x, y, z_hi * 2 + z_lo, core, tile, lax.axis_size("tile")]).astype(jnp.int32)
 
 
 def owner(x0, y0, core, j, m):
@@ -90,8 +92,12 @@
     return found
 
 
-def list_kernel(codes, marked, spilled, count):
-    cells = [codes[pl.ds(d * 32 + r, BLOCKS, stride=4), :] for r in range(4) for d in range(DEPTHS)]
+def list_kernel(codes, marked, extra, parts):
+    cells = [
+        codes[pl.ds(d * HERE * ROWS + r, STRIPS, stride=TALL), :]
+        for r in range(TALL)
+        for d in range(DEPTHS)
+    ]
     later = []
     for a in range(GROUP):
         hit = None
@@ -111,14 +117,17 @@
     marked[...] = 2 * jnp.where(flags > 0, CODES + rank, entries)
     rank = jnp.where(flags > 0, rank, -1)
     for s in range(SPILL):
-        spilled[pl.ds(s, 1), :] = jnp.sum(
+        parts[pl.ds(s, 1), :] = jnp.sum(
             jnp.where(rank == s, 2 * entries, 0), axis=0, keepdims=True
         )
-    spilled[...] = jnp.broadcast_to(
-        jnp.sum(spilled[...].astype(F32), axis=1, keepdims=True), (SPILL, 128)
-    ).astype(jnp.int32)
-    whole = jnp.sum(per_row, axis=0, keepdims=True).astype(jnp.int32)
-    count[...] = jnp.broadcast_to(whole, (8, 128))
+    codes_of = jnp.sum(parts[...].astype(F32), axis=1, keepdims=True)
+    square = lax.broadcasted_iota(jnp.int32, (SPILL, 128), 0) == lax.broadcasted_iota(
+        jnp.int32, (SPILL, 128), 1
+    )
+    spilled = jnp.sum(jnp.where(square, codes_of, 0.0), axis=0, keepdims=True)
+    whole = jnp.sum(per_row, axis=0, keepdims=True)
+    both = jnp.concatenate([jnp.broadcast_to(spilled, (4, 128)), jnp.broadcast_to(whole, (4, 128))])
+    extra[...] = both.astype(jnp.int32)
 
 
 def entry_lists(codes):
@@ -127,22 +136,25 @@
         list_kernel,
         out_shape=[
             jax.ShapeDtypeStruct((128, 128), ints),
-            jax.ShapeDtypeStruct((SPILL, 128), ints),
             jax.ShapeDtypeStruct((8, 128), ints),
         ],
+        scratch_shapes=[pltpu.VMEM((SPILL, 128), ints)],
     )(codes.reshape(128, 128))
 
 
 def quantizer_kernel(
-    spilled, info, count,
+    extra, info,
     marked, plain, codebook, feats, above, below, weights, up,
-    grad, send, keep, weight_send, weight_keep,
-    table, sums, lat, raw, near, taps, window, weight_sum, weight_out, ids, sems,
+    grad, grad_first, grad_last, send, keep, weight_send, weight_keep,
+    table, sums, lat, raw, near, taps, window, weight_sum, weight_out, all_ids, sems, *ids,
 ):
-    many = count[0, 0]
+    many = extra[4, 0]
     windows = window_copies(above, feats, below, window, sems)
     get_taps = pltpu.make_async_copy(weights, taps, sems.at[6])
-    get_ids = pltpu.make_async_copy(marked, ids, sems.at[7])
+    get_ids = [
+        pltpu.make_async_copy(marked.at[pl.ds(c * GROUPS, GROUPS)], ids[c], sems.at[26 + c])
+        for c in range(GROUP)
+    ]
     get_up = pltpu.make_async_copy(up, near, sems.at[8])
     chunk = CODES // CHUNKS
 
@@ -150,14 +162,20 @@
         rows = pl.ds(c * chunk, chunk)
         return pltpu.make_async_copy(codebook.at[rows], raw.at[rows], sems.at[16 + c])
 
-    for copy in windows + [get_taps]:
+    early = [get_taps] + windows[:3]
+    for copy in early + windows[3:]:
         copy.start()
+    for copy in early + windows[3:]:
+        copy.wait()
+    close_frame(info, window)
     for c in range(CHUNKS):
         get_table(c).start()
-    get_ids.start()
-    get_up.start()
-    for copy in windows + [get_taps]:
-        copy.wait()
+    for copy in get_ids + [get_up]:
+        copy.start()
+
+    def line(block, r):
+        row = block * 4 + r
+        return pl.multiple_of(row // TALL * (2 * TALL * COLS), 8) + 2 * (row % TALL)
 
     def convolve(block, carry):
         clip = block // (ROWS // 4)
@@ -170,10 +188,10 @@
                 cols[b] = term if a == 0 else cols[b] + term
         latent = shifted(cols[0], 1) + cols[1] + shifted(cols[2], -1)
         for r in range(4):
-            at = pl.multiple_of(block * (2 * BLOCK), 8) + 2 * r
+            at = line(block, r)
             own = latent[r * COLS : (r + 1) * COLS]
-            lat[pl.ds(at, COLS, stride=8), :] = own[:, :128]
-            lat[pl.ds(at + 1, COLS, stride=8), :] = own[:, 128:]
+            lat[pl.ds(at, COLS, stride=2 * TALL), :] = own[:, :128]
+            lat[pl.ds(at + 1, COLS, stride=2 * TALL), :] = own[:, 128:]
         return carry
 
     lax.fori_loop(0, BLOCKS, convolve, 0)
@@ -195,15 +213,15 @@
     sums[pl.ds(2 * CODES, 2 * SPILL), :] = jnp.zeros((2 * SPILL, 128), F32)
 
     def lend(s, carry):
-        table[pl.ds(2 * (CODES + s), 2), :] = table[pl.ds(spilled[s, 0], 2), :]
+        table[pl.ds(2 * (CODES + s), 2), :] = table[pl.ds(extra[0, s], 2), :]
         return carry
 
     lax.fori_loop(0, jnp.minimum(many, SPILL), lend, 0)
 
     def resids(group, code):
         found = []
-        first = pl.multiple_of(group * 8, 8)
-        for r in range(4):
+        first = pl.multiple_of(group * (2 * TALL), 8)
+        for r in range(TALL):
             here = pl.ds(first + 2 * r, 2)
             resid, total = lat[here, :], None
             for d in range(DEPTHS):
@@ -214,14 +232,15 @@
             lat[here, :] = total
         return found
 
-    get_ids.wait()
+    for copy in get_ids:
+        copy.wait()
 
     @pl.when(many <= SPILL)
     def _():
         def blocks(block, carry):
             def step(col, carry):
                 first = block * COLS + col
-                found = resids(first, lambda r, d: ids[first + (r * DEPTHS + d) * GROUPS])
+                found = resids(first, lambda r, d: ids[r * DEPTHS + d][first])
                 new = [sums[pl.ds(k, 2), :] + v for k, v in found]
                 for (k, _), v in zip(found, new):
                     sums[pl.ds(k, 2), :] = v
@@ -229,10 +248,10 @@
 
             return lax.fori_loop(0, COLS, step, carry, unroll=UNROLL)
 
-        lax.fori_loop(0, BLOCKS, blocks, 0)
+        lax.fori_loop(0, STRIPS, blocks, 0)
 
         def give_back(s, carry):
-            k = spilled[s, 0]
+            k = extra[0, s]
             sums[pl.ds(k, 2), :] = sums[pl.ds(k, 2), :] + sums[pl.ds(2 * (CODES + s), 2), :]
             return carry
 
@@ -240,20 +259,20 @@
 
     @pl.when(many > SPILL)
     def _():
-        again = pltpu.make_async_copy(plain, ids, sems.at[7])
+        again = pltpu.make_async_copy(plain, all_ids, sems.at[7])
         again.start()
         again.wait()
 
         def blocks(block, carry):
             def step(col, carry):
-                spot = block * BLOCK + col
-                for k, v in resids(block * COLS + col, lambda r, d: 2 * ids[d * SPOTS + spot + r * COLS]):
+                spot = block * (TALL * COLS) + col
+                for k, v in resids(block * COLS + col, lambda r, d: 2 * all_ids[d * SPOTS + spot + r * COLS]):
                     sums[pl.ds(k, 2), :] = sums[pl.ds(k, 2), :] + v
                 return carry
 
             return lax.fori_loop(0, COLS, step, carry)
 
-        lax.fori_loop(0, BLOCKS, blocks, 0)
+        lax.fori_loop(0, STRIPS, blocks, 0)
 
     get_up.wait()
 
@@ -263,9 +282,10 @@
 
     def gradient(block, carry):
         rows = pl.ds(pl.multiple_of(block * BLOCK, 16), BLOCK)
-        at = pl.multiple_of(block * (2 * BLOCK), 8)
         halves = [
-            jnp.concatenate([lat[pl.ds(at + 2 * r + h, COLS, stride=8), :] for r in range(4)], axis=0)
+            jnp.concatenate(
+                [lat[pl.ds(line(block, r) + h, COLS, stride=2 * TALL), :] for r in range(4)], axis=0
+            )
             for h in range(2)
         ]
         total = jnp.concatenate(halves, axis=1)
@@ -274,6 +294,17 @@
         return carry
 
     lax.fori_loop(0, BLOCKS, gradient, 0)
+    put_edges = []
+    for out, row in ((grad_first, 0), (grad_last, ROWS - 1)):
+        for n in range(HERE):
+            rows = pl.ds((n * ROWS + row) * COLS, COLS)
+            put_edges.append(
+                pltpu.make_async_copy(
+                    near.at[rows], out.at[n, 0], sems.at[26 + GROUP + len(put_edges)]
+                )
+            )
+    for copy in put_edges:
+        copy.start()
 
     def put_out(out, first, j):
         rows = pl.ds((first + j) * 16 * SHARE, 16 * SHARE)
@@ -310,21 +341,23 @@
 
     lax.fori_loop(0, BLOCKS, weigh, 0)
 
-    def cut(m, carry, side, core, j):
-        near_by = jnp.where(core == 0, info[0], info[1])
-        b = jnp.minimum(core * 64 + (near_by + j) % 4 * 16 + m, PIECES - 1)
-        rows = weight_sum[pl.ds(pl.multiple_of(b * 8, 8), 8), :]
-        both = jnp.concatenate([rows[:, :384], rows[:, 384:]], axis=0)
-        weight_out[side, j, m] = both.astype(BF16)
-        return carry
+    def cut(side, core, j):
+        ring = (jnp.where(core == 0, info[0], info[1]) + j) % 4
+        first = pl.multiple_of(jnp.minimum(core * 64 + ring * 16, PIECES - 16) * 8, 128)
+        for m in range(16):
+            rows = weight_sum[pl.ds(first + 8 * m, 8), :]
+            both = jnp.concatenate([rows[:, :384], rows[:, 384:]], axis=0)
+            weight_out[side, j, m] = both.astype(BF16)
 
     def put_weights(out, side):
         return pltpu.make_async_copy(weight_out.at[side], out, sems.at[24 + side])
 
     for side, core, out in ((0, 1 - info[3], weight_send), (1, info[3], weight_keep)):
         for j in range(4):
-            lax.fori_loop(0, 16, functools.partial(cut, side=side, core=core, j=j), 0, unroll=4)
+            cut(side, core, j)
         put_weights(out, side).start()
+    for copy in put_edges:
+        copy.wait()
     for block in range(BLOCKS):
         put_grad(block).wait()
     for first, out in ((0, send), (4, keep)):
@@ -334,15 +367,15 @@
     put_weights(weight_keep, 1).wait()
 
 
-def quantizer(marked, plain, spilled, info, count, codebook, feats, above, below, weights, up):
+def quantizer(marked, plain, extra, info, codebook, feats, above, below, weights, up):
     hbm = pl.BlockSpec(memory_space=pl.ANY)
     smem = pl.BlockSpec(memory_space=pltpu.SMEM)
     out_shape = (4, 16 * SHARE, CHANS)
     weight_shape = (4, 16) + PIECE
     return pl.pallas_call(
         quantizer_kernel,
-        in_specs=[smem] * 3 + [hbm] * 8,
-        out_specs=[hbm] * 5,
+        in_specs=[smem] * 2 + [hbm] * 8,
+        out_specs=[hbm] * 7,
         scratch_shapes=[
             pltpu.VMEM((2 * (CODES + SPILL), 128), F32),
             pltpu.VMEM((2 * (CODES + SPILL), 128), F32),
@@ -354,10 +387,13 @@
             pltpu.VMEM((3 * CHANS, 3 * CHANS), F32),
             pltpu.VMEM((2,) + weight_shape, BF16),
             pltpu.SMEM((DEPTHS * SPOTS,), jnp.int32),
-            pltpu.SemaphoreType.DMA((26,)),
-        ],
+            pltpu.SemaphoreType.DMA((26 + GROUP + 2 * HERE,)),
+        ]
+        + [pltpu.SMEM((GROUPS,), jnp.int32)] * GROUP,
         out_shape=[
             jax.ShapeDtypeStruct((SPOTS, CHANS), BF16),
+            jax.ShapeDtypeStruct((HERE, 1, COLS, CHANS), BF16),
+            jax.ShapeDtypeStruct((HERE, 1, COLS, CHANS), BF16),
             jax.ShapeDtypeStruct(out_shape, BF16),
             jax.ShapeDtypeStruct(out_shape, BF16),
             jax.ShapeDtypeStruct(weight_shape, BF16),
@@ -367,10 +403,10 @@
         cost_estimate=pl.CostEstimate(
             flops=4 * 9 * SPOTS * CHANS * CHANS, bytes_accessed=64 << 20, transcendentals=0
         ),
-    )(spilled, info, count, marked, plain, codebook, feats, above, below, weights, up)
-
-
-def back_kernel(grad, above, below, weights, out, window, sems):
+    )(extra, info, marked, plain, codebook, feats, above, below, weights, up)
+
+
+def back_kernel(info, grad, above, below, weights, out, window, sems):
     i = pl.program_id(0)
 
     copies = window_copies(above, grad, below, window, sems)
@@ -381,6 +417,7 @@
             copy.start()
         for copy in copies:
             copy.wait()
+        close_frame(info, window)
 
     clip = i // (ROWS // 4)
     row = (i % (ROWS // 4)) * 4
@@ -396,11 +433,12 @@
     out[...] = back.astype(BF16)
 
 
-def feature_grads(grad, above, below, weights):
+def feature_grads(info, grad, above, below, weights):
     return pl.pallas_call(
         back_kernel,
         grid=(BLOCKS,),
         in_specs=[
+            pl.BlockSpec(memory_space=pltpu.SMEM),
             pl.BlockSpec(memory_space=pl.ANY),
             pl.BlockSpec(memory_space=pl.ANY),
             pl.BlockSpec(memory_space=pl.ANY),
@@ -418,7 +456,7 @@
         cost_estimate=pl.CostEstimate(
             flops=2 * 9 * SPOTS * CHANS * CHANS, bytes_accessed=8 << 20, transcendentals=0
         ),
-    )(grad, above, below, weights)
+    )(info, grad, above, below, weights)
 
 
 def turn_kernel(info, *refs):
@@ -471,26 +509,34 @@
     )(info, mine, theirs)
 
 
-def edges(array):
+def edges(first, last):
     n = lax.axis_size("tile")
-    up = [(i, i + 1) for i in range(n - 1)]
-    down = [(i + 1, i) for i in range(n - 1)]
-    above = lax.ppermute(array[:, -1:], "tile", up)
-    below = lax.ppermute(array[:, :1], "tile", down)
+    above = lax.ppermute(last, "tile", [(i, (i + 1) % n) for i in range(n)])
+    below = lax.ppermute(first, "tile", [((i + 1) % n, i) for i in range(n)])
     return above, below
+
+
+def close_frame(info, window):
+    @pl.when(info[4] == 0)
+    def _():
+        window[:, 0] = jnp.zeros((HERE, COLS, CHANS), BF16)
+
+    @pl.when(info[4] == info[5] - 1)
+    def _():
+        window[:, ROWS + 1] = jnp.zeros((HERE, COLS, CHANS), BF16)
 
 
 def on_device(features, conv_weight, codebook, codes, upstream):
     info = place()
-    above, below = edges(features)
-    marked, spilled, count = entry_lists(codes)
-    grad, send, keep, weight_send, weight_keep = quantizer(
-        marked.reshape(-1), codes.reshape(-1), spilled, info, count, codebook, features, above,
-        below, conv_weight, upstream.reshape(SPOTS, CHANS),
+    above, below = edges(features[:, :1], features[:, -1:])
+    marked, extra = entry_lists(codes)
+    grad, grad_first, grad_last, send, keep, weight_send, weight_keep = quantizer(
+        marked.reshape(-1), codes.reshape(-1), extra, info, codebook, features, above, below,
+        conv_weight, upstream.reshape(SPOTS, CHANS),
     )
     got = lax.ppermute(send, BOTH, SWAP)
     grad4 = grad.reshape(features.shape)
-    grad_above, grad_below = edges(grad4)
+    grad_above, grad_below = edges(grad_first, grad_last)
     weight_got = lax.ppermute(weight_send, BOTH, SWAP)
     weight_chip = (weight_keep.astype(F32) + weight_got.astype(F32)).astype(BF16)
     keep, got, grad_above, grad_below = lax.optimization_barrier(
@@ -499,20 +545,23 @@
     weight_ring = weight_chip[0].astype(F32)
     for d in (1, 2, 3):
         weight_ring = weight_ring + lax.ppermute(weight_chip[d], BOTH, first_ring(d)).astype(F32)
-    chip = (keep.astype(F32) + got.astype(F32)).astype(BF16).reshape(4, 16, SHARE, CHANS)
+    chip = [
+        (keep[j].astype(F32) + got[j].astype(F32)).astype(BF16).reshape(16, SHARE, CHANS)
+        for j in range(4)
+    ]
     others = [lax.ppermute(chip[d], BOTH, first_ring(d)) for d in (1, 2, 3)]
-    plane = lax.all_to_all(weight_ring.astype(BF16), BOTH, 0, 0, axis_index_groups=PLANES)
+    weight_ring, grad_above = lax.optimization_barrier((weight_ring.astype(BF16), grad_above))
+    plane = lax.all_to_all(weight_ring, BOTH, 0, 0, axis_index_groups=PLANES)
+    back = feature_grads(info, grad4, grad_above, grad_below, conv_weight)
     piece = plane.astype(F32).sum(0).astype(BF16)
-    piece, grad_above = lax.optimization_barrier((piece, grad_above))
+    piece, back = lax.optimization_barrier((piece, back))
     pieces = lax.all_to_all(
         jnp.broadcast_to(piece[None], (16,) + PIECE), BOTH, 0, 0, axis_index_groups=PLANES
     )
-    back = feature_grads(grad4, grad_above, grad_below, conv_weight)
     ring = chip[0].astype(F32)
     for other in others:
         ring = ring + other.astype(F32)
-    ring, pieces, back = lax.optimization_barrier((ring.astype(BF16), pieces, back))
-    plane = lax.all_to_all(ring, BOTH, 0, 0, axis_index_groups=PLANES)
+    plane = lax.all_to_all(ring.astype(BF16), BOTH, 0, 0, axis_index_groups=PLANES)
     around = [lax.ppermute(pieces, BOTH, first_ring(d)) for d in (1, 2, 3)]
     mine = turned(info, pieces, around)
     theirs = lax.ppermute(mine, BOTH, SWAP)

time: 161 us -> 149 us (0.925)
  starting transfers between devices: 48.9 us -> 44.6 us
  Pallas kernels: 65.8 us -> 62.4 us
  local copies, waits for them, and re-layouts: 7.98 us -> 4.89 us
  blocking collectives: 16.3 us -> 14.5 us
    all_to_all x2, starting transfers between devices: 13.5 us -> 8.68 us  [the longest x1 4.86 us: on_device(): plane = lax.all_to_all(weight_ring, BOTH, 0, 0, axis_index_groups=PLANES)]
    pallas_call x1, Pallas kernels: 51.1 us -> 47 us  [quantizer(): pl.pallas_call(quantizer_kernel, in_specs=[smem] * 2 + [hbm] * 8, out_spe...]
    slice x3 -> x1, local copies, waits for them, and re-layouts: 4.06 us -> 0.99 us  [on_device(): above, below = edges(features[:, :1], features[:, -1:])]
    ppermute x1, starting transfers between devices: 8.56 us -> 11.4 us  [on_device(): theirs = lax.ppermute(mine, BOTH, SWAP)]
    all_to_all x1, blocking collectives: 16.3 us -> 14.5 us  [on_device(): lax.all_to_all(jnp.broadcast_to(piece[None], (16,) + PIECE), BOTH, 0, 0,...]
    ppermute x1, starting transfers between devices: 2.3 us -> 0.55 us  [on_device(): got = lax.ppermute(send, BOTH, SWAP)]
  transfers between devices with their start and end apart: 18 -> 18, of which waited for: 3 -> 4; matrix products, arithmetic and copies ran while one was open for 9% -> 8% of each run, Pallas kernels for 9% -> 10%
where the time goes in v4:
time: 149 us; the launch traced here: 148 us
  Pallas kernels  62.4 us (42%)
  starting transfers between devices  44.6 us (30%)
  blocking collectives  14.5 us (10%)
  other arithmetic  11.8 us (8%)
  waiting for transfers between devices  8.75 us (6%)
  local copies, waits for them, and re-layouts  4.89 us (3%)
    pallas_call x1, Pallas kernels, quantizer(): pl.pallas_call(quantizer_kernel, in_specs=[smem] * 2 + [hbm] * 8, out_spe...  47 us
    all_to_all x1, blocking collectives, on_device(): lax.all_to_all(jnp.broadcast_to(piece[None], (16,) + PIECE), BOTH, 0, 0,...  14.5 us
    ppermute x1, starting transfers between devices, on_device(): theirs = lax.ppermute(mine, BOTH, SWAP)  11.4 us
    pallas_call x1, Pallas kernels, feature_grads(): pl.pallas_call(back_kernel, grid=(BLOCKS,), in_specs=[pl.BlockSpec(memory...  8.51 us
    ppermute x2, starting transfers between devices, edges(): below = lax.ppermute(first, 'tile', [((i + 1) % n, i) for i in range(n)])  6.56 us
    ppermute x2, starting transfers between devices, edges(): above = lax.ppermute(last, 'tile', [(i, (i + 1) % n) for i in range(n)])  5.29 us
    ppermute x3, starting transfers between devices, on_device(): lax.ppermute(weight_chip[d], BOTH, first_ring(d)).astype(F32)  5.09 us
    all_to_all x1, starting transfers between devices, on_device(): plane = lax.all_to_all(weight_ring, BOTH, 0, 0, axis_index_groups=PLANES)  4.86 us
  transfers between devices with their start and end apart: 18, of which 4 were waited for; matrix products, arithmetic and copies ran while one was open for 8% of the time, Pallas kernels for 10%

profile of v4, /device:TPU:1, one launch (start us, length us, event | category | flops | bytes accessed | tf_op | source)
XLA Modules:
  0.0 147.7 jit_solution(5593016726690734726)
XLA Ops:
  0.6 1.0 fusion.6
  1.6 4.5 %collective-permute-start = (bf16[2,1,128,256]{3,2,1,0:T(8,128)(2,1)S(1)}, bf16[2,1,128,256]{3,2,1,0:T(8,128)(2,1)S(1)}, u32[]{:S(2)}, u32[]{:S(2)}) collective-permute-start(bf16[2,1,128,256]{3,2,1,0:T(8,128)(2,1)S(1)} %get-tuple-element.42), channel_id=1, source_target_pairs={{0,1},{1,2},{2,3},{3,4},{4,5},{5,6},{6,7},{7,0},{8,9},{9,10},{10,1... | collective-permute-start | bytes 393224 | tf_op jit(solution)/shard_map/ppermute | solution.py:514
  6.1 2.3 %collective-permute-start.1 = (bf16[2,1,128,256]{3,2,1,0:T(8,128)(2,1)S(1)}, bf16[2,1,128,256]{3,2,1,0:T(8,128)(2,1)S(1)}, u32[]{:S(2)}, u32[]{:S(2)}) collective-permute-start(bf16[2,1,128,256]{3,2,1,0:T(8,128)(2,1)S(1)} %get-tuple-element.41), channel_id=1, source_target_pairs={{1,0},{2,1},{3,2},{4,3},{5,4},{6,5},{7,6},{0,7},{9,8},{10,9},{11,1... | collective-permute-start | bytes 393224 | tf_op jit(solution)/shard_map/ppermute | solution.py:515
  8.4 2.4 %shard_map.76 = (s32[128,128]{1,0:T(8,128)}, s32[8,128]{1,0:T(8,128)}) custom-call(s32[128,128]{1,0:T(8,128)} %bitcast.29), custom_call_target="tpu_custom_call" | custom-call | tf_op jit(solution)/shard_map/pallas_call | solution.py:135
  11.5 3.5 %collective-permute-done.1.below = bf16[2,1,128,256]{3,2,1,0:T(8,128)(2,1)S(1)} collective-permute-done((bf16[2,1,128,256]{3,2,1,0:T(8,128)(2,1)S(1)}, bf16[2,1,128,256]{3,2,1,0:T(8,128)(2,1)S(1)}, u32[]{:S(2)}, u32[]{:S(2)}) %collective-permute-start.1) | collective-permute-done | bytes 131104 | tf_op jit(solution)/shard_map/ppermute | solution.py:515
  15.7 47.0 %shard_map.77 = (bf16[4096,256]{1,0:T(8,128)(2,1)}, bf16[2,1,128,256]{3,2,1,0:T(8,128)(2,1)}, bf16[2,1,128,256]{3,2,1,0:T(8,128)(2,1)}, bf16[4,2048,256]{2,1,0:T...) custom-call(s32[8,128]{1,0:T(8,128)} %get-tuple-element.20.extra, ...), custom_call_target="tpu_custom_call" | custom-call | flops 9663676416 | bytes 67108864 | tf_op jit(solution)/shard_map/pallas_call | solution.py:375
  63.4 0.8 collective-permute-start.7
  64.2 4.3 %collective-permute-start.8 = (bf16[2,1,128,256]{3,2,1,0:T(8,128)(2,1)}, bf16[2,1,128,256]{3,2,1,0:T(8,128)(2,1)S(1)}, u32[]{:S(2)}, u32[]{:S(2)}) collective-permute-start(bf16[2,1,128,256]{3,2,1,0:T(8,128)(2,1)} %get-tuple-element.27), channel_id=1, source_target_pairs={{1,0},{2,1},{3,2},{4,3},{5,4},{6,5},{7,6},{0,7},{9,8},{10,9},{11,1... | collective-permute-start | bytes 393224 | tf_op jit(solution)/shard_map/ppermute | solution.py:515
  68.5 2.9 %collective-permute-done.2 = bf16[4,16,16,384]{3,2,1,0:T(8,128)(2,1)S(1)} collective-permute-done((bf16[4,16,16,384]{3,2,1,0:T(8,128)(2,1)}, bf16[4,16,16,384]{3,2,1,0:T(8,128)(2,1)S(1)}, u32[]{:S(2)}, u32[]{:S(2)}) %collective-permute-start.2) | collective-permute-done | bytes 786464 | tf_op jit(solution)/shard_map/ppermute | solution.py:540
  71.4 1.3 add_convert_fusion.4
  72.8 1.4 collective-permute-start.3
  74.2 2.6 %collective-permute-start.4 = (bf16[16,16,384]{2,1,0:T(8,128)(2,1)S(1)}, bf16[16,16,384]{2,1,0:T(8,128)(2,1)S(1)}, u32[]{:S(2)}, u32[]{:S(2)}) collective-permute-start(bf16[16,16,384]{2,1,0:T(8,128)(2,1)S(1)} %get-tuple-element.45), channel_id=1, source_target_pairs={{0,4},{8,40},{64,68},{72,104},{1,5},{9,41},{65,69},{73,105},{16,20... | collective-permute-start | bytes 589832 | tf_op jit(solution)/shard_map/ppermute | solution.py:547
  76.8 1.1 collective-permute-start.5
  78.0 4.1 %add_convert_fusion.2 = (bf16[1,2048,256]{2,1,0:T(8,128)(2,1)}, bf16[1,2048,256]{2,1,0:T(8,128)(2,1)}, bf16[1,2048,256]{2,1,0:T(8,128)(2,1)}, bf16[1,2048,256]{2,1,0:T(8,128)(2,1)}) fusion(bf16[4,2048,256]{2,1,0:T(8,128)(2,1)S(1)} %collective-permute-done.6, bf16[4,2048,256]{2,1,0:T(8,128)(2,1)} %get-tuple-element.35), kind=kLoop, calls=%fused_computation.7 | loop fusion | flops 8388608 | bytes 12582912 | tf_op jit(solution)/shard_map/convert_element_type | solution.py:549
  82.4 0.8 collective-permute-start.14
  83.3 1.6 %collective-permute-start.15 = (bf16[16,128,256]{2,1,0:T(8,128)(2,1)}, bf16[16,128,256]{2,1,0:T(8,128)(2,1)}, u32[]{:S(2)}, u32[]{:S(2)}) collective-permute-start(bf16[16,128,256]{2,1,0:T(8,128)(2,1)} %bitcast.18), channel_id=1, source_target_pairs={{0,6},{8,56},{64,70},{72,120},{1,7},{9,57},{65,71},{73,121},{16,22... | collective-permute-start | bytes 3145736 | tf_op jit(solution)/shard_map/ppermute | solution.py:552
  84.9 0.8 fusion.5
  85.7 4.9 %all-to-all-start = ((bf16[16,16,384]{2,1,0:T(8,128)(2,1)}), bf16[16,16,384]{2,1,0:T(8,128)(2,1)}, u32[]{:S(2)}, u32[]{:S(2)}) async-start(bf16[16,16,384]{2,1,0:T(8,128)(2,1)} %fusion.5), calls=%async_computation | async-start | bytes 393216 | tf_op jit(solution)/shard_map/all_to_all | solution.py:554
  90.6 8.5 %shard_map.78 = bf16[4096,256]{1,0:T(8,128)(2,1)} custom-call(s32[6]{0:T(128)S(1)} %copy-done.1, bf16[2,16,128,256]{3,2,1,0:T(8,128)(2,1)S(1)} %bitcast.27, bf16[2,1,128,256]{3,2,1,0:T(8,128)(2,1)S(1)} %collective-permute-done.7.above, bf16[2,1,128,256]{3,2,1,0:T(8,128)(2,1)S(1)} %collective-permute-done.8.below, bf16[9,256,256]{2,1,0:T(8,128)(2,1)S(1)} %copy-done.3), custom_call_target="tpu_custom_call" | custom-call | flops 4831838208 | bytes 8388608 | tf_op jit(solution)/shard_map/pallas_call | solution.py:437
  99.1 1.0 reduce_sum.21
  100.1 14.5 %all_to_all.15.refs_0_ = bf16[16,16,384]{2,1,0:T(8,128)(2,1)S(1)} all-to-all(bf16[16,16,384]{2,1,0:T(8,128)(2,1)S(1)} %broadcast_in_dim.2), channel_id=1, replica_groups={{0,64,1,65,16,80,17,81,32,96,33,97,48,112,49,113},{2,66,3,67,18,82,19,8..., dimensions={0} | all-to-all | bytes 393216 | tf_op jit(solution)/shard_map/all_to_all | solution.py:558
  114.6 2.6 %collective-permute-start.10 = (bf16[16,16,384]{2,1,0:T(8,128)(2,1)S(1)}, bf16[16,16,384]{2,1,0:T(8,128)(2,1)S(1)}, u32[]{:S(2)}, u32[]{:S(2)}) collective-permute-start(bf16[16,16,384]{2,1,0:T(8,128)(2,1)S(1)} %all_to_all.15.refs_0_), channel_id=1, source_target_pairs={{0,4},{8,40},{64,68},{72,104},{1,5},{9,41},{65,69},{73,105},{16,20... | collective-permute-start | bytes 589832 | tf_op jit(solution)/shard_map/ppermute | solution.py:565
  117.2 0.8 collective-permute-start.11
  118.0 0.7 collective-permute-start.9
  118.7 3.9 %fusion.2 = bf16[16,128,256]{2,1,0:T(8,128)(2,1)} fusion(bf16[16,128,256]{2,1,0:T(8,128)(2,1)} %bitcast.28, bf16[16,128,256]{2,1,0:T(8,128)(2,1)} %collective-permute-done.15, bf16[16,128,256]{2,1,0:T(8,128)(2,1)} %collective-permute-done.14, bf16[16,128,256]{2,1,0:T(8,128)(2,1)} %collective-permute-done.13), kind=kLoop, calls=%fused_computation.3 | loop fusion | flops 4194304 | bytes 5242880 | tf_op jit(solution)/shard_map/convert_element_type | solution.py:564
  122.5 3.8 %all-to-all-start.2 = ((bf16[16,128,256]{2,1,0:T(8,128)(2,1)}), bf16[16,128,256]{2,1,0:T(8,128)(2,1)S(1)}, u32[]{:S(2)}, u32[]{:S(2)}) async-start(bf16[16,128,256]{2,1,0:T(8,128)(2,1)} %fusion.2), calls=%async_computation.2 | async-start | bytes 2097152 | tf_op jit(solution)/shard_map/all_to_all | solution.py:564
  127.8 2.2 %shard_map.79.mine = bf16[4,16,16,384]{3,2,1,0:T(8,128)(2,1)} custom-call(s32[6]{0:T(128)} %stack.23.info, bf16[16,16,384]{2,1,0:T(8,128)(2,1)} %copy-done.5, bf16[16,16,384]{2,1,0:T(8,128)(2,1)} %copy-done.8, bf16[16,16,384]{2,1,0:T(8,128)(2,1)} %copy-done.6, bf16[16,16,384]{2,1,0:T(8,128)(2,1)} %copy-done.7), custom_call_target="tpu_custom_call" | custom-call | tf_op jit(solution)/shard_map/pallas_call | solution.py:469
  130.0 11.4 %collective-permute-start.12 = (bf16[4,16,16,384]{3,2,1,0:T(8,128)(2,1)}, bf16[4,16,16,384]{3,2,1,0:T(8,128)(2,1)S(1)}, u32[]{:S(2)}, u32[]{:S(2)}) collective-permute-start(bf16[4,16,16,384]{3,2,1,0:T(8,128)(2,1)} %shard_map.79.mine), channel_id=1, source_target_pairs={{0,8},{8,0},{64,72},{72,64},{1,9},{9,1},{65,73},{73,65},{16,24},{2... | collective-permute-start | bytes 2359304 | tf_op jit(solution)/shard_map/ppermute | solution.py:567
  141.4 2.1 %collective-permute-done.12.theirs = bf16[4,16,16,384]{3,2,1,0:T(8,128)(2,1)S(1)} collective-permute-done((bf16[4,16,16,384]{3,2,1,0:T(8,128)(2,1)}, bf16[4,16,16,384]{3,2,1,0:T(8,128)(2,1)S(1)}, u32[]{:S(2)}, u32[]{:S(2)}) %collective-permute-start.12) | collective-permute-done | bytes 786464 | tf_op jit(solution)/shard_map/ppermute | solution.py:567
  143.5 1.1 copy-done
  144.7 2.2 %shard_map.80 = f32[9,256,256]{2,1,0:T(8,128)} custom-call(s32[6]{0:T(128)S(1)} %copy-done.2, bf16[4,16,16,384]{3,2,1,0:T(8,128)(2,1)S(1)} %copy-done, bf16[4,16,16,384]{3,2,1,0:T(8,128)(2,1)S(1)} %collective-permute-done.12.theirs), custom_call_target="tpu_custom_call" | custom-call | tf_op jit(solution)/shard_map/pallas_call | solution.py:504
  146.9 0.8 convert_reduce_fusion
  (42 shorter events, 3.9 us)
Async XLA Ops:
  1.6 9.9 %collective-permute-start = (bf16[2,1,128,256]{3,2,1,0:T(8,128)(2,1)S(1)}, bf16[2,1,128,256]{3,2,1,0:T(8,128)(2,1)S(1)}, u32[]{:S(2)}, u32[]{:S(2)}) collective-permute-start(bf16[2,1,128,256]{3,2,1,0:T(8,128)(2,1)S(1)} %get-tuple-element.42), channel_id=1, source_target_pairs={{0,1},{1,2},{2,3},{3,4},{4,5},{5,6},{6,7},{7,0},{8,9},{9,10},{10,1... | collective-permute-start | bytes 393224 | tf_op jit(solution)/shard_map/ppermute | solution.py:514
  6.1 9.0 %collective-permute-start.1 = (bf16[2,1,128,256]{3,2,1,0:T(8,128)(2,1)S(1)}, bf16[2,1,128,256]{3,2,1,0:T(8,128)(2,1)S(1)}, u32[]{:S(2)}, u32[]{:S(2)}) collective-permute-start(bf16[2,1,128,256]{3,2,1,0:T(8,128)(2,1)S(1)} %get-tuple-element.41), channel_id=1, source_target_pairs={{1,0},{2,1},{3,2},{4,3},{5,4},{6,5},{7,6},{0,7},{9,8},{10,9},{11,1... | collective-permute-start | bytes 393224 | tf_op jit(solution)/shard_map/ppermute | solution.py:515
  11.5 3.5 %copy-start.9 = (bf16[2,1,128,256]{3,2,1,0:T(8,128)(2,1)}, bf16[2,1,128,256]{3,2,1,0:T(8,128)(2,1)S(1)}, u32[]{:S(2)}) copy-start(bf16[2,1,128,256]{3,2,1,0:T(8,128)(2,1)S(1)} %collective-permute-done.above) | copy-start | bytes 393220
  15.1 0.6 copy-start.10
  62.8 15.2 %collective-permute-start.6 = (bf16[4,2048,256]{2,1,0:T(8,128)(2,1)}, bf16[4,2048,256]{2,1,0:T(8,128)(2,1)S(1)}, u32[]{:S(2)}, u32[]{:S(2)}) collective-permute-start(bf16[4,2048,256]{2,1,0:T(8,128)(2,1)} %get-tuple-element.25), channel_id=1, source_target_pairs={{0,8},{8,0},{64,72},{72,64},{1,9},{9,1},{65,73},{73,65},{16,24},{2... | collective-permute-start | bytes 12582920 | tf_op jit(solution)/shard_map/ppermute | solution.py:537
  63.3 8.1 %collective-permute-start.2 = (bf16[4,16,16,384]{3,2,1,0:T(8,128)(2,1)}, bf16[4,16,16,384]{3,2,1,0:T(8,128)(2,1)S(1)}, u32[]{:S(2)}, u32[]{:S(2)}) collective-permute-start(bf16[4,16,16,384]{3,2,1,0:T(8,128)(2,1)} %get-tuple-element.23), channel_id=1, source_target_pairs={{0,8},{8,0},{64,72},{72,64},{1,9},{9,1},{65,73},{73,65},{16,24},{2... | collective-permute-start | bytes 2359304 | tf_op jit(solution)/shard_map/ppermute | solution.py:540
  63.4 13.4 %collective-permute-start.7 = (bf16[2,1,128,256]{3,2,1,0:T(8,128)(2,1)}, bf16[2,1,128,256]{3,2,1,0:T(8,128)(2,1)S(1)}, u32[]{:S(2)}, u32[]{:S(2)}) collective-permute-start(bf16[2,1,128,256]{3,2,1,0:T(8,128)(2,1)} %get-tuple-element.26), channel_id=1, source_target_pairs={{0,1},{1,2},{2,3},{3,4},{4,5},{5,6},{6,7},{7,0},{8,9},{9,10},{10,1... | collective-permute-start | bytes 393224 | tf_op jit(solution)/shard_map/ppermute | solution.py:514
  64.2 13.7 %collective-permute-start.8 = (bf16[2,1,128,256]{3,2,1,0:T(8,128)(2,1)}, bf16[2,1,128,256]{3,2,1,0:T(8,128)(2,1)S(1)}, u32[]{:S(2)}, u32[]{:S(2)}) collective-permute-start(bf16[2,1,128,256]{3,2,1,0:T(8,128)(2,1)} %get-tuple-element.27), channel_id=1, source_target_pairs={{1,0},{2,1},{3,2},{4,3},{5,4},{6,5},{7,6},{0,7},{9,8},{10,9},{11,1... | collective-permute-start | bytes 393224 | tf_op jit(solution)/shard_map/ppermute | solution.py:515
  72.8 10.4 %collective-permute-start.3 = (bf16[16,16,384]{2,1,0:T(8,128)(2,1)S(1)}, bf16[16,16,384]{2,1,0:T(8,128)(2,1)S(1)}, u32[]{:S(2)}, u32[]{:S(2)}) collective-permute-start(bf16[16,16,384]{2,1,0:T(8,128)(2,1)S(1)} %get-tuple-element.43), channel_id=1, source_target_pairs={{0,2},{8,24},{64,66},{72,88},{1,3},{9,25},{65,67},{73,89},{16,18},... | collective-permute-start | bytes 589832 | tf_op jit(solution)/shard_map/ppermute | solution.py:547
  74.2 10.7 %collective-permute-start.4 = (bf16[16,16,384]{2,1,0:T(8,128)(2,1)S(1)}, bf16[16,16,384]{2,1,0:T(8,128)(2,1)S(1)}, u32[]{:S(2)}, u32[]{:S(2)}) collective-permute-start(bf16[16,16,384]{2,1,0:T(8,128)(2,1)S(1)} %get-tuple-element.45), channel_id=1, source_target_pairs={{0,4},{8,40},{64,68},{72,104},{1,5},{9,41},{65,69},{73,105},{16,20... | collective-permute-start | bytes 589832 | tf_op jit(solution)/shard_map/ppermute | solution.py:547
  76.8 8.1 %collective-permute-start.5 = (bf16[16,16,384]{2,1,0:T(8,128)(2,1)S(1)}, bf16[16,16,384]{2,1,0:T(8,128)(2,1)S(1)}, u32[]{:S(2)}, u32[]{:S(2)}) collective-permute-start(bf16[16,16,384]{2,1,0:T(8,128)(2,1)S(1)} %get-tuple-element.44), channel_id=1, source_target_pairs={{0,6},{8,56},{64,70},{72,120},{1,7},{9,57},{65,71},{73,121},{16,22... | collective-permute-start | bytes 589832 | tf_op jit(solution)/shard_map/ppermute | solution.py:547
  77.9 12.6 %copy-start.1 = (s32[6]{0:T(128)S(1)}, s32[6]{0:T(128)}, u32[]{:S(2)}) copy-start(s32[6]{0:T(128)} %stack.23.info) | copy-start | bytes 76
  77.9 12.6 %copy-start.3 = (bf16[9,256,256]{2,1,0:T(8,128)(2,1)S(1)}, bf16[9,256,256]{2,1,0:T(8,128)(2,1)}, u32[]{:S(2)}) copy-start(bf16[9,256,256]{2,1,0:T(8,128)(2,1)} %weights.3) | copy-start | bytes 3538948
  77.9 12.6 %copy-start.4 = (bf16[4096,256]{1,0:T(8,128)(2,1)S(1)}, bf16[4096,256]{1,0:T(8,128)(2,1)}, u32[]{:S(2)}) copy-start(bf16[4096,256]{1,0:T(8,128)(2,1)} %get-tuple-element.30) | copy-start | bytes 6291460
  82.1 35.9 %collective-permute-start.13 = (bf16[16,128,256]{2,1,0:T(8,128)(2,1)}, bf16[16,128,256]{2,1,0:T(8,128)(2,1)}, u32[]{:S(2)}, u32[]{:S(2)}) collective-permute-start(bf16[16,128,256]{2,1,0:T(8,128)(2,1)} %bitcast.16), channel_id=1, source_target_pairs={{0,2},{8,24},{64,66},{72,88},{1,3},{9,25},{65,67},{73,89},{16,18},... | collective-permute-start | bytes 3145736 | tf_op jit(solution)/shard_map/ppermute | solution.py:552
  82.4 36.3 %collective-permute-start.14 = (bf16[16,128,256]{2,1,0:T(8,128)(2,1)}, bf16[16,128,256]{2,1,0:T(8,128)(2,1)}, u32[]{:S(2)}, u32[]{:S(2)}) collective-permute-start(bf16[16,128,256]{2,1,0:T(8,128)(2,1)} %bitcast.17), channel_id=1, source_target_pairs={{0,4},{8,40},{64,68},{72,104},{1,5},{9,41},{65,69},{73,105},{16,20... | collective-permute-start | bytes 3145736 | tf_op jit(solution)/shard_map/ppermute | solution.py:552
  83.3 35.4 %collective-permute-start.15 = (bf16[16,128,256]{2,1,0:T(8,128)(2,1)}, bf16[16,128,256]{2,1,0:T(8,128)(2,1)}, u32[]{:S(2)}, u32[]{:S(2)}) collective-permute-start(bf16[16,128,256]{2,1,0:T(8,128)(2,1)} %bitcast.18), channel_id=1, source_target_pairs={{0,6},{8,56},{64,70},{72,120},{1,7},{9,57},{65,71},{73,121},{16,22... | collective-permute-start | bytes 3145736 | tf_op jit(solution)/shard_map/ppermute | solution.py:552
  85.7 13.4 %all-to-all-start = ((bf16[16,16,384]{2,1,0:T(8,128)(2,1)}), bf16[16,16,384]{2,1,0:T(8,128)(2,1)}, u32[]{:S(2)}, u32[]{:S(2)}) async-start(bf16[16,16,384]{2,1,0:T(8,128)(2,1)} %fusion.5), calls=%async_computation | async-start | bytes 393216 | tf_op jit(solution)/shard_map/all_to_all | solution.py:554
  114.6 8.0 %copy-start.5 = (bf16[16,16,384]{2,1,0:T(8,128)(2,1)}, bf16[16,16,384]{2,1,0:T(8,128)(2,1)S(1)}, u32[]{:S(2)}) copy-start(bf16[16,16,384]{2,1,0:T(8,128)(2,1)S(1)} %all_to_all.15.refs_0_) | copy-start | bytes 589828
  114.6 11.8 %collective-permute-start.10 = (bf16[16,16,384]{2,1,0:T(8,128)(2,1)S(1)}, bf16[16,16,384]{2,1,0:T(8,128)(2,1)S(1)}, u32[]{:S(2)}, u32[]{:S(2)}) collective-permute-start(bf16[16,16,384]{2,1,0:T(8,128)(2,1)S(1)} %all_to_all.15.refs_0_), channel_id=1, source_target_pairs={{0,4},{8,40},{64,68},{72,104},{1,5},{9,41},{65,69},{73,105},{16,20... | collective-permute-start | bytes 589832 | tf_op jit(solution)/shard_map/ppermute | solution.py:565
  117.2 9.2 %collective-permute-start.11 = (bf16[16,16,384]{2,1,0:T(8,128)(2,1)S(1)}, bf16[16,16,384]{2,1,0:T(8,128)(2,1)S(1)}, u32[]{:S(2)}, u32[]{:S(2)}) collective-permute-start(bf16[16,16,384]{2,1,0:T(8,128)(2,1)S(1)} %all_to_all.15.refs_0_), channel_id=1, source_target_pairs={{0,6},{8,56},{64,70},{72,120},{1,7},{9,57},{65,71},{73,121},{16,22... | collective-permute-start | bytes 589832 | tf_op jit(solution)/shard_map/ppermute | solution.py:565
  118.0 8.4 %collective-permute-start.9 = (bf16[16,16,384]{2,1,0:T(8,128)(2,1)S(1)}, bf16[16,16,384]{2,1,0:T(8,128)(2,1)S(1)}, u32[]{:S(2)}, u32[]{:S(2)}) collective-permute-start(bf16[16,16,384]{2,1,0:T(8,128)(2,1)S(1)} %all_to_all.15.refs_0_), channel_id=1, source_target_pairs={{0,2},{8,24},{64,66},{72,88},{1,3},{9,25},{65,67},{73,89},{16,18},... | collective-permute-start | bytes 589832 | tf_op jit(solution)/shard_map/ppermute | solution.py:565
  122.5 21.0 %copy-start.2 = (s32[6]{0:T(128)S(1)}, s32[6]{0:T(128)}, u32[]{:S(2)}) copy-start(s32[6]{0:T(128)} %stack.23.info) | copy-start | bytes 76
  122.5 24.3 %all-to-all-start.2 = ((bf16[16,128,256]{2,1,0:T(8,128)(2,1)}), bf16[16,128,256]{2,1,0:T(8,128)(2,1)S(1)}, u32[]{:S(2)}, u32[]{:S(2)}) async-start(bf16[16,128,256]{2,1,0:T(8,128)(2,1)} %fusion.2), calls=%async_computation.2 | async-start | bytes 2097152 | tf_op jit(solution)/shard_map/all_to_all | solution.py:564
  126.4 0.7 copy-start.6
  126.4 0.7 copy-start.7
  127.1 0.7 copy-start.8
  130.0 13.5 %collective-permute-start.12 = (bf16[4,16,16,384]{3,2,1,0:T(8,128)(2,1)}, bf16[4,16,16,384]{3,2,1,0:T(8,128)(2,1)S(1)}, u32[]{:S(2)}, u32[]{:S(2)}) collective-permute-start(bf16[4,16,16,384]{3,2,1,0:T(8,128)(2,1)} %shard_map.79.mine), channel_id=1, source_target_pairs={{0,8},{8,0},{64,72},{72,64},{1,9},{9,1},{65,73},{73,65},{16,24},{2... | collective-permute-start | bytes 2359304 | tf_op jit(solution)/shard_map/ppermute | solution.py:567
  143.5 1.1 copy-start

commit v5 on v4

--- a/solution.py
+++ b/solution.py
@@ -26,14 +26,14 @@
 GROUPS = DEPTHS * SPOTS // GROUP
 SPILL = 64
 CHUNKS = 8
-UNROLL = 8
+UNROLL = 16
 PIECES = 96
 PIECE = (16, 384)
 SHARE = CODES // 128
 
 
 def lin(x, y, z, core):
-    return (((z % 2) * 4 + y) * 2 + core) * 8 + x * 2 + z // 2
+    return (((z & 1) * 4 + y) * 2 + core) * 8 + x * 2 + (z >> 1)
 
 
 def moves(where):
@@ -66,9 +66,9 @@
 
 
 def owner(x0, y0, core, j, m):
-    other, z = m // 4, m % 4
-    x = jnp.where(core == 0, (x0 + j) % 4, other)
-    y = jnp.where(core == 0, other, (y0 + j) % 4)
+    other, z = m >> 2, m & 3
+    x = jnp.where(core == 0, (x0 + j) & 3, other)
+    y = jnp.where(core == 0, other, (y0 + j) & 3)
     return lin(x, y, z, core)
 
 
@@ -174,12 +174,11 @@
         copy.start()
 
     def line(block, r):
-        row = block * 4 + r
-        return pl.multiple_of(row // TALL * (2 * TALL * COLS), 8) + 2 * (row % TALL)
+        return pl.multiple_of(block * (2 * TALL * COLS), 8) + 2 * r
 
     def convolve(block, carry):
-        clip = block // (ROWS // 4)
-        row = (block % (ROWS // 4)) * 4
+        clip = block >> 2
+        row = (block & 3) * 4
         cols = [None] * 3
         for a in range(3):
             part = window[clip, pl.ds(row + a, 4)].reshape(BLOCK, CHANS)
@@ -370,11 +369,12 @@
 def quantizer(marked, plain, extra, info, codebook, feats, above, below, weights, up):
     hbm = pl.BlockSpec(memory_space=pl.ANY)
     smem = pl.BlockSpec(memory_space=pltpu.SMEM)
+    vmem = pl.BlockSpec(memory_space=pltpu.VMEM)
     out_shape = (4, 16 * SHARE, CHANS)
     weight_shape = (4, 16) + PIECE
     return pl.pallas_call(
         quantizer_kernel,
-        in_specs=[smem] * 2 + [hbm] * 8,
+        in_specs=[smem] * 2 + [hbm] * 4 + [vmem] * 2 + [hbm] * 2,
         out_specs=[hbm] * 7,
         scratch_shapes=[
             pltpu.VMEM((2 * (CODES + SPILL), 128), F32),
@@ -457,6 +457,35 @@
             flops=2 * 9 * SPOTS * CHANS * CHANS, bytes_accessed=8 << 20, transcendentals=0
         ),
     )(info, grad, above, below, weights)
+
+
+def add_kernel(*refs):
+    *parts, out = refs
+    rows = 256
+
+    def add(i, carry):
+        here = pl.ds(pl.multiple_of(i * rows, 16), rows)
+        total = parts[0][here, :].astype(F32)
+        for part in parts[1:]:
+            total = total + part[here, :].astype(F32)
+        out[here, :] = total.astype(BF16)
+        return carry
+
+    lax.fori_loop(0, out.shape[0] // rows, add, 0)
+
+
+def added(*parts):
+    shape = parts[0].shape
+    flat = [part.reshape(-1, CHANS) for part in parts]
+    total = pl.pallas_call(
+        add_kernel,
+        out_shape=jax.ShapeDtypeStruct(flat[0].shape, BF16),
+        compiler_params=pltpu.CompilerParams(vmem_limit_bytes=24 << 20),
+        cost_estimate=pl.CostEstimate(
+            flops=2 * flat[0].size, bytes_accessed=8 * flat[0].size, transcendentals=0
+        ),
+    )(*flat)
+    return total.reshape(shape)
 
 
 def turn_kernel(info, *refs):
@@ -558,10 +587,8 @@
     pieces = lax.all_to_all(
         jnp.broadcast_to(piece[None], (16,) + PIECE), BOTH, 0, 0, axis_index_groups=PLANES
     )
-    ring = chip[0].astype(F32)
-    for other in others:
-        ring = ring + other.astype(F32)
-    plane = lax.all_to_all(ring.astype(BF16), BOTH, 0, 0, axis_index_groups=PLANES)
+    ring = added(chip[0], *others)
+    plane = lax.all_to_all(ring, BOTH, 0, 0, axis_index_groups=PLANES)
     around = [lax.ppermute(pieces, BOTH, first_ring(d)) for d in (1, 2, 3)]
     mine = turned(info, pieces, around)
     theirs = lax.ppermute(mine, BOTH, SWAP)

time: 149 us -> 146 us (0.980)
  other arithmetic: 11.8 us -> 7.61 us
  local copies, waits for them, and re-layouts: 4.89 us -> 7.03 us
    convert_element_type x1 -> x0, other arithmetic: 3.86 us -> none  [on_device(): ring.astype(BF16)]
    unnamed x22 -> x18, local copies, waits for them, and re-layouts: 3.18 us -> 5.33 us
    pallas_call x1 -> x2, Pallas kernels: 47 us -> 48.3 us  [the longest x1 45.5 us: quantizer(): pl.pallas_call(quantizer_kernel, in_specs=[smem] * 2 + [hbm] * 4 + [vmem]...]
  transfers between devices with their start and end apart: 18 -> 18, of which waited for: 4 -> 4; matrix products, arithmetic and copies ran while one was open for 8% -> 5% of each run, Pallas kernels for 10% -> 12%
where the time goes in v5:
time: 146 us; the launch traced here: 145 us
  Pallas kernels  63.6 us (44%)
  starting transfers between devices  44.2 us (30%)
  blocking collectives  13.3 us (9%)
  waiting for transfers between devices  8.76 us (6%)
  other arithmetic  7.61 us (5%)
  local copies, waits for them, and re-layouts  7.03 us (5%)
    pallas_call x1, Pallas kernels, quantizer(): pl.pallas_call(quantizer_kernel, in_specs=[smem] * 2 + [hbm] * 4 + [vmem]...  45.5 us
    all_to_all x1, blocking collectives, on_device(): lax.all_to_all(jnp.broadcast_to(piece[None], (16,) + PIECE), BOTH, 0, 0,...  13.3 us
    ppermute x1, starting transfers between devices, on_device(): theirs = lax.ppermute(mine, BOTH, SWAP)  11.5 us
    pallas_call x1, Pallas kernels, feature_grads(): pl.pallas_call(back_kernel, grid=(BLOCKS,), in_specs=[pl.BlockSpec(memory...  8.48 us
    ppermute x2, starting transfers between devices, edges(): below = lax.ppermute(first, 'tile', [((i + 1) % n, i) for i in range(n)])  6.61 us
    unnamed x18, local copies, waits for them, and re-layouts  5.33 us
    ppermute x2, starting transfers between devices, edges(): above = lax.ppermute(last, 'tile', [(i, (i + 1) % n) for i in range(n)])  5.24 us
    ppermute x3, starting transfers between devices, on_device(): lax.ppermute(weight_chip[d], BOTH, first_ring(d)).astype(F32)  5.04 us
  transfers between devices with their start and end apart: 18, of which 4 were waited for; matrix products, arithmetic and copies ran while one was open for 5% of the time, Pallas kernels for 12%

profile of v5, /device:TPU:1, one launch (start us, length us, event | category | flops | bytes accessed | tf_op | source)
XLA Modules:
  0.0 145.3 jit_solution(15835145771106216819)
XLA Ops:
  0.6 1.0 fusion.4
  1.6 4.5 %collective-permute-start = (bf16[2,1,128,256]{3,2,1,0:T(8,128)(2,1)S(1)}, bf16[2,1,128,256]{3,2,1,0:T(8,128)(2,1)S(1)}, u32[]{:S(2)}, u32[]{:S(2)}) collective-permute-start(bf16[2,1,128,256]{3,2,1,0:T(8,128)(2,1)S(1)} %get-tuple-element.42), channel_id=1, source_target_pairs={{0,1},{1,2},{2,3},{3,4},{4,5},{5,6},{6,7},{7,0},{8,9},{9,10},{10,1... | collective-permute-start | bytes 393224 | tf_op jit(solution)/shard_map/ppermute | solution.py:543
  6.1 2.3 %collective-permute-start.1 = (bf16[2,1,128,256]{3,2,1,0:T(8,128)(2,1)S(1)}, bf16[2,1,128,256]{3,2,1,0:T(8,128)(2,1)S(1)}, u32[]{:S(2)}, u32[]{:S(2)}) collective-permute-start(bf16[2,1,128,256]{3,2,1,0:T(8,128)(2,1)S(1)} %get-tuple-element.41), channel_id=1, source_target_pairs={{1,0},{2,1},{3,2},{4,3},{5,4},{6,5},{7,6},{0,7},{9,8},{10,9},{11,1... | collective-permute-start | bytes 393224 | tf_op jit(solution)/shard_map/ppermute | solution.py:544
  8.4 2.4 %shard_map.76 = (s32[128,128]{1,0:T(8,128)}, s32[8,128]{1,0:T(8,128)}) custom-call(s32[128,128]{1,0:T(8,128)} %bitcast.34), custom_call_target="tpu_custom_call" | custom-call | tf_op jit(solution)/shard_map/pallas_call | solution.py:135
  11.5 3.5 %collective-permute-done.1.below = bf16[2,1,128,256]{3,2,1,0:T(8,128)(2,1)S(1)} collective-permute-done((bf16[2,1,128,256]{3,2,1,0:T(8,128)(2,1)S(1)}, bf16[2,1,128,256]{3,2,1,0:T(8,128)(2,1)S(1)}, u32[]{:S(2)}, u32[]{:S(2)}) %collective-permute-start.1) | collective-permute-done | bytes 131104 | tf_op jit(solution)/shard_map/ppermute | solution.py:544
  15.7 45.5 %shard_map.77 = (bf16[4096,256]{1,0:T(8,128)(2,1)}, bf16[2,1,128,256]{3,2,1,0:T(8,128)(2,1)}, bf16[2,1,128,256]{3,2,1,0:T(8,128)(2,1)}, bf16[4,2048,256]{2,1,0:T...) custom-call(s32[8,128]{1,0:T(8,128)} %get-tuple-element.20.extra, ...), custom_call_target="tpu_custom_call" | custom-call | flops 9663676416 | bytes 67108864 | tf_op jit(solution)/shard_map/pallas_call | solution.py:375
  62.7 4.3 %collective-permute-start.8 = (bf16[2,1,128,256]{3,2,1,0:T(8,128)(2,1)}, bf16[2,1,128,256]{3,2,1,0:T(8,128)(2,1)S(1)}, u32[]{:S(2)}, u32[]{:S(2)}) collective-permute-start(bf16[2,1,128,256]{3,2,1,0:T(8,128)(2,1)} %get-tuple-element.27), channel_id=1, source_target_pairs={{1,0},{2,1},{3,2},{4,3},{5,4},{6,5},{7,6},{0,7},{9,8},{10,9},{11,1... | collective-permute-start | bytes 393224 | tf_op jit(solution)/shard_map/ppermute | solution.py:544
  67.0 2.9 %collective-permute-done.2 = bf16[4,16,16,384]{3,2,1,0:T(8,128)(2,1)S(1)} collective-permute-done((bf16[4,16,16,384]{3,2,1,0:T(8,128)(2,1)}, bf16[4,16,16,384]{3,2,1,0:T(8,128)(2,1)S(1)}, u32[]{:S(2)}, u32[]{:S(2)}) %collective-permute-start.2) | collective-permute-done | bytes 786464 | tf_op jit(solution)/shard_map/ppermute | solution.py:569
  70.0 1.3 add_convert_fusion.4
  71.4 1.3 collective-permute-start.3
  72.7 2.6 %collective-permute-start.4 = (bf16[16,16,384]{2,1,0:T(8,128)(2,1)S(1)}, bf16[16,16,384]{2,1,0:T(8,128)(2,1)S(1)}, u32[]{:S(2)}, u32[]{:S(2)}) collective-permute-start(bf16[16,16,384]{2,1,0:T(8,128)(2,1)S(1)} %get-tuple-element.45), channel_id=1, source_target_pairs={{0,4},{8,40},{64,68},{72,104},{1,5},{9,41},{65,69},{73,105},{16,20... | collective-permute-start | bytes 589832 | tf_op jit(solution)/shard_map/ppermute | solution.py:576
  75.4 1.1 collective-permute-start.5
  76.5 3.7 %add_convert_fusion = (bf16[1,2048,256]{2,1,0:T(8,128)(2,1)}, bf16[1,2048,256]{2,1,0:T(8,128)(2,1)}, bf16[1,2048,256]{2,1,0:T(8,128)(2,1)}, bf16[2048,256]{1,0:T(8,128)(2,1)S(1)}) fusion(bf16[4,2048,256]{2,1,0:T(8,128)(2,1)S(1)} %collective-permute-done.6, bf16[4,2048,256]{2,1,0:T(8,128)(2,1)} %get-tuple-element.35), kind=kLoop, calls=%fused_computation.1 | loop fusion | flops 8388608 | bytes 12582912 | tf_op jit(solution)/shard_map/convert_element_type | solution.py:578
  80.6 0.8 collective-permute-start.14
  81.4 1.7 %collective-permute-start.15 = (bf16[16,128,256]{2,1,0:T(8,128)(2,1)}, bf16[16,128,256]{2,1,0:T(8,128)(2,1)}, u32[]{:S(2)}, u32[]{:S(2)}) collective-permute-start(bf16[16,128,256]{2,1,0:T(8,128)(2,1)} %bitcast.20), channel_id=1, source_target_pairs={{0,6},{8,56},{64,70},{72,120},{1,7},{9,57},{65,71},{73,121},{16,22... | collective-permute-start | bytes 3145736 | tf_op jit(solution)/shard_map/ppermute | solution.py:581
  83.1 0.8 fusion.3
  83.8 4.9 %all-to-all-start = ((bf16[16,16,384]{2,1,0:T(8,128)(2,1)}), bf16[16,16,384]{2,1,0:T(8,128)(2,1)}, u32[]{:S(2)}, u32[]{:S(2)}) async-start(bf16[16,16,384]{2,1,0:T(8,128)(2,1)} %fusion.3), calls=%async_computation | async-start | bytes 393216 | tf_op jit(solution)/shard_map/all_to_all | solution.py:583
  88.7 1.3 copy-done.3
  90.0 1.6 %copy-done.4 = bf16[4096,256]{1,0:T(8,128)(2,1)S(1)} copy-done((bf16[4096,256]{1,0:T(8,128)(2,1)S(1)}, bf16[4096,256]{1,0:T(8,128)(2,1)}, u32[]{:S(2)}) %copy-start.4) | copy-done | bytes 2097176
  91.6 8.5 %shard_map.78 = bf16[4096,256]{1,0:T(8,128)(2,1)} custom-call(s32[6]{0:T(128)S(1)} %copy-done.1, bf16[2,16,128,256]{3,2,1,0:T(8,128)(2,1)S(1)} %bitcast.33, bf16[2,1,128,256]{3,2,1,0:T(8,128)(2,1)S(1)} %collective-permute-done.7.above, bf16[2,1,128,256]{3,2,1,0:T(8,128)(2,1)S(1)} %collective-permute-done.8.below, bf16[9,256,256]{2,1,0:T(8,128)(2,1)S(1)} %copy-done.3), custom_call_target="tpu_custom_call" | custom-call | flops 4831838208 | bytes 8388608 | tf_op jit(solution)/shard_map/pallas_call | solution.py:437
  100.1 1.0 reduce_sum.21
  101.1 13.3 %all_to_all.15.refs_0_ = bf16[16,16,384]{2,1,0:T(8,128)(2,1)S(1)} all-to-all(bf16[16,16,384]{2,1,0:T(8,128)(2,1)S(1)} %broadcast_in_dim.2), channel_id=1, replica_groups={{0,64,1,65,16,80,17,81,32,96,33,97,48,112,49,113},{2,66,3,67,18,82,19,8..., dimensions={0} | all-to-all | bytes 393216 | tf_op jit(solution)/shard_map/all_to_all | solution.py:587
  114.4 2.2 %collective-permute-start.10 = (bf16[16,16,384]{2,1,0:T(8,128)(2,1)S(1)}, bf16[16,16,384]{2,1,0:T(8,128)(2,1)S(1)}, u32[]{:S(2)}, u32[]{:S(2)}) collective-permute-start(bf16[16,16,384]{2,1,0:T(8,128)(2,1)S(1)} %all_to_all.15.refs_0_), channel_id=1, source_target_pairs={{0,4},{8,40},{64,68},{72,104},{1,5},{9,41},{65,69},{73,105},{16,20... | collective-permute-start | bytes 589832 | tf_op jit(solution)/shard_map/ppermute | solution.py:592
  117.2 0.9 collective-permute-start.9
  118.1 2.7 %shard_map.81 = bf16[2048,256]{1,0:T(8,128)(2,1)} custom-call(bf16[2048,256]{1,0:T(8,128)(2,1)S(1)} %get-tuple-element.40.refs_0_, bf16[2048,256]{1,0:T(8,128)(2,1)S(1)} %bitcast.31, bf16[2048,256]{1,0:T(8,128)(2,1)S(1)} %bitcast.32, bf16[2048,256]{1,0:T(8,128)(2,1)} %bitcast.21.refs_3_), custom_call_target="tpu_custom_call" | custom-call | flops 1048576 | bytes 4194304 | tf_op jit(solution)/shard_map/pallas_call | solution.py:480
  120.8 3.8 %all-to-all-start.2 = ((bf16[16,128,256]{2,1,0:T(8,128)(2,1)}), bf16[16,128,256]{2,1,0:T(8,128)(2,1)S(1)}, u32[]{:S(2)}, u32[]{:S(2)}) async-start(bf16[16,128,256]{2,1,0:T(8,128)(2,1)} %bitcast.22), calls=%async_computation.2 | async-start | bytes 2097152 | tf_op jit(solution)/shard_map/all_to_all | solution.py:591
  125.3 2.2 %shard_map.79.mine = bf16[4,16,16,384]{3,2,1,0:T(8,128)(2,1)} custom-call(s32[6]{0:T(128)} %stack.23.info, bf16[16,16,384]{2,1,0:T(8,128)(2,1)} %copy-done.5, bf16[16,16,384]{2,1,0:T(8,128)(2,1)} %collective-permute-done.9.refs_1_, bf16[16,16,384]{2,1,0:T(8,128)(2,1)} %copy-done.6, bf16[16,16,384]{2,1,0:T(8,128)(2,1)} %collective-permute-done.11.refs_3_), custom_call_target="tpu_custom_call" | custom-call | tf_op jit(solution)/shard_map/pallas_call | solution.py:498
  127.5 11.5 %collective-permute-start.12 = (bf16[4,16,16,384]{3,2,1,0:T(8,128)(2,1)}, bf16[4,16,16,384]{3,2,1,0:T(8,128)(2,1)S(1)}, u32[]{:S(2)}, u32[]{:S(2)}) collective-permute-start(bf16[4,16,16,384]{3,2,1,0:T(8,128)(2,1)} %shard_map.79.mine), channel_id=1, source_target_pairs={{0,8},{8,0},{64,72},{72,64},{1,9},{9,1},{65,73},{73,65},{16,24},{2... | collective-permute-start | bytes 2359304 | tf_op jit(solution)/shard_map/ppermute | solution.py:594
  139.0 2.1 %collective-permute-done.12.theirs = bf16[4,16,16,384]{3,2,1,0:T(8,128)(2,1)S(1)} collective-permute-done((bf16[4,16,16,384]{3,2,1,0:T(8,128)(2,1)}, bf16[4,16,16,384]{3,2,1,0:T(8,128)(2,1)S(1)}, u32[]{:S(2)}, u32[]{:S(2)}) %collective-permute-start.12) | collective-permute-done | bytes 786464 | tf_op jit(solution)/shard_map/ppermute | solution.py:594
  141.1 1.1 copy-done
  142.3 2.2 %shard_map.80 = f32[9,256,256]{2,1,0:T(8,128)} custom-call(s32[6]{0:T(128)S(1)} %copy-done.2, bf16[4,16,16,384]{3,2,1,0:T(8,128)(2,1)S(1)} %copy-done, bf16[4,16,16,384]{3,2,1,0:T(8,128)(2,1)S(1)} %collective-permute-done.12.theirs), custom_call_target="tpu_custom_call" | custom-call | tf_op jit(solution)/shard_map/pallas_call | solution.py:533
  144.5 0.8 convert_reduce_fusion
  (38 shorter events, 4.6 us)
Async XLA Ops:
  1.6 9.9 %collective-permute-start = (bf16[2,1,128,256]{3,2,1,0:T(8,128)(2,1)S(1)}, bf16[2,1,128,256]{3,2,1,0:T(8,128)(2,1)S(1)}, u32[]{:S(2)}, u32[]{:S(2)}) collective-permute-start(bf16[2,1,128,256]{3,2,1,0:T(8,128)(2,1)S(1)} %get-tuple-element.42), channel_id=1, source_target_pairs={{0,1},{1,2},{2,3},{3,4},{4,5},{5,6},{6,7},{7,0},{8,9},{9,10},{10,1... | collective-permute-start | bytes 393224 | tf_op jit(solution)/shard_map/ppermute | solution.py:543
  6.1 9.0 %collective-permute-start.1 = (bf16[2,1,128,256]{3,2,1,0:T(8,128)(2,1)S(1)}, bf16[2,1,128,256]{3,2,1,0:T(8,128)(2,1)S(1)}, u32[]{:S(2)}, u32[]{:S(2)}) collective-permute-start(bf16[2,1,128,256]{3,2,1,0:T(8,128)(2,1)S(1)} %get-tuple-element.41), channel_id=1, source_target_pairs={{1,0},{2,1},{3,2},{4,3},{5,4},{6,5},{7,6},{0,7},{9,8},{10,9},{11,1... | collective-permute-start | bytes 393224 | tf_op jit(solution)/shard_map/ppermute | solution.py:544
  11.5 3.5 %copy-start.7 = (bf16[2,1,128,256]{3,2,1,0:T(8,128)(2,1)}, bf16[2,1,128,256]{3,2,1,0:T(8,128)(2,1)S(1)}, u32[]{:S(2)}) copy-start(bf16[2,1,128,256]{3,2,1,0:T(8,128)(2,1)S(1)} %collective-permute-done.above) | copy-start | bytes 393220
  15.1 0.7 copy-start.8
  61.3 15.2 %collective-permute-start.6 = (bf16[4,2048,256]{2,1,0:T(8,128)(2,1)}, bf16[4,2048,256]{2,1,0:T(8,128)(2,1)S(1)}, u32[]{:S(2)}, u32[]{:S(2)}) collective-permute-start(bf16[4,2048,256]{2,1,0:T(8,128)(2,1)} %get-tuple-element.25), channel_id=1, source_target_pairs={{0,8},{8,0},{64,72},{72,64},{1,9},{9,1},{65,73},{73,65},{16,24},{2... | collective-permute-start | bytes 12582920 | tf_op jit(solution)/shard_map/ppermute | solution.py:566
  61.9 8.1 %collective-permute-start.2 = (bf16[4,16,16,384]{3,2,1,0:T(8,128)(2,1)}, bf16[4,16,16,384]{3,2,1,0:T(8,128)(2,1)S(1)}, u32[]{:S(2)}, u32[]{:S(2)}) collective-permute-start(bf16[4,16,16,384]{3,2,1,0:T(8,128)(2,1)} %get-tuple-element.23), channel_id=1, source_target_pairs={{0,8},{8,0},{64,72},{72,64},{1,9},{9,1},{65,73},{73,65},{16,24},{2... | collective-permute-start | bytes 2359304 | tf_op jit(solution)/shard_map/ppermute | solution.py:569
  62.0 13.4 %collective-permute-start.7 = (bf16[2,1,128,256]{3,2,1,0:T(8,128)(2,1)}, bf16[2,1,128,256]{3,2,1,0:T(8,128)(2,1)S(1)}, u32[]{:S(2)}, u32[]{:S(2)}) collective-permute-start(bf16[2,1,128,256]{3,2,1,0:T(8,128)(2,1)} %get-tuple-element.26), channel_id=1, source_target_pairs={{0,1},{1,2},{2,3},{3,4},{4,5},{5,6},{6,7},{7,0},{8,9},{9,10},{10,1... | collective-permute-start | bytes 393224 | tf_op jit(solution)/shard_map/ppermute | solution.py:543
  62.7 13.7 %collective-permute-start.8 = (bf16[2,1,128,256]{3,2,1,0:T(8,128)(2,1)}, bf16[2,1,128,256]{3,2,1,0:T(8,128)(2,1)S(1)}, u32[]{:S(2)}, u32[]{:S(2)}) collective-permute-start(bf16[2,1,128,256]{3,2,1,0:T(8,128)(2,1)} %get-tuple-element.27), channel_id=1, source_target_pairs={{1,0},{2,1},{3,2},{4,3},{5,4},{6,5},{7,6},{0,7},{9,8},{10,9},{11,1... | collective-permute-start | bytes 393224 | tf_op jit(solution)/shard_map/ppermute | solution.py:544
  71.4 10.0 %collective-permute-start.3 = (bf16[16,16,384]{2,1,0:T(8,128)(2,1)S(1)}, bf16[16,16,384]{2,1,0:T(8,128)(2,1)S(1)}, u32[]{:S(2)}, u32[]{:S(2)}) collective-permute-start(bf16[16,16,384]{2,1,0:T(8,128)(2,1)S(1)} %get-tuple-element.43), channel_id=1, source_target_pairs={{0,2},{8,24},{64,66},{72,88},{1,3},{9,25},{65,67},{73,89},{16,18},... | collective-permute-start | bytes 589832 | tf_op jit(solution)/shard_map/ppermute | solution.py:576
  72.7 10.3 %collective-permute-start.4 = (bf16[16,16,384]{2,1,0:T(8,128)(2,1)S(1)}, bf16[16,16,384]{2,1,0:T(8,128)(2,1)S(1)}, u32[]{:S(2)}, u32[]{:S(2)}) collective-permute-start(bf16[16,16,384]{2,1,0:T(8,128)(2,1)S(1)} %get-tuple-element.45), channel_id=1, source_target_pairs={{0,4},{8,40},{64,68},{72,104},{1,5},{9,41},{65,69},{73,105},{16,20... | collective-permute-start | bytes 589832 | tf_op jit(solution)/shard_map/ppermute | solution.py:576
  75.4 7.7 %collective-permute-start.5 = (bf16[16,16,384]{2,1,0:T(8,128)(2,1)S(1)}, bf16[16,16,384]{2,1,0:T(8,128)(2,1)S(1)}, u32[]{:S(2)}, u32[]{:S(2)}) collective-permute-start(bf16[16,16,384]{2,1,0:T(8,128)(2,1)S(1)} %get-tuple-element.44), channel_id=1, source_target_pairs={{0,6},{8,56},{64,70},{72,120},{1,7},{9,57},{65,71},{73,121},{16,22... | collective-permute-start | bytes 589832 | tf_op jit(solution)/shard_map/ppermute | solution.py:576
  76.4 12.3 %copy-start.1 = (s32[6]{0:T(128)S(1)}, s32[6]{0:T(128)}, u32[]{:S(2)}) copy-start(s32[6]{0:T(128)} %stack.23.info) | copy-start | bytes 76
  80.2 37.0 %collective-permute-start.13 = (bf16[16,128,256]{2,1,0:T(8,128)(2,1)}, bf16[16,128,256]{2,1,0:T(8,128)(2,1)S(1)}, u32[]{:S(2)}, u32[]{:S(2)}) collective-permute-start(bf16[16,128,256]{2,1,0:T(8,128)(2,1)} %bitcast.16), channel_id=1, source_target_pairs={{0,2},{8,24},{64,66},{72,88},{1,3},{9,25},{65,67},{73,89},{16,18},... | collective-permute-start | bytes 3145736 | tf_op jit(solution)/shard_map/ppermute | solution.py:581
  80.6 37.5 %collective-permute-start.14 = (bf16[16,128,256]{2,1,0:T(8,128)(2,1)}, bf16[16,128,256]{2,1,0:T(8,128)(2,1)S(1)}, u32[]{:S(2)}, u32[]{:S(2)}) collective-permute-start(bf16[16,128,256]{2,1,0:T(8,128)(2,1)} %bitcast.18), channel_id=1, source_target_pairs={{0,4},{8,40},{64,68},{72,104},{1,5},{9,41},{65,69},{73,105},{16,20... | collective-permute-start | bytes 3145736 | tf_op jit(solution)/shard_map/ppermute | solution.py:581
  81.4 36.7 %collective-permute-start.15 = (bf16[16,128,256]{2,1,0:T(8,128)(2,1)}, bf16[16,128,256]{2,1,0:T(8,128)(2,1)}, u32[]{:S(2)}, u32[]{:S(2)}) collective-permute-start(bf16[16,128,256]{2,1,0:T(8,128)(2,1)} %bitcast.20), channel_id=1, source_target_pairs={{0,6},{8,56},{64,70},{72,120},{1,7},{9,57},{65,71},{73,121},{16,22... | collective-permute-start | bytes 3145736 | tf_op jit(solution)/shard_map/ppermute | solution.py:581
  83.8 16.2 %all-to-all-start = ((bf16[16,16,384]{2,1,0:T(8,128)(2,1)}), bf16[16,16,384]{2,1,0:T(8,128)(2,1)}, u32[]{:S(2)}, u32[]{:S(2)}) async-start(bf16[16,16,384]{2,1,0:T(8,128)(2,1)} %fusion.3), calls=%async_computation | async-start | bytes 393216 | tf_op jit(solution)/shard_map/all_to_all | solution.py:583
  88.7 1.3 copy-start.3
  90.0 1.6 %copy-start.4 = (bf16[4096,256]{1,0:T(8,128)(2,1)S(1)}, bf16[4096,256]{1,0:T(8,128)(2,1)}, u32[]{:S(2)}) copy-start(bf16[4096,256]{1,0:T(8,128)(2,1)} %get-tuple-element.30) | copy-start | bytes 6291460
  114.4 6.4 %copy-start.5 = (bf16[16,16,384]{2,1,0:T(8,128)(2,1)}, bf16[16,16,384]{2,1,0:T(8,128)(2,1)S(1)}, u32[]{:S(2)}) copy-start(bf16[16,16,384]{2,1,0:T(8,128)(2,1)S(1)} %all_to_all.15.refs_0_) | copy-start | bytes 589828
  114.4 10.2 %collective-permute-start.10 = (bf16[16,16,384]{2,1,0:T(8,128)(2,1)S(1)}, bf16[16,16,384]{2,1,0:T(8,128)(2,1)S(1)}, u32[]{:S(2)}, u32[]{:S(2)}) collective-permute-start(bf16[16,16,384]{2,1,0:T(8,128)(2,1)S(1)} %all_to_all.15.refs_0_), channel_id=1, source_target_pairs={{0,4},{8,40},{64,68},{72,104},{1,5},{9,41},{65,69},{73,105},{16,20... | collective-permute-start | bytes 589832 | tf_op jit(solution)/shard_map/ppermute | solution.py:592
  116.6 8.0 %collective-permute-start.11 = (bf16[16,16,384]{2,1,0:T(8,128)(2,1)S(1)}, bf16[16,16,384]{2,1,0:T(8,128)(2,1)}, u32[]{:S(2)}, u32[]{:S(2)}) collective-permute-start(bf16[16,16,384]{2,1,0:T(8,128)(2,1)S(1)} %all_to_all.15.refs_0_), channel_id=1, source_target_pairs={{0,6},{8,56},{64,70},{72,120},{1,7},{9,57},{65,71},{73,121},{16,22... | collective-permute-start | bytes 589832 | tf_op jit(solution)/shard_map/ppermute | solution.py:592
  117.2 7.4 %collective-permute-start.9 = (bf16[16,16,384]{2,1,0:T(8,128)(2,1)S(1)}, bf16[16,16,384]{2,1,0:T(8,128)(2,1)}, u32[]{:S(2)}, u32[]{:S(2)}) collective-permute-start(bf16[16,16,384]{2,1,0:T(8,128)(2,1)S(1)} %all_to_all.15.refs_0_), channel_id=1, source_target_pairs={{0,2},{8,24},{64,66},{72,88},{1,3},{9,25},{65,67},{73,89},{16,18},... | collective-permute-start | bytes 589832 | tf_op jit(solution)/shard_map/ppermute | solution.py:592
  120.8 20.3 %copy-start.2 = (s32[6]{0:T(128)S(1)}, s32[6]{0:T(128)}, u32[]{:S(2)}) copy-start(s32[6]{0:T(128)} %stack.23.info) | copy-start | bytes 76
  120.8 23.7 %all-to-all-start.2 = ((bf16[16,128,256]{2,1,0:T(8,128)(2,1)}), bf16[16,128,256]{2,1,0:T(8,128)(2,1)S(1)}, u32[]{:S(2)}, u32[]{:S(2)}) async-start(bf16[16,128,256]{2,1,0:T(8,128)(2,1)} %bitcast.22), calls=%async_computation.2 | async-start | bytes 2097152 | tf_op jit(solution)/shard_map/all_to_all | solution.py:591
  124.6 0.7 copy-start.6
  127.5 13.6 %collective-permute-start.12 = (bf16[4,16,16,384]{3,2,1,0:T(8,128)(2,1)}, bf16[4,16,16,384]{3,2,1,0:T(8,128)(2,1)S(1)}, u32[]{:S(2)}, u32[]{:S(2)}) collective-permute-start(bf16[4,16,16,384]{3,2,1,0:T(8,128)(2,1)} %shard_map.79.mine), channel_id=1, source_target_pairs={{0,8},{8,0},{64,72},{72,64},{1,9},{9,1},{65,73},{73,65},{16,24},{2... | collective-permute-start | bytes 2359304 | tf_op jit(solution)/shard_map/ppermute | solution.py:594
  141.1 1.1 copy-start

commit v6 on v5

--- a/solution.py
+++ b/solution.py
@@ -120,7 +120,7 @@
         parts[pl.ds(s, 1), :] = jnp.sum(
             jnp.where(rank == s, 2 * entries, 0), axis=0, keepdims=True
         )
-    codes_of = jnp.sum(parts[...].astype(F32), axis=1, keepdims=True)
+    codes_of = jnp.sum(parts[pl.ds(0, SPILL), :].astype(F32), axis=1, keepdims=True)
     square = lax.broadcasted_iota(jnp.int32, (SPILL, 128), 0) == lax.broadcasted_iota(
         jnp.int32, (SPILL, 128), 1
     )
@@ -138,7 +138,7 @@
             jax.ShapeDtypeStruct((128, 128), ints),
             jax.ShapeDtypeStruct((8, 128), ints),
         ],
-        scratch_shapes=[pltpu.VMEM((SPILL, 128), ints)],
+        scratch_shapes=[pltpu.VMEM((SPILL + 8, 128), ints)],
     )(codes.reshape(128, 128))
 
 
@@ -377,9 +377,9 @@
         in_specs=[smem] * 2 + [hbm] * 4 + [vmem] * 2 + [hbm] * 2,
         out_specs=[hbm] * 7,
         scratch_shapes=[
-            pltpu.VMEM((2 * (CODES + SPILL), 128), F32),
-            pltpu.VMEM((2 * (CODES + SPILL), 128), F32),
-            pltpu.VMEM((2 * SPOTS, 128), F32),
+            pltpu.VMEM((2 * (CODES + SPILL) + 8, 128), F32),
+            pltpu.VMEM((2 * (CODES + SPILL) + 8, 128), F32),
+            pltpu.VMEM((2 * SPOTS + 8, 128), F32),
             pltpu.VMEM((CODES, CHANS), BF16),
             pltpu.VMEM((SPOTS, CHANS), BF16),
             pltpu.VMEM((9, CHANS, CHANS), BF16),
@@ -588,6 +588,7 @@
         jnp.broadcast_to(piece[None], (16,) + PIECE), BOTH, 0, 0, axis_index_groups=PLANES
     )
     ring = added(chip[0], *others)
+    pieces, ring = lax.optimization_barrier((pieces, ring))
     plane = lax.all_to_all(ring, BOTH, 0, 0, axis_index_groups=PLANES)
     around = [lax.ppermute(pieces, BOTH, first_ring(d)) for d in (1, 2, 3)]
     mine = turned(info, pieces, around)

time: 146 us -> 144 us (0.986)
  waiting for transfers between devices: 8.76 us -> 22.2 us
  blocking collectives: 13.3 us -> 0 us
  starting transfers between devices: 44.2 us -> 41.6 us
    all_to_all x1 -> x0, blocking collectives: 13.3 us -> none  [on_device(): lax.all_to_all(jnp.broadcast_to(piece[None], (16,) + PIECE), BOTH, 0, 0,...]
    ppermute x3, waiting for transfers between devices: 0.01 us -> 9.4 us  [on_device(): around = [lax.ppermute(pieces, BOTH, first_ring(d)) for d in (1, 2, 3)]]
    ppermute x1, starting transfers between devices: 11.5 us -> 2.33 us  [on_device(): theirs = lax.ppermute(mine, BOTH, SWAP)]
    all_to_all x0 -> x1, starting transfers between devices: none -> 6.54 us  [on_device(): lax.all_to_all(jnp.broadcast_to(piece[None], (16,) + PIECE), BOTH, 0, 0,...]
    ppermute x2, starting transfers between devices: 5.24 us -> 0.01 us  [edges(): above = lax.ppermute(last, 'tile', [(i, (i + 1) % n) for i in range(n)])]
    ppermute x2, starting transfers between devices: 6.61 us -> 11.8 us  [edges(): below = lax.ppermute(first, 'tile', [((i + 1) % n, i) for i in range(n)])]
    ppermute x2, waiting for transfers between devices: 0.11 us -> 4.36 us  [edges(): above = lax.ppermute(last, 'tile', [(i, (i + 1) % n) for i in range(n)])]
    all_to_all x0 -> x1, waiting for transfers between devices: none -> 3.92 us  [on_device(): lax.all_to_all(jnp.broadcast_to(piece[None], (16,) + PIECE), BOTH, 0, 0,...]
  transfers between devices with their start and end apart: 18 -> 19, of which waited for: 4 -> 7; matrix products, arithmetic and copies ran while one was open for 5% -> 6% of each run, Pallas kernels for 12% -> 11%
where the time goes in v6:
time: 144 us
  Pallas kernels  63.7 us (44%)
  starting transfers between devices  41.6 us (29%)
  waiting for transfers between devices  22.2 us (15%)
  local copies, waits for them, and re-layouts  7.75 us (5%)
  other arithmetic  7.58 us (5%)
    pallas_call x1, Pallas kernels, quantizer(): pl.pallas_call(quantizer_kernel, in_specs=[smem] * 2 + [hbm] * 4 + [vmem]...  45.7 us
    ppermute x2, starting transfers between devices, edges(): below = lax.ppermute(first, 'tile', [((i + 1) % n, i) for i in range(n)])  11.8 us
    ppermute x3, waiting for transfers between devices, on_device(): around = [lax.ppermute(pieces, BOTH, first_ring(d)) for d in (1, 2, 3)]  9.4 us
    pallas_call x1, Pallas kernels, feature_grads(): pl.pallas_call(back_kernel, grid=(BLOCKS,), in_specs=[pl.BlockSpec(memory...  8.48 us
    all_to_all x1, starting transfers between devices, on_device(): lax.all_to_all(jnp.broadcast_to(piece[None], (16,) + PIECE), BOTH, 0, 0,...  6.54 us
    unnamed x22, local copies, waits for them, and re-layouts  5.32 us
    ppermute x3, starting transfers between devices, on_device(): lax.ppermute(weight_chip[d], BOTH, first_ring(d)).astype(F32)  4.43 us
    ppermute x2, waiting for transfers between devices, edges(): above = lax.ppermute(last, 'tile', [(i, (i + 1) % n) for i in range(n)])  4.36 us
  transfers between devices with their start and end apart: 19, of which 7 were waited for; matrix products, arithmetic and copies ran while one was open for 6% of the time, Pallas kernels for 11%

profile of v6, /device:TPU:1, one launch (start us, length us, event | category | flops | bytes accessed | tf_op | source)
XLA Modules:
  0.0 143.6 jit_solution(5411523082849326768)
XLA Ops:
  0.6 1.0 fusion.4
  1.6 6.7 %collective-permute-start.1 = (bf16[2,1,128,256]{3,2,1,0:T(8,128)(2,1)S(1)}, bf16[2,1,128,256]{3,2,1,0:T(8,128)(2,1)S(1)}, u32[]{:S(2)}, u32[]{:S(2)}) collective-permute-start(bf16[2,1,128,256]{3,2,1,0:T(8,128)(2,1)S(1)} %get-tuple-element.45), channel_id=1, source_target_pairs={{1,0},{2,1},{3,2},{4,3},{5,4},{6,5},{7,6},{0,7},{9,8},{10,9},{11,1... | collective-permute-start | bytes 393224 | tf_op jit(solution)/shard_map/ppermute | solution.py:544
  8.3 2.4 %shard_map.76 = (s32[128,128]{1,0:T(8,128)}, s32[8,128]{1,0:T(8,128)}) custom-call(s32[128,128]{1,0:T(8,128)} %bitcast.34), custom_call_target="tpu_custom_call" | custom-call | tf_op jit(solution)/shard_map/pallas_call | solution.py:135
  11.4 4.4 %collective-permute-done.above = bf16[2,1,128,256]{3,2,1,0:T(8,128)(2,1)S(1)} collective-permute-done((bf16[2,1,128,256]{3,2,1,0:T(8,128)(2,1)S(1)}, bf16[2,1,128,256]{3,2,1,0:T(8,128)(2,1)S(1)}, u32[]{:S(2)}, u32[]{:S(2)}) %collective-permute-start) | collective-permute-done | bytes 131104 | tf_op jit(solution)/shard_map/ppermute | solution.py:543
  16.4 45.7 %shard_map.77 = (bf16[4096,256]{1,0:T(8,128)(2,1)}, bf16[2,1,128,256]{3,2,1,0:T(8,128)(2,1)}, bf16[2,1,128,256]{3,2,1,0:T(8,128)(2,1)}, bf16[4,2048,256]{2,1,0:T...) custom-call(s32[8,128]{1,0:T(8,128)} %get-tuple-element.22.extra, ...), custom_call_target="tpu_custom_call" | custom-call | flops 9663676416 | bytes 67108864 | tf_op jit(solution)/shard_map/pallas_call | solution.py:375
  62.1 2.1 %collective-permute-start.6 = (bf16[4,2048,256]{2,1,0:T(8,128)(2,1)}, bf16[4,2048,256]{2,1,0:T(8,128)(2,1)S(1)}, u32[]{:S(2)}, u32[]{:S(2)}) collective-permute-start(bf16[4,2048,256]{2,1,0:T(8,128)(2,1)} %get-tuple-element.27), channel_id=1, source_target_pairs={{0,8},{8,0},{64,72},{72,64},{1,9},{9,1},{65,73},{73,65},{16,24},{2... | collective-permute-start | bytes 12582920 | tf_op jit(solution)/shard_map/ppermute | solution.py:566
  64.3 5.1 %collective-permute-start.8 = (bf16[2,1,128,256]{3,2,1,0:T(8,128)(2,1)}, bf16[2,1,128,256]{3,2,1,0:T(8,128)(2,1)S(1)}, u32[]{:S(2)}, u32[]{:S(2)}) collective-permute-start(bf16[2,1,128,256]{3,2,1,0:T(8,128)(2,1)} %get-tuple-element.29), channel_id=1, source_target_pairs={{1,0},{2,1},{3,2},{4,3},{5,4},{6,5},{7,6},{0,7},{9,8},{10,9},{11,1... | collective-permute-start | bytes 393224 | tf_op jit(solution)/shard_map/ppermute | solution.py:544
  69.4 2.9 %collective-permute-done.2 = bf16[4,16,16,384]{3,2,1,0:T(8,128)(2,1)S(1)} collective-permute-done((bf16[4,16,16,384]{3,2,1,0:T(8,128)(2,1)}, bf16[4,16,16,384]{3,2,1,0:T(8,128)(2,1)S(1)}, u32[]{:S(2)}, u32[]{:S(2)}) %collective-permute-start.2) | collective-permute-done | bytes 786464 | tf_op jit(solution)/shard_map/ppermute | solution.py:569
  72.3 1.3 add_convert_fusion.4
  73.7 1.4 collective-permute-start.3
  75.1 1.5 %collective-permute-start.5 = (bf16[16,16,384]{2,1,0:T(8,128)(2,1)S(1)}, bf16[16,16,384]{2,1,0:T(8,128)(2,1)S(1)}, u32[]{:S(2)}, u32[]{:S(2)}) collective-permute-start(bf16[16,16,384]{2,1,0:T(8,128)(2,1)S(1)} %get-tuple-element.48), channel_id=1, source_target_pairs={{0,6},{8,56},{64,70},{72,120},{1,7},{9,57},{65,71},{73,121},{16,22... | collective-permute-start | bytes 589832 | tf_op jit(solution)/shard_map/ppermute | solution.py:576
  76.6 1.5 %collective-permute-start.4 = (bf16[16,16,384]{2,1,0:T(8,128)(2,1)S(1)}, bf16[16,16,384]{2,1,0:T(8,128)(2,1)S(1)}, u32[]{:S(2)}, u32[]{:S(2)}) collective-permute-start(bf16[16,16,384]{2,1,0:T(8,128)(2,1)S(1)} %get-tuple-element.49), channel_id=1, source_target_pairs={{0,4},{8,40},{64,68},{72,104},{1,5},{9,41},{65,69},{73,105},{16,20... | collective-permute-start | bytes 589832 | tf_op jit(solution)/shard_map/ppermute | solution.py:576
  78.2 3.7 %add_convert_fusion = (bf16[1,2048,256]{2,1,0:T(8,128)(2,1)}, bf16[1,2048,256]{2,1,0:T(8,128)(2,1)}, bf16[1,2048,256]{2,1,0:T(8,128)(2,1)}, bf16[2048,256]{1,0:T(8,128)(2,1)S(1)}) fusion(bf16[4,2048,256]{2,1,0:T(8,128)(2,1)S(1)} %collective-permute-done.6, bf16[4,2048,256]{2,1,0:T(8,128)(2,1)} %get-tuple-element.37), kind=kLoop, calls=%fused_computation.1 | loop fusion | flops 8388608 | bytes 12582912 | tf_op jit(solution)/shard_map/convert_element_type | solution.py:578
  81.9 1.5 %collective-permute-start.10 = (bf16[16,128,256]{2,1,0:T(8,128)(2,1)}, bf16[16,128,256]{2,1,0:T(8,128)(2,1)S(1)}, u32[]{:S(2)}, u32[]{:S(2)}) collective-permute-start(bf16[16,128,256]{2,1,0:T(8,128)(2,1)} %bitcast.18), channel_id=1, source_target_pairs={{0,4},{8,40},{64,68},{72,104},{1,5},{9,41},{65,69},{73,105},{16,20... | collective-permute-start | bytes 3145736 | tf_op jit(solution)/shard_map/ppermute | solution.py:581
  83.3 1.4 collective-permute-start.11
  85.6 4.2 %all-to-all-start = ((bf16[16,16,384]{2,1,0:T(8,128)(2,1)}), bf16[16,16,384]{2,1,0:T(8,128)(2,1)}, u32[]{:S(2)}, u32[]{:S(2)}) async-start(bf16[16,16,384]{2,1,0:T(8,128)(2,1)} %fusion.3), calls=%async_computation | async-start | bytes 393216 | tf_op jit(solution)/shard_map/all_to_all | solution.py:583
  89.8 1.3 copy-done.3
  91.1 1.6 %copy-done.4 = bf16[4096,256]{1,0:T(8,128)(2,1)S(1)} copy-done((bf16[4096,256]{1,0:T(8,128)(2,1)S(1)}, bf16[4096,256]{1,0:T(8,128)(2,1)}, u32[]{:S(2)}) %copy-start.4) | copy-done | bytes 2097176
  92.7 8.5 %shard_map.78 = bf16[4096,256]{1,0:T(8,128)(2,1)} custom-call(s32[6]{0:T(128)S(1)} %copy-done.1, bf16[2,16,128,256]{3,2,1,0:T(8,128)(2,1)S(1)} %bitcast.33, bf16[2,1,128,256]{3,2,1,0:T(8,128)(2,1)S(1)} %collective-permute-done.7.above, bf16[2,1,128,256]{3,2,1,0:T(8,128)(2,1)S(1)} %collective-permute-done.8.below, bf16[9,256,256]{2,1,0:T(8,128)(2,1)S(1)} %copy-done.3), custom_call_target="tpu_custom_call" | custom-call | flops 4831838208 | bytes 8388608 | tf_op jit(solution)/shard_map/pallas_call | solution.py:437
  101.2 1.0 reduce_sum.21
  102.8 6.5 %all-to-all-start.1 = ((bf16[16,16,384]{2,1,0:T(8,128)(2,1)}), bf16[16,16,384]{2,1,0:T(8,128)(2,1)S(1)}, u32[]{:S(2)}, u32[]{:S(2)}) async-start(bf16[16,16,384]{2,1,0:T(8,128)(2,1)} %broadcast_in_dim.2), calls=%async_computation.1 | async-start | bytes 393216 | tf_op jit(solution)/shard_map/all_to_all | solution.py:587
  109.6 2.7 %shard_map.79 = bf16[2048,256]{1,0:T(8,128)(2,1)} custom-call(bf16[2048,256]{1,0:T(8,128)(2,1)S(1)} %get-tuple-element.44.refs_0_, bf16[2048,256]{1,0:T(8,128)(2,1)} %bitcast.17.refs_1_, bf16[2048,256]{1,0:T(8,128)(2,1)S(1)} %bitcast.31, bf16[2048,256]{1,0:T(8,128)(2,1)S(1)} %bitcast.32), custom_call_target="tpu_custom_call" | custom-call | flops 1048576 | bytes 4194304 | tf_op jit(solution)/shard_map/pallas_call | solution.py:480
  112.4 3.9 %all-to-all-done.1.refs_0_ = bf16[16,16,384]{2,1,0:T(8,128)(2,1)S(1)} async-done(((bf16[16,16,384]{2,1,0:T(8,128)(2,1)}), bf16[16,16,384]{2,1,0:T(8,128)(2,1)S(1)}, u32[]{:S(2)}, u32[]{:S(2)}) %all-to-all-start.1) | async-done | bytes 196640 | tf_op jit(solution)/shard_map/all_to_all | solution.py:587
  116.3 3.9 %all-to-all-start.2 = ((bf16[16,128,256]{2,1,0:T(8,128)(2,1)}), bf16[16,128,256]{2,1,0:T(8,128)(2,1)S(1)}, u32[]{:S(2)}, u32[]{:S(2)}) async-start(bf16[16,128,256]{2,1,0:T(8,128)(2,1)} %bitcast.22), calls=%async_computation.2 | async-start | bytes 2097152 | tf_op jit(solution)/shard_map/all_to_all | solution.py:592
  120.2 2.7 %collective-permute-start.14 = (bf16[16,16,384]{2,1,0:T(8,128)(2,1)S(1)}, bf16[16,16,384]{2,1,0:T(8,128)(2,1)S(1)}, u32[]{:S(2)}, u32[]{:S(2)}) collective-permute-start(bf16[16,16,384]{2,1,0:T(8,128)(2,1)S(1)} %all-to-all-done.1.refs_0_), channel_id=1, source_target_pairs={{0,6},{8,56},{64,70},{72,120},{1,7},{9,57},{65,71},{73,121},{16,22... | collective-permute-start | bytes 589832 | tf_op jit(solution)/shard_map/ppermute | solution.py:593
  123.5 8.0 %collective-permute-done.14.refs_3_ = bf16[16,16,384]{2,1,0:T(8,128)(2,1)S(1)} collective-permute-done((bf16[16,16,384]{2,1,0:T(8,128)(2,1)S(1)}, bf16[16,16,384]{2,1,0:T(8,128)(2,1)S(1)}, u32[]{:S(2)}, u32[]{:S(2)}) %collective-permute-start.14) | collective-permute-done | bytes 196640 | tf_op jit(solution)/shard_map/ppermute | solution.py:593
  131.5 1.4 %collective-permute-done.12.refs_1_ = bf16[16,16,384]{2,1,0:T(8,128)(2,1)S(1)} collective-permute-done((bf16[16,16,384]{2,1,0:T(8,128)(2,1)S(1)}, bf16[16,16,384]{2,1,0:T(8,128)(2,1)S(1)}, u32[]{:S(2)}, u32[]{:S(2)}) %collective-permute-start.12) | collective-permute-done | bytes 196640 | tf_op jit(solution)/shard_map/ppermute | solution.py:593
  133.6 2.2 %shard_map.80.mine = bf16[4,16,16,384]{3,2,1,0:T(8,128)(2,1)} custom-call(s32[6]{0:T(128)} %stack.23.info, bf16[16,16,384]{2,1,0:T(8,128)(2,1)} %copy-done.5, bf16[16,16,384]{2,1,0:T(8,128)(2,1)} %copy-done.8, bf16[16,16,384]{2,1,0:T(8,128)(2,1)} %copy-done.7, bf16[16,16,384]{2,1,0:T(8,128)(2,1)} %copy-done.6), custom_call_target="tpu_custom_call" | custom-call | tf_op jit(solution)/shard_map/pallas_call | solution.py:498
  135.8 2.3 %collective-permute-start.15 = (bf16[4,16,16,384]{3,2,1,0:T(8,128)(2,1)}, bf16[4,16,16,384]{3,2,1,0:T(8,128)(2,1)S(1)}, u32[]{:S(2)}, u32[]{:S(2)}) collective-permute-start(bf16[4,16,16,384]{3,2,1,0:T(8,128)(2,1)} %shard_map.80.mine), channel_id=1, source_target_pairs={{0,8},{8,0},{64,72},{72,64},{1,9},{9,1},{65,73},{73,65},{16,24},{2... | collective-permute-start | bytes 2359304 | tf_op jit(solution)/shard_map/ppermute | solution.py:595
  138.9 1.3 collective-permute-done.15.theirs
  140.2 1.1 copy-done
  141.4 2.2 %shard_map.81 = f32[9,256,256]{2,1,0:T(8,128)} custom-call(s32[6]{0:T(128)S(1)} %copy-done.2, bf16[4,16,16,384]{3,2,1,0:T(8,128)(2,1)S(1)} %copy-done, bf16[4,16,16,384]{3,2,1,0:T(8,128)(2,1)S(1)} %collective-permute-done.15.theirs), custom_call_target="tpu_custom_call" | custom-call | tf_op jit(solution)/shard_map/pallas_call | solution.py:533
  (43 shorter events, 5.5 us)
Async XLA Ops:
  1.6 9.8 %collective-permute-start.1 = (bf16[2,1,128,256]{3,2,1,0:T(8,128)(2,1)S(1)}, bf16[2,1,128,256]{3,2,1,0:T(8,128)(2,1)S(1)}, u32[]{:S(2)}, u32[]{:S(2)}) collective-permute-start(bf16[2,1,128,256]{3,2,1,0:T(8,128)(2,1)S(1)} %get-tuple-element.45), channel_id=1, source_target_pairs={{1,0},{2,1},{3,2},{4,3},{5,4},{6,5},{7,6},{0,7},{9,8},{10,9},{11,1... | collective-permute-start | bytes 393224 | tf_op jit(solution)/shard_map/ppermute | solution.py:544
  8.3 7.4 %collective-permute-start = (bf16[2,1,128,256]{3,2,1,0:T(8,128)(2,1)S(1)}, bf16[2,1,128,256]{3,2,1,0:T(8,128)(2,1)S(1)}, u32[]{:S(2)}, u32[]{:S(2)}) collective-permute-start(bf16[2,1,128,256]{3,2,1,0:T(8,128)(2,1)S(1)} %get-tuple-element.46), channel_id=1, source_target_pairs={{0,1},{1,2},{2,3},{3,4},{4,5},{5,6},{6,7},{7,0},{8,9},{9,10},{10,1... | collective-permute-start | bytes 393224 | tf_op jit(solution)/shard_map/ppermute | solution.py:543
  11.4 4.4 %copy-start.9 = (bf16[2,1,128,256]{3,2,1,0:T(8,128)(2,1)}, bf16[2,1,128,256]{3,2,1,0:T(8,128)(2,1)S(1)}, u32[]{:S(2)}) copy-start(bf16[2,1,128,256]{3,2,1,0:T(8,128)(2,1)S(1)} %collective-permute-done.1.below) | copy-start | bytes 393220
  15.7 0.7 copy-start.10
  62.1 16.1 %collective-permute-start.6 = (bf16[4,2048,256]{2,1,0:T(8,128)(2,1)}, bf16[4,2048,256]{2,1,0:T(8,128)(2,1)S(1)}, u32[]{:S(2)}, u32[]{:S(2)}) collective-permute-start(bf16[4,2048,256]{2,1,0:T(8,128)(2,1)} %get-tuple-element.27), channel_id=1, source_target_pairs={{0,8},{8,0},{64,72},{72,64},{1,9},{9,1},{65,73},{73,65},{16,24},{2... | collective-permute-start | bytes 12582920 | tf_op jit(solution)/shard_map/ppermute | solution.py:566
  64.2 8.1 %collective-permute-start.2 = (bf16[4,16,16,384]{3,2,1,0:T(8,128)(2,1)}, bf16[4,16,16,384]{3,2,1,0:T(8,128)(2,1)S(1)}, u32[]{:S(2)}, u32[]{:S(2)}) collective-permute-start(bf16[4,16,16,384]{3,2,1,0:T(8,128)(2,1)} %get-tuple-element.25), channel_id=1, source_target_pairs={{0,8},{8,0},{64,72},{72,64},{1,9},{9,1},{65,73},{73,65},{16,24},{2... | collective-permute-start | bytes 2359304 | tf_op jit(solution)/shard_map/ppermute | solution.py:569
  64.3 12.4 %collective-permute-start.7 = (bf16[2,1,128,256]{3,2,1,0:T(8,128)(2,1)}, bf16[2,1,128,256]{3,2,1,0:T(8,128)(2,1)S(1)}, u32[]{:S(2)}, u32[]{:S(2)}) collective-permute-start(bf16[2,1,128,256]{3,2,1,0:T(8,128)(2,1)} %get-tuple-element.28), channel_id=1, source_target_pairs={{0,1},{1,2},{2,3},{3,4},{4,5},{5,6},{6,7},{7,0},{8,9},{9,10},{10,1... | collective-permute-start | bytes 393224 | tf_op jit(solution)/shard_map/ppermute | solution.py:543
  64.3 13.9 %collective-permute-start.8 = (bf16[2,1,128,256]{3,2,1,0:T(8,128)(2,1)}, bf16[2,1,128,256]{3,2,1,0:T(8,128)(2,1)S(1)}, u32[]{:S(2)}, u32[]{:S(2)}) collective-permute-start(bf16[2,1,128,256]{3,2,1,0:T(8,128)(2,1)} %get-tuple-element.29), channel_id=1, source_target_pairs={{1,0},{2,1},{3,2},{4,3},{5,4},{6,5},{7,6},{0,7},{9,8},{10,9},{11,1... | collective-permute-start | bytes 393224 | tf_op jit(solution)/shard_map/ppermute | solution.py:544
  73.7 11.0 %collective-permute-start.3 = (bf16[16,16,384]{2,1,0:T(8,128)(2,1)S(1)}, bf16[16,16,384]{2,1,0:T(8,128)(2,1)S(1)}, u32[]{:S(2)}, u32[]{:S(2)}) collective-permute-start(bf16[16,16,384]{2,1,0:T(8,128)(2,1)S(1)} %get-tuple-element.47), channel_id=1, source_target_pairs={{0,2},{8,24},{64,66},{72,88},{1,3},{9,25},{65,67},{73,89},{16,18},... | collective-permute-start | bytes 589832 | tf_op jit(solution)/shard_map/ppermute | solution.py:576
  75.1 9.7 %collective-permute-start.5 = (bf16[16,16,384]{2,1,0:T(8,128)(2,1)S(1)}, bf16[16,16,384]{2,1,0:T(8,128)(2,1)S(1)}, u32[]{:S(2)}, u32[]{:S(2)}) collective-permute-start(bf16[16,16,384]{2,1,0:T(8,128)(2,1)S(1)} %get-tuple-element.48), channel_id=1, source_target_pairs={{0,6},{8,56},{64,70},{72,120},{1,7},{9,57},{65,71},{73,121},{16,22... | collective-permute-start | bytes 589832 | tf_op jit(solution)/shard_map/ppermute | solution.py:576
  76.6 8.2 %collective-permute-start.4 = (bf16[16,16,384]{2,1,0:T(8,128)(2,1)S(1)}, bf16[16,16,384]{2,1,0:T(8,128)(2,1)S(1)}, u32[]{:S(2)}, u32[]{:S(2)}) collective-permute-start(bf16[16,16,384]{2,1,0:T(8,128)(2,1)S(1)} %get-tuple-element.49), channel_id=1, source_target_pairs={{0,4},{8,40},{64,68},{72,104},{1,5},{9,41},{65,69},{73,105},{16,20... | collective-permute-start | bytes 589832 | tf_op jit(solution)/shard_map/ppermute | solution.py:576
  78.1 11.6 %copy-start.1 = (s32[6]{0:T(128)S(1)}, s32[6]{0:T(128)}, u32[]{:S(2)}) copy-start(s32[6]{0:T(128)} %stack.23.info) | copy-start | bytes 76
  81.9 27.5 %collective-permute-start.10 = (bf16[16,128,256]{2,1,0:T(8,128)(2,1)}, bf16[16,128,256]{2,1,0:T(8,128)(2,1)S(1)}, u32[]{:S(2)}, u32[]{:S(2)}) collective-permute-start(bf16[16,128,256]{2,1,0:T(8,128)(2,1)} %bitcast.18), channel_id=1, source_target_pairs={{0,4},{8,40},{64,68},{72,104},{1,5},{9,41},{65,69},{73,105},{16,20... | collective-permute-start | bytes 3145736 | tf_op jit(solution)/shard_map/ppermute | solution.py:581
  83.3 26.0 %collective-permute-start.11 = (bf16[16,128,256]{2,1,0:T(8,128)(2,1)}, bf16[16,128,256]{2,1,0:T(8,128)(2,1)S(1)}, u32[]{:S(2)}, u32[]{:S(2)}) collective-permute-start(bf16[16,128,256]{2,1,0:T(8,128)(2,1)} %bitcast.20), channel_id=1, source_target_pairs={{0,6},{8,56},{64,70},{72,120},{1,7},{9,57},{65,71},{73,121},{16,22... | collective-permute-start | bytes 3145736 | tf_op jit(solution)/shard_map/ppermute | solution.py:581
  84.7 24.9 %collective-permute-start.9 = (bf16[16,128,256]{2,1,0:T(8,128)(2,1)}, bf16[16,128,256]{2,1,0:T(8,128)(2,1)}, u32[]{:S(2)}, u32[]{:S(2)}) collective-permute-start(bf16[16,128,256]{2,1,0:T(8,128)(2,1)} %bitcast.16), channel_id=1, source_target_pairs={{0,2},{8,24},{64,66},{72,88},{1,3},{9,25},{65,67},{73,89},{16,18},... | collective-permute-start | bytes 3145736 | tf_op jit(solution)/shard_map/ppermute | solution.py:581
  85.6 15.5 %all-to-all-start = ((bf16[16,16,384]{2,1,0:T(8,128)(2,1)}), bf16[16,16,384]{2,1,0:T(8,128)(2,1)}, u32[]{:S(2)}, u32[]{:S(2)}) async-start(bf16[16,16,384]{2,1,0:T(8,128)(2,1)} %fusion.3), calls=%async_computation | async-start | bytes 393216 | tf_op jit(solution)/shard_map/all_to_all | solution.py:583
  89.8 1.3 copy-start.3
  91.1 1.6 %copy-start.4 = (bf16[4096,256]{1,0:T(8,128)(2,1)S(1)}, bf16[4096,256]{1,0:T(8,128)(2,1)}, u32[]{:S(2)}) copy-start(bf16[4096,256]{1,0:T(8,128)(2,1)} %get-tuple-element.32) | copy-start | bytes 6291460
  102.8 13.5 %all-to-all-start.1 = ((bf16[16,16,384]{2,1,0:T(8,128)(2,1)}), bf16[16,16,384]{2,1,0:T(8,128)(2,1)S(1)}, u32[]{:S(2)}, u32[]{:S(2)}) async-start(bf16[16,16,384]{2,1,0:T(8,128)(2,1)} %broadcast_in_dim.2), calls=%async_computation.1 | async-start | bytes 393216 | tf_op jit(solution)/shard_map/all_to_all | solution.py:587
  116.3 16.6 %copy-start.5 = (bf16[16,16,384]{2,1,0:T(8,128)(2,1)}, bf16[16,16,384]{2,1,0:T(8,128)(2,1)S(1)}, u32[]{:S(2)}) copy-start(bf16[16,16,384]{2,1,0:T(8,128)(2,1)S(1)} %all-to-all-done.1.refs_0_) | copy-start | bytes 589828
  116.3 23.9 %copy-start.2 = (s32[6]{0:T(128)S(1)}, s32[6]{0:T(128)}, u32[]{:S(2)}) copy-start(s32[6]{0:T(128)} %stack.23.info) | copy-start | bytes 76
  116.3 21.8 %all-to-all-start.2 = ((bf16[16,128,256]{2,1,0:T(8,128)(2,1)}), bf16[16,128,256]{2,1,0:T(8,128)(2,1)S(1)}, u32[]{:S(2)}, u32[]{:S(2)}) async-start(bf16[16,128,256]{2,1,0:T(8,128)(2,1)} %bitcast.22), calls=%async_computation.2 | async-start | bytes 2097152 | tf_op jit(solution)/shard_map/all_to_all | solution.py:592
  120.2 11.3 %collective-permute-start.14 = (bf16[16,16,384]{2,1,0:T(8,128)(2,1)S(1)}, bf16[16,16,384]{2,1,0:T(8,128)(2,1)S(1)}, u32[]{:S(2)}, u32[]{:S(2)}) collective-permute-start(bf16[16,16,384]{2,1,0:T(8,128)(2,1)S(1)} %all-to-all-done.1.refs_0_), channel_id=1, source_target_pairs={{0,6},{8,56},{64,70},{72,120},{1,7},{9,57},{65,71},{73,121},{16,22... | collective-permute-start | bytes 589832 | tf_op jit(solution)/shard_map/ppermute | solution.py:593
  122.8 8.6 %collective-permute-start.13 = (bf16[16,16,384]{2,1,0:T(8,128)(2,1)S(1)}, bf16[16,16,384]{2,1,0:T(8,128)(2,1)S(1)}, u32[]{:S(2)}, u32[]{:S(2)}) collective-permute-start(bf16[16,16,384]{2,1,0:T(8,128)(2,1)S(1)} %all-to-all-done.1.refs_0_), channel_id=1, source_target_pairs={{0,4},{8,40},{64,68},{72,104},{1,5},{9,41},{65,69},{73,105},{16,20... | collective-permute-start | bytes 589832 | tf_op jit(solution)/shard_map/ppermute | solution.py:593
  122.8 10.1 %collective-permute-start.12 = (bf16[16,16,384]{2,1,0:T(8,128)(2,1)S(1)}, bf16[16,16,384]{2,1,0:T(8,128)(2,1)S(1)}, u32[]{:S(2)}, u32[]{:S(2)}) collective-permute-start(bf16[16,16,384]{2,1,0:T(8,128)(2,1)S(1)} %all-to-all-done.1.refs_0_), channel_id=1, source_target_pairs={{0,2},{8,24},{64,66},{72,88},{1,3},{9,25},{65,67},{73,89},{16,18},... | collective-permute-start | bytes 589832 | tf_op jit(solution)/shard_map/ppermute | solution.py:593
  131.5 1.5 %copy-start.6 = (bf16[16,16,384]{2,1,0:T(8,128)(2,1)}, bf16[16,16,384]{2,1,0:T(8,128)(2,1)S(1)}, u32[]{:S(2)}) copy-start(bf16[16,16,384]{2,1,0:T(8,128)(2,1)S(1)} %collective-permute-done.14.refs_3_) | copy-start | bytes 589828
  131.5 1.5 %copy-start.7 = (bf16[16,16,384]{2,1,0:T(8,128)(2,1)}, bf16[16,16,384]{2,1,0:T(8,128)(2,1)S(1)}, u32[]{:S(2)}) copy-start(bf16[16,16,384]{2,1,0:T(8,128)(2,1)S(1)} %collective-permute-done.13.refs_2_) | copy-start | bytes 589828
  132.9 0.7 copy-start.8
  135.8 4.5 %collective-permute-start.15 = (bf16[4,16,16,384]{3,2,1,0:T(8,128)(2,1)}, bf16[4,16,16,384]{3,2,1,0:T(8,128)(2,1)S(1)}, u32[]{:S(2)}, u32[]{:S(2)}) collective-permute-start(bf16[4,16,16,384]{3,2,1,0:T(8,128)(2,1)} %shard_map.80.mine), channel_id=1, source_target_pairs={{0,8},{8,0},{64,72},{72,64},{1,9},{9,1},{65,73},{73,65},{16,24},{2... | collective-permute-start | bytes 2359304 | tf_op jit(solution)/shard_map/ppermute | solution.py:595
  140.2 1.1 copy-start

commit v7 on v6

--- a/solution.py
+++ b/solution.py
@@ -26,7 +26,7 @@
 GROUPS = DEPTHS * SPOTS // GROUP
 SPILL = 64
 CHUNKS = 8
-UNROLL = 16
+UNROLL = 32
 PIECES = 96
 PIECE = (16, 384)
 SHARE = CODES // 128
@@ -318,7 +318,7 @@
 
     for first, core, out in ((0, 1 - info[3], send), (4, info[3], keep)):
         for j in range(4):
-            lax.fori_loop(0, 16, functools.partial(fill, first=first, core=core, j=j), 0, unroll=2)
+            lax.fori_loop(0, 16, functools.partial(fill, first=first, core=core, j=j), 0, unroll=4)
             put_out(out, first, j).start()
 
     weight_sum[...] = jnp.zeros_like(weight_sum)

time: 144 us -> 144 us (level)
  no operation moved by 1% of the time
where the time goes in v7:
time: 144 us; the launch traced here: 143 us
  Pallas kernels  63 us (44%)
  starting transfers between devices  41.7 us (29%)
  waiting for transfers between devices  22.2 us (15%)
  local copies, waits for them, and re-layouts  7.75 us (5%)
  other arithmetic  7.58 us (5%)
    pallas_call x1, Pallas kernels, quantizer(): pl.pallas_call(quantizer_kernel, in_specs=[smem] * 2 + [hbm] * 4 + [vmem]...  45 us
    ppermute x2, starting transfers between devices, edges(): below = lax.ppermute(first, 'tile', [((i + 1) % n, i) for i in range(n)])  11.8 us
    ppermute x3, waiting for transfers between devices, on_device(): around = [lax.ppermute(pieces, BOTH, first_ring(d)) for d in (1, 2, 3)]  9.38 us
    pallas_call x1, Pallas kernels, feature_grads(): pl.pallas_call(back_kernel, grid=(BLOCKS,), in_specs=[pl.BlockSpec(memory...  8.48 us
    all_to_all x1, starting transfers between devices, on_device(): lax.all_to_all(jnp.broadcast_to(piece[None], (16,) + PIECE), BOTH, 0, 0,...  6.54 us
    unnamed x22, local copies, waits for them, and re-layouts  5.32 us
    ppermute x3, starting transfers between devices, on_device(): lax.ppermute(weight_chip[d], BOTH, first_ring(d)).astype(F32)  4.56 us
    ppermute x2, waiting for transfers between devices, edges(): above = lax.ppermute(last, 'tile', [(i, (i + 1) % n) for i in range(n)])  4.36 us
  transfers between devices with their start and end apart: 19, of which 7 were waited for; matrix products, arithmetic and copies ran while one was open for 6% of the time, Pallas kernels for 11%

profile of v7, /device:TPU:1, one launch (start us, length us, event | category | flops | bytes accessed | tf_op | source)
XLA Modules:
  0.0 143.0 jit_solution(9731027248925889107)
XLA Ops:
  0.6 1.0 fusion.4
  1.6 6.7 %collective-permute-start.1 = (bf16[2,1,128,256]{3,2,1,0:T(8,128)(2,1)S(1)}, bf16[2,1,128,256]{3,2,1,0:T(8,128)(2,1)S(1)}, u32[]{:S(2)}, u32[]{:S(2)}) collective-permute-start(bf16[2,1,128,256]{3,2,1,0:T(8,128)(2,1)S(1)} %get-tuple-element.45), channel_id=1, source_target_pairs={{1,0},{2,1},{3,2},{4,3},{5,4},{6,5},{7,6},{0,7},{9,8},{10,9},{11,1... | collective-permute-start | bytes 393224 | tf_op jit(solution)/shard_map/ppermute | solution.py:544
  8.3 2.4 %shard_map.76 = (s32[128,128]{1,0:T(8,128)}, s32[8,128]{1,0:T(8,128)}) custom-call(s32[128,128]{1,0:T(8,128)} %bitcast.34), custom_call_target="tpu_custom_call" | custom-call | tf_op jit(solution)/shard_map/pallas_call | solution.py:135
  11.4 4.4 %collective-permute-done.above = bf16[2,1,128,256]{3,2,1,0:T(8,128)(2,1)S(1)} collective-permute-done((bf16[2,1,128,256]{3,2,1,0:T(8,128)(2,1)S(1)}, bf16[2,1,128,256]{3,2,1,0:T(8,128)(2,1)S(1)}, u32[]{:S(2)}, u32[]{:S(2)}) %collective-permute-start) | collective-permute-done | bytes 131104 | tf_op jit(solution)/shard_map/ppermute | solution.py:543
  16.4 45.0 %shard_map.77 = (bf16[4096,256]{1,0:T(8,128)(2,1)}, bf16[2,1,128,256]{3,2,1,0:T(8,128)(2,1)}, bf16[2,1,128,256]{3,2,1,0:T(8,128)(2,1)}, bf16[4,2048,256]{2,1,0:T...) custom-call(s32[8,128]{1,0:T(8,128)} %get-tuple-element.22.extra, ...), custom_call_target="tpu_custom_call" | custom-call | flops 9663676416 | bytes 67108864 | tf_op jit(solution)/shard_map/pallas_call | solution.py:375
  61.4 2.1 %collective-permute-start.6 = (bf16[4,2048,256]{2,1,0:T(8,128)(2,1)}, bf16[4,2048,256]{2,1,0:T(8,128)(2,1)S(1)}, u32[]{:S(2)}, u32[]{:S(2)}) collective-permute-start(bf16[4,2048,256]{2,1,0:T(8,128)(2,1)} %get-tuple-element.27), channel_id=1, source_target_pairs={{0,8},{8,0},{64,72},{72,64},{1,9},{9,1},{65,73},{73,65},{16,24},{2... | collective-permute-start | bytes 12582920 | tf_op jit(solution)/shard_map/ppermute | solution.py:566
  63.6 5.1 %collective-permute-start.8 = (bf16[2,1,128,256]{3,2,1,0:T(8,128)(2,1)}, bf16[2,1,128,256]{3,2,1,0:T(8,128)(2,1)S(1)}, u32[]{:S(2)}, u32[]{:S(2)}) collective-permute-start(bf16[2,1,128,256]{3,2,1,0:T(8,128)(2,1)} %get-tuple-element.29), channel_id=1, source_target_pairs={{1,0},{2,1},{3,2},{4,3},{5,4},{6,5},{7,6},{0,7},{9,8},{10,9},{11,1... | collective-permute-start | bytes 393224 | tf_op jit(solution)/shard_map/ppermute | solution.py:544
  68.7 2.9 %collective-permute-done.2 = bf16[4,16,16,384]{3,2,1,0:T(8,128)(2,1)S(1)} collective-permute-done((bf16[4,16,16,384]{3,2,1,0:T(8,128)(2,1)}, bf16[4,16,16,384]{3,2,1,0:T(8,128)(2,1)S(1)}, u32[]{:S(2)}, u32[]{:S(2)}) %collective-permute-start.2) | collective-permute-done | bytes 786464 | tf_op jit(solution)/shard_map/ppermute | solution.py:569
  71.7 1.3 add_convert_fusion.4
  73.1 1.4 collective-permute-start.3
  74.4 1.6 %collective-permute-start.5 = (bf16[16,16,384]{2,1,0:T(8,128)(2,1)S(1)}, bf16[16,16,384]{2,1,0:T(8,128)(2,1)S(1)}, u32[]{:S(2)}, u32[]{:S(2)}) collective-permute-start(bf16[16,16,384]{2,1,0:T(8,128)(2,1)S(1)} %get-tuple-element.48), channel_id=1, source_target_pairs={{0,6},{8,56},{64,70},{72,120},{1,7},{9,57},{65,71},{73,121},{16,22... | collective-permute-start | bytes 589832 | tf_op jit(solution)/shard_map/ppermute | solution.py:576
  76.0 1.6 %collective-permute-start.4 = (bf16[16,16,384]{2,1,0:T(8,128)(2,1)S(1)}, bf16[16,16,384]{2,1,0:T(8,128)(2,1)S(1)}, u32[]{:S(2)}, u32[]{:S(2)}) collective-permute-start(bf16[16,16,384]{2,1,0:T(8,128)(2,1)S(1)} %get-tuple-element.49), channel_id=1, source_target_pairs={{0,4},{8,40},{64,68},{72,104},{1,5},{9,41},{65,69},{73,105},{16,20... | collective-permute-start | bytes 589832 | tf_op jit(solution)/shard_map/ppermute | solution.py:576
  77.6 3.7 %add_convert_fusion = (bf16[1,2048,256]{2,1,0:T(8,128)(2,1)}, bf16[1,2048,256]{2,1,0:T(8,128)(2,1)}, bf16[1,2048,256]{2,1,0:T(8,128)(2,1)}, bf16[2048,256]{1,0:T(8,128)(2,1)S(1)}) fusion(bf16[4,2048,256]{2,1,0:T(8,128)(2,1)S(1)} %collective-permute-done.6, bf16[4,2048,256]{2,1,0:T(8,128)(2,1)} %get-tuple-element.37), kind=kLoop, calls=%fused_computation.1 | loop fusion | flops 8388608 | bytes 12582912 | tf_op jit(solution)/shard_map/convert_element_type | solution.py:578
  81.4 1.4 collective-permute-start.10
  82.7 1.4 collective-permute-start.11
  85.0 4.2 %all-to-all-start = ((bf16[16,16,384]{2,1,0:T(8,128)(2,1)}), bf16[16,16,384]{2,1,0:T(8,128)(2,1)}, u32[]{:S(2)}, u32[]{:S(2)}) async-start(bf16[16,16,384]{2,1,0:T(8,128)(2,1)} %fusion.3), calls=%async_computation | async-start | bytes 393216 | tf_op jit(solution)/shard_map/all_to_all | solution.py:583
  89.2 1.3 copy-done.3
  90.5 1.6 %copy-done.4 = bf16[4096,256]{1,0:T(8,128)(2,1)S(1)} copy-done((bf16[4096,256]{1,0:T(8,128)(2,1)S(1)}, bf16[4096,256]{1,0:T(8,128)(2,1)}, u32[]{:S(2)}) %copy-start.4) | copy-done | bytes 2097176
  92.0 8.5 %shard_map.78 = bf16[4096,256]{1,0:T(8,128)(2,1)} custom-call(s32[6]{0:T(128)S(1)} %copy-done.1, bf16[2,16,128,256]{3,2,1,0:T(8,128)(2,1)S(1)} %bitcast.33, bf16[2,1,128,256]{3,2,1,0:T(8,128)(2,1)S(1)} %collective-permute-done.7.above, bf16[2,1,128,256]{3,2,1,0:T(8,128)(2,1)S(1)} %collective-permute-done.8.below, bf16[9,256,256]{2,1,0:T(8,128)(2,1)S(1)} %copy-done.3), custom_call_target="tpu_custom_call" | custom-call | flops 4831838208 | bytes 8388608 | tf_op jit(solution)/shard_map/pallas_call | solution.py:437
  100.5 1.0 reduce_sum.21
  102.2 6.5 %all-to-all-start.1 = ((bf16[16,16,384]{2,1,0:T(8,128)(2,1)}), bf16[16,16,384]{2,1,0:T(8,128)(2,1)S(1)}, u32[]{:S(2)}, u32[]{:S(2)}) async-start(bf16[16,16,384]{2,1,0:T(8,128)(2,1)} %broadcast_in_dim.2), calls=%async_computation.1 | async-start | bytes 393216 | tf_op jit(solution)/shard_map/all_to_all | solution.py:587
  109.1 2.7 %shard_map.79 = bf16[2048,256]{1,0:T(8,128)(2,1)} custom-call(bf16[2048,256]{1,0:T(8,128)(2,1)S(1)} %get-tuple-element.44.refs_0_, bf16[2048,256]{1,0:T(8,128)(2,1)} %bitcast.17.refs_1_, bf16[2048,256]{1,0:T(8,128)(2,1)S(1)} %bitcast.31, bf16[2048,256]{1,0:T(8,128)(2,1)S(1)} %bitcast.32), custom_call_target="tpu_custom_call" | custom-call | flops 1048576 | bytes 4194304 | tf_op jit(solution)/shard_map/pallas_call | solution.py:480
  111.8 3.8 %all-to-all-done.1.refs_0_ = bf16[16,16,384]{2,1,0:T(8,128)(2,1)S(1)} async-done(((bf16[16,16,384]{2,1,0:T(8,128)(2,1)}), bf16[16,16,384]{2,1,0:T(8,128)(2,1)S(1)}, u32[]{:S(2)}, u32[]{:S(2)}) %all-to-all-start.1) | async-done | bytes 196640 | tf_op jit(solution)/shard_map/all_to_all | solution.py:587
  115.7 3.9 %all-to-all-start.2 = ((bf16[16,128,256]{2,1,0:T(8,128)(2,1)}), bf16[16,128,256]{2,1,0:T(8,128)(2,1)S(1)}, u32[]{:S(2)}, u32[]{:S(2)}) async-start(bf16[16,128,256]{2,1,0:T(8,128)(2,1)} %bitcast.22), calls=%async_computation.2 | async-start | bytes 2097152 | tf_op jit(solution)/shard_map/all_to_all | solution.py:592
  119.6 2.7 %collective-permute-start.14 = (bf16[16,16,384]{2,1,0:T(8,128)(2,1)S(1)}, bf16[16,16,384]{2,1,0:T(8,128)(2,1)S(1)}, u32[]{:S(2)}, u32[]{:S(2)}) collective-permute-start(bf16[16,16,384]{2,1,0:T(8,128)(2,1)S(1)} %all-to-all-done.1.refs_0_), channel_id=1, source_target_pairs={{0,6},{8,56},{64,70},{72,120},{1,7},{9,57},{65,71},{73,121},{16,22... | collective-permute-start | bytes 589832 | tf_op jit(solution)/shard_map/ppermute | solution.py:593
  122.9 6.6 %collective-permute-done.14.refs_3_ = bf16[16,16,384]{2,1,0:T(8,128)(2,1)S(1)} collective-permute-done((bf16[16,16,384]{2,1,0:T(8,128)(2,1)S(1)}, bf16[16,16,384]{2,1,0:T(8,128)(2,1)S(1)}, u32[]{:S(2)}, u32[]{:S(2)}) %collective-permute-start.14) | collective-permute-done | bytes 196640 | tf_op jit(solution)/shard_map/ppermute | solution.py:593
  129.5 2.8 %collective-permute-done.12.refs_1_ = bf16[16,16,384]{2,1,0:T(8,128)(2,1)S(1)} collective-permute-done((bf16[16,16,384]{2,1,0:T(8,128)(2,1)S(1)}, bf16[16,16,384]{2,1,0:T(8,128)(2,1)S(1)}, u32[]{:S(2)}, u32[]{:S(2)}) %collective-permute-start.12) | collective-permute-done | bytes 196640 | tf_op jit(solution)/shard_map/ppermute | solution.py:593
  133.0 2.2 %shard_map.80.mine = bf16[4,16,16,384]{3,2,1,0:T(8,128)(2,1)} custom-call(s32[6]{0:T(128)} %stack.23.info, bf16[16,16,384]{2,1,0:T(8,128)(2,1)} %copy-done.5, bf16[16,16,384]{2,1,0:T(8,128)(2,1)} %copy-done.8, bf16[16,16,384]{2,1,0:T(8,128)(2,1)} %copy-done.7, bf16[16,16,384]{2,1,0:T(8,128)(2,1)} %copy-done.6), custom_call_target="tpu_custom_call" | custom-call | tf_op jit(solution)/shard_map/pallas_call | solution.py:498
  135.2 2.4 %collective-permute-start.15 = (bf16[4,16,16,384]{3,2,1,0:T(8,128)(2,1)}, bf16[4,16,16,384]{3,2,1,0:T(8,128)(2,1)S(1)}, u32[]{:S(2)}, u32[]{:S(2)}) collective-permute-start(bf16[4,16,16,384]{3,2,1,0:T(8,128)(2,1)} %shard_map.80.mine), channel_id=1, source_target_pairs={{0,8},{8,0},{64,72},{72,64},{1,9},{9,1},{65,73},{73,65},{16,24},{2... | collective-permute-start | bytes 2359304 | tf_op jit(solution)/shard_map/ppermute | solution.py:595
  138.3 1.3 collective-permute-done.15.theirs
  139.6 1.1 copy-done
  140.8 2.2 %shard_map.81 = f32[9,256,256]{2,1,0:T(8,128)} custom-call(s32[6]{0:T(128)S(1)} %copy-done.2, bf16[4,16,16,384]{3,2,1,0:T(8,128)(2,1)S(1)} %copy-done, bf16[4,16,16,384]{3,2,1,0:T(8,128)(2,1)S(1)} %collective-permute-done.15.theirs), custom_call_target="tpu_custom_call" | custom-call | tf_op jit(solution)/shard_map/pallas_call | solution.py:533
  (43 shorter events, 5.6 us)
Async XLA Ops:
  1.6 9.8 %collective-permute-start.1 = (bf16[2,1,128,256]{3,2,1,0:T(8,128)(2,1)S(1)}, bf16[2,1,128,256]{3,2,1,0:T(8,128)(2,1)S(1)}, u32[]{:S(2)}, u32[]{:S(2)}) collective-permute-start(bf16[2,1,128,256]{3,2,1,0:T(8,128)(2,1)S(1)} %get-tuple-element.45), channel_id=1, source_target_pairs={{1,0},{2,1},{3,2},{4,3},{5,4},{6,5},{7,6},{0,7},{9,8},{10,9},{11,1... | collective-permute-start | bytes 393224 | tf_op jit(solution)/shard_map/ppermute | solution.py:544
  8.3 7.4 %collective-permute-start = (bf16[2,1,128,256]{3,2,1,0:T(8,128)(2,1)S(1)}, bf16[2,1,128,256]{3,2,1,0:T(8,128)(2,1)S(1)}, u32[]{:S(2)}, u32[]{:S(2)}) collective-permute-start(bf16[2,1,128,256]{3,2,1,0:T(8,128)(2,1)S(1)} %get-tuple-element.46), channel_id=1, source_target_pairs={{0,1},{1,2},{2,3},{3,4},{4,5},{5,6},{6,7},{7,0},{8,9},{9,10},{10,1... | collective-permute-start | bytes 393224 | tf_op jit(solution)/shard_map/ppermute | solution.py:543
  11.4 4.4 %copy-start.9 = (bf16[2,1,128,256]{3,2,1,0:T(8,128)(2,1)}, bf16[2,1,128,256]{3,2,1,0:T(8,128)(2,1)S(1)}, u32[]{:S(2)}) copy-start(bf16[2,1,128,256]{3,2,1,0:T(8,128)(2,1)S(1)} %collective-permute-done.1.below) | copy-start | bytes 393220
  15.7 0.7 copy-start.10
  61.4 16.2 %collective-permute-start.6 = (bf16[4,2048,256]{2,1,0:T(8,128)(2,1)}, bf16[4,2048,256]{2,1,0:T(8,128)(2,1)S(1)}, u32[]{:S(2)}, u32[]{:S(2)}) collective-permute-start(bf16[4,2048,256]{2,1,0:T(8,128)(2,1)} %get-tuple-element.27), channel_id=1, source_target_pairs={{0,8},{8,0},{64,72},{72,64},{1,9},{9,1},{65,73},{73,65},{16,24},{2... | collective-permute-start | bytes 12582920 | tf_op jit(solution)/shard_map/ppermute | solution.py:566
  63.5 8.1 %collective-permute-start.2 = (bf16[4,16,16,384]{3,2,1,0:T(8,128)(2,1)}, bf16[4,16,16,384]{3,2,1,0:T(8,128)(2,1)S(1)}, u32[]{:S(2)}, u32[]{:S(2)}) collective-permute-start(bf16[4,16,16,384]{3,2,1,0:T(8,128)(2,1)} %get-tuple-element.25), channel_id=1, source_target_pairs={{0,8},{8,0},{64,72},{72,64},{1,9},{9,1},{65,73},{73,65},{16,24},{2... | collective-permute-start | bytes 2359304 | tf_op jit(solution)/shard_map/ppermute | solution.py:569
  63.6 12.4 %collective-permute-start.7 = (bf16[2,1,128,256]{3,2,1,0:T(8,128)(2,1)}, bf16[2,1,128,256]{3,2,1,0:T(8,128)(2,1)S(1)}, u32[]{:S(2)}, u32[]{:S(2)}) collective-permute-start(bf16[2,1,128,256]{3,2,1,0:T(8,128)(2,1)} %get-tuple-element.28), channel_id=1, source_target_pairs={{0,1},{1,2},{2,3},{3,4},{4,5},{5,6},{6,7},{7,0},{8,9},{9,10},{10,1... | collective-permute-start | bytes 393224 | tf_op jit(solution)/shard_map/ppermute | solution.py:543
  63.6 14.0 %collective-permute-start.8 = (bf16[2,1,128,256]{3,2,1,0:T(8,128)(2,1)}, bf16[2,1,128,256]{3,2,1,0:T(8,128)(2,1)S(1)}, u32[]{:S(2)}, u32[]{:S(2)}) collective-permute-start(bf16[2,1,128,256]{3,2,1,0:T(8,128)(2,1)} %get-tuple-element.29), channel_id=1, source_target_pairs={{1,0},{2,1},{3,2},{4,3},{5,4},{6,5},{7,6},{0,7},{9,8},{10,9},{11,1... | collective-permute-start | bytes 393224 | tf_op jit(solution)/shard_map/ppermute | solution.py:544
  73.1 11.1 %collective-permute-start.3 = (bf16[16,16,384]{2,1,0:T(8,128)(2,1)S(1)}, bf16[16,16,384]{2,1,0:T(8,128)(2,1)S(1)}, u32[]{:S(2)}, u32[]{:S(2)}) collective-permute-start(bf16[16,16,384]{2,1,0:T(8,128)(2,1)S(1)} %get-tuple-element.47), channel_id=1, source_target_pairs={{0,2},{8,24},{64,66},{72,88},{1,3},{9,25},{65,67},{73,89},{16,18},... | collective-permute-start | bytes 589832 | tf_op jit(solution)/shard_map/ppermute | solution.py:576
  74.4 9.8 %collective-permute-start.5 = (bf16[16,16,384]{2,1,0:T(8,128)(2,1)S(1)}, bf16[16,16,384]{2,1,0:T(8,128)(2,1)S(1)}, u32[]{:S(2)}, u32[]{:S(2)}) collective-permute-start(bf16[16,16,384]{2,1,0:T(8,128)(2,1)S(1)} %get-tuple-element.48), channel_id=1, source_target_pairs={{0,6},{8,56},{64,70},{72,120},{1,7},{9,57},{65,71},{73,121},{16,22... | collective-permute-start | bytes 589832 | tf_op jit(solution)/shard_map/ppermute | solution.py:576
  76.0 8.2 %collective-permute-start.4 = (bf16[16,16,384]{2,1,0:T(8,128)(2,1)S(1)}, bf16[16,16,384]{2,1,0:T(8,128)(2,1)S(1)}, u32[]{:S(2)}, u32[]{:S(2)}) collective-permute-start(bf16[16,16,384]{2,1,0:T(8,128)(2,1)S(1)} %get-tuple-element.49), channel_id=1, source_target_pairs={{0,4},{8,40},{64,68},{72,104},{1,5},{9,41},{65,69},{73,105},{16,20... | collective-permute-start | bytes 589832 | tf_op jit(solution)/shard_map/ppermute | solution.py:576
  77.6 11.5 %copy-start.1 = (s32[6]{0:T(128)S(1)}, s32[6]{0:T(128)}, u32[]{:S(2)}) copy-start(s32[6]{0:T(128)} %stack.23.info) | copy-start | bytes 76
  81.4 27.4 %collective-permute-start.10 = (bf16[16,128,256]{2,1,0:T(8,128)(2,1)}, bf16[16,128,256]{2,1,0:T(8,128)(2,1)S(1)}, u32[]{:S(2)}, u32[]{:S(2)}) collective-permute-start(bf16[16,128,256]{2,1,0:T(8,128)(2,1)} %bitcast.18), channel_id=1, source_target_pairs={{0,4},{8,40},{64,68},{72,104},{1,5},{9,41},{65,69},{73,105},{16,20... | collective-permute-start | bytes 3145736 | tf_op jit(solution)/shard_map/ppermute | solution.py:581
  82.7 26.0 %collective-permute-start.11 = (bf16[16,128,256]{2,1,0:T(8,128)(2,1)}, bf16[16,128,256]{2,1,0:T(8,128)(2,1)S(1)}, u32[]{:S(2)}, u32[]{:S(2)}) collective-permute-start(bf16[16,128,256]{2,1,0:T(8,128)(2,1)} %bitcast.20), channel_id=1, source_target_pairs={{0,6},{8,56},{64,70},{72,120},{1,7},{9,57},{65,71},{73,121},{16,22... | collective-permute-start | bytes 3145736 | tf_op jit(solution)/shard_map/ppermute | solution.py:581
  84.1 25.0 %collective-permute-start.9 = (bf16[16,128,256]{2,1,0:T(8,128)(2,1)}, bf16[16,128,256]{2,1,0:T(8,128)(2,1)}, u32[]{:S(2)}, u32[]{:S(2)}) collective-permute-start(bf16[16,128,256]{2,1,0:T(8,128)(2,1)} %bitcast.16), channel_id=1, source_target_pairs={{0,2},{8,24},{64,66},{72,88},{1,3},{9,25},{65,67},{73,89},{16,18},... | collective-permute-start | bytes 3145736 | tf_op jit(solution)/shard_map/ppermute | solution.py:581
  85.0 15.5 %all-to-all-start = ((bf16[16,16,384]{2,1,0:T(8,128)(2,1)}), bf16[16,16,384]{2,1,0:T(8,128)(2,1)}, u32[]{:S(2)}, u32[]{:S(2)}) async-start(bf16[16,16,384]{2,1,0:T(8,128)(2,1)} %fusion.3), calls=%async_computation | async-start | bytes 393216 | tf_op jit(solution)/shard_map/all_to_all | solution.py:583
  89.2 1.3 copy-start.3
  90.4 1.6 %copy-start.4 = (bf16[4096,256]{1,0:T(8,128)(2,1)S(1)}, bf16[4096,256]{1,0:T(8,128)(2,1)}, u32[]{:S(2)}) copy-start(bf16[4096,256]{1,0:T(8,128)(2,1)} %get-tuple-element.32) | copy-start | bytes 6291460
  102.2 13.5 %all-to-all-start.1 = ((bf16[16,16,384]{2,1,0:T(8,128)(2,1)}), bf16[16,16,384]{2,1,0:T(8,128)(2,1)S(1)}, u32[]{:S(2)}, u32[]{:S(2)}) async-start(bf16[16,16,384]{2,1,0:T(8,128)(2,1)} %broadcast_in_dim.2), calls=%async_computation.1 | async-start | bytes 393216 | tf_op jit(solution)/shard_map/all_to_all | solution.py:587
  115.7 16.6 %copy-start.5 = (bf16[16,16,384]{2,1,0:T(8,128)(2,1)}, bf16[16,16,384]{2,1,0:T(8,128)(2,1)S(1)}, u32[]{:S(2)}) copy-start(bf16[16,16,384]{2,1,0:T(8,128)(2,1)S(1)} %all-to-all-done.1.refs_0_) | copy-start | bytes 589828
  115.7 24.0 %copy-start.2 = (s32[6]{0:T(128)S(1)}, s32[6]{0:T(128)}, u32[]{:S(2)}) copy-start(s32[6]{0:T(128)} %stack.23.info) | copy-start | bytes 76
  115.7 21.8 %all-to-all-start.2 = ((bf16[16,128,256]{2,1,0:T(8,128)(2,1)}), bf16[16,128,256]{2,1,0:T(8,128)(2,1)S(1)}, u32[]{:S(2)}, u32[]{:S(2)}) async-start(bf16[16,128,256]{2,1,0:T(8,128)(2,1)} %bitcast.22), calls=%async_computation.2 | async-start | bytes 2097152 | tf_op jit(solution)/shard_map/all_to_all | solution.py:592
  119.6 9.9 %collective-permute-start.14 = (bf16[16,16,384]{2,1,0:T(8,128)(2,1)S(1)}, bf16[16,16,384]{2,1,0:T(8,128)(2,1)S(1)}, u32[]{:S(2)}, u32[]{:S(2)}) collective-permute-start(bf16[16,16,384]{2,1,0:T(8,128)(2,1)S(1)} %all-to-all-done.1.refs_0_), channel_id=1, source_target_pairs={{0,6},{8,56},{64,70},{72,120},{1,7},{9,57},{65,71},{73,121},{16,22... | collective-permute-start | bytes 589832 | tf_op jit(solution)/shard_map/ppermute | solution.py:593
  122.2 7.2 %collective-permute-start.13 = (bf16[16,16,384]{2,1,0:T(8,128)(2,1)S(1)}, bf16[16,16,384]{2,1,0:T(8,128)(2,1)S(1)}, u32[]{:S(2)}, u32[]{:S(2)}) collective-permute-start(bf16[16,16,384]{2,1,0:T(8,128)(2,1)S(1)} %all-to-all-done.1.refs_0_), channel_id=1, source_target_pairs={{0,4},{8,40},{64,68},{72,104},{1,5},{9,41},{65,69},{73,105},{16,20... | collective-permute-start | bytes 589832 | tf_op jit(solution)/shard_map/ppermute | solution.py:593
  122.2 10.1 %collective-permute-start.12 = (bf16[16,16,384]{2,1,0:T(8,128)(2,1)S(1)}, bf16[16,16,384]{2,1,0:T(8,128)(2,1)S(1)}, u32[]{:S(2)}, u32[]{:S(2)}) collective-permute-start(bf16[16,16,384]{2,1,0:T(8,128)(2,1)S(1)} %all-to-all-done.1.refs_0_), channel_id=1, source_target_pairs={{0,2},{8,24},{64,66},{72,88},{1,3},{9,25},{65,67},{73,89},{16,18},... | collective-permute-start | bytes 589832 | tf_op jit(solution)/shard_map/ppermute | solution.py:593
  129.4 2.8 %copy-start.6 = (bf16[16,16,384]{2,1,0:T(8,128)(2,1)}, bf16[16,16,384]{2,1,0:T(8,128)(2,1)S(1)}, u32[]{:S(2)}) copy-start(bf16[16,16,384]{2,1,0:T(8,128)(2,1)S(1)} %collective-permute-done.14.refs_3_) | copy-start | bytes 589828
  129.5 2.8 %copy-start.7 = (bf16[16,16,384]{2,1,0:T(8,128)(2,1)}, bf16[16,16,384]{2,1,0:T(8,128)(2,1)S(1)}, u32[]{:S(2)}) copy-start(bf16[16,16,384]{2,1,0:T(8,128)(2,1)S(1)} %collective-permute-done.13.refs_2_) | copy-start | bytes 589828
  132.3 0.7 copy-start.8
  135.2 4.5 %collective-permute-start.15 = (bf16[4,16,16,384]{3,2,1,0:T(8,128)(2,1)}, bf16[4,16,16,384]{3,2,1,0:T(8,128)(2,1)S(1)}, u32[]{:S(2)}, u32[]{:S(2)}) collective-permute-start(bf16[4,16,16,384]{3,2,1,0:T(8,128)(2,1)} %shard_map.80.mine), channel_id=1, source_target_pairs={{0,8},{8,0},{64,72},{72,64},{1,9},{9,1},{65,73},{73,65},{16,24},{2... | collective-permute-start | bytes 2359304 | tf_op jit(solution)/shard_map/ppermute | solution.py:595
  139.6 1.1 copy-start
